TPU v7x, 32 devices: a whole 2x2x4 slice. The times are simulated.
32 devices in a mesh: parts: 2 (over x), wide: 16 (over z, y, core).
Axes of the slice: x: 2, y: 2, z: 4, core: 2. Of those that a mesh axis runs over, the one named last changes fastest.
Arguments:
- tokens: bfloat16 [4096, 5120], P(('parts', 'wide')), parts along dimension 0, may hold values from -6 to 6
- key_weight_matrix: bfloat16 [5120, 1024], P('wide'), may hold values from -0.078125 to 0.078125
- key_bias_vector: bfloat16 [1024], replicated, may hold values from -3 to 3
- shrink_factors: bfloat16 [5120, 16384], P(None, ('parts', 'wide')), parts along dimension 1, may hold values from -0.078125 to 0.078125
- expand_factors: bfloat16 [16384, 1024], P(('parts', 'wide')), parts along dimension 0, may hold values from -1.5 to 1.5
- adapter_slot_index: int32 [1024], P('parts'), parts along dimension 0, may hold values from 0 to 511, as said below
- row_adapter_index: int32 [4096], P(('parts', 'wide')), parts along dimension 0, may hold values from 0 to 511, as said below
Outputs:
- keys_out: bfloat16 [4096, 1024], P(('parts', 'wide')), parts along dimension 0
There are 2 independent parts, one for each index of `parts`. A program takes and returns all parts, laid end to end along the dimension named above; an argument that names none is the same for every part. Nothing has to cross between parts.
Inputs may be any that keep to these rules, and one draw needn't show every extreme that they name: A permutation: adapter a's factors sit in slot adapter_slot_index[a]; slot s belongs to device s // 32 of wide. `row_adapter_index`: among the rows of one device, at most 16 have adapters whose slots lie on one device of wide; some device of wide receives exactly 16 from every device.
All inputs are finite; a program needn't handle non-finite values.
Results may differ from a plain program's by a relative error of at most 0.0054.
Values may be sent and summed in bfloat16 or wider, within the bound.
No kernel may reach another device: no remote copies, remote signals or barrier semaphores. Data moves between devices by JAX's collectives and lax.ppermute only.
A program may use at most 64 MiB of HBM per device.

v0:
```python
import jax
import jax.numpy as jnp
from jax import lax
from jax.sharding import PartitionSpec as P

ADAPTER_RANK = 16
ADP_DEV = 32


def per_device(
    tokens,
    key_weight_matrix,
    key_bias_vector,
    shrink_factors,
    expand_factors,
    adapter_slot_index,
    row_adapter_index,
):
    rows, width = tokens.shape
    slot_keepers = lax.axis_size("wide")
    slot_capacity = 2 * rows // slot_keepers
    slot = adapter_slot_index[row_adapter_index]
    holder = slot // ADP_DEV
    local = slot % ADP_DEV
    onehot = (holder[:, None] == jnp.arange(slot_keepers, dtype=jnp.int32)[None, :]).astype(
        jnp.int32
    )
    rank_in = jnp.sum(jnp.cumsum(onehot, axis=0) * onehot, axis=1) - 1
    slot_position = holder * slot_capacity + rank_in
    outgoing = (
        jnp.zeros((slot_keepers * slot_capacity, width), jnp.bfloat16).at[slot_position].set(tokens)
    )
    outgoing = outgoing.reshape(slot_keepers, slot_capacity, width)
    labels = (
        jnp.zeros((slot_keepers * slot_capacity,), jnp.bfloat16)
        .at[slot_position]
        .set((local + 1).astype(jnp.bfloat16))
    )
    labels = labels.reshape(slot_keepers, slot_capacity)
    owner = (jnp.arange(ADP_DEV * ADAPTER_RANK, dtype=jnp.int32) // ADAPTER_RANK + 1).astype(
        jnp.float32
    )
    arrived = lax.all_to_all(outgoing, "wide", split_axis=0, concat_axis=0, tiled=True)
    marks = lax.all_to_all(labels, "wide", split_axis=0, concat_axis=0, tiled=True)
    count_sender, count_entry = marks.shape
    flattened = arrived.reshape(count_sender * count_entry, width)
    key_projected = jnp.dot(flattened, shrink_factors, preferred_element_type=jnp.float32)
    keep = marks.reshape(count_sender * count_entry, 1).astype(jnp.float32) == owner[None, :]
    shrink_output = jnp.where(keep, key_projected, 0.0).astype(jnp.bfloat16)
    adapter_update = jnp.dot(
        shrink_output, expand_factors, preferred_element_type=jnp.float32
    ).astype(jnp.bfloat16)
    adapter_update = adapter_update.reshape(count_sender, count_entry, expand_factors.shape[1])
    returned_rows = lax.all_to_all(adapter_update, "wide", split_axis=0, concat_axis=0, tiled=True)
    adapter_update = returned_rows.reshape(slot_keepers * slot_capacity, expand_factors.shape[1])[
        slot_position
    ]
    gathered = lax.all_gather(key_weight_matrix, "wide", axis=0, tiled=True)
    base = jnp.dot(tokens, gathered, preferred_element_type=jnp.float32)
    total = base + key_bias_vector.astype(jnp.float32) + 2.0 * adapter_update.astype(jnp.float32)
    return total.astype(jnp.bfloat16)


def solution(mesh):
    placed = (
        P(("parts", "wide"), None),
        P("wide", None),
        P(),
        P(None, ("parts", "wide")),
        P(("parts", "wide"), None),
        P("parts"),
        P(("parts", "wide")),
    )
    return jax.shard_map(
        per_device,
        mesh=mesh,
        in_specs=placed,
        out_specs=P(("parts", "wide"), None),
        check_vma=False,
    )
```

profile of v0, /device:TPU:0, one launch (start us, length us, event | category | flops | bytes accessed | tf_op | source)
XLA Modules:
  0.0 180.9 jit_solution(3474294360549557165)
XLA Ops:
  6.5 0.0 copy-start
  6.5 0.0 all-gather.2.cloned.1.call-start
  6.5 0.7 all-gather.2.cloned.1.call-update
  7.3 0.7 compare_select_fusion.1
  7.9 1.6 gather_fusion
  9.6 0.1 fusion.9
  9.7 0.2 reduce_window_sum.11
  9.8 0.2 select_reduce_fusion
  10.0 1.3 scatter_custom_fusion
  11.4 0.7 all_to_all.16
  12.1 7.4 %all-to-all-start = ((bf16[16,1,16]{2,1,0:T(2,128)(2,1)}), bf16[16,1,16]{2,1,0:T(2,128)(2,1)S(1)}, u32[]{:S(2)}, u32[]{:S(2)}) async-start(bf16[16,1,16]{2,1,0:T(2,128)(2,1)} %all_to_all.16), calls=%async_computation | async-start | bytes 16384 | tf_op jit(solution)/shard_map/all_to_all | solution.py:44
  19.5 5.1 %scatter_custom_fusion.1 = bf16[256,5120]{1,0:T(8,128)(2,1)} fusion(s32[128]{0:T(128)S(1)} %fusion.17, bf16[128,5120]{1,0:T(8,128)(2,1)} %param.7, bf16[]{:T(256)} %constant.51.clone.1), kind=kCustom, calls=%fused_computation.4 | custom fusion | bytes 2621952 | tf_op jit(solution)/shard_map/scatter | solution.py:31
  24.6 1.3 all-to-all-done
  25.9 4.7 %all-to-all-start.1 = ((bf16[16,16,5120]{2,1,0:T(8,128)(2,1)}), bf16[16,16,5120]{2,1,0:T(8,128)(2,1)}, u32[]{:S(2)}, u32[]{:S(2)}) async-start(bf16[16,16,5120]{2,1,0:T(8,128)(2,1)} %bitcast.26), calls=%async_computation.1 | async-start | bytes 5242880 | tf_op jit(solution)/shard_map/all_to_all | solution.py:43
  30.7 0.1 reshape.122
  30.8 83.6 %all-to-all-done.1 = bf16[16,16,5120]{2,1,0:T(8,128)(2,1)} async-done(((bf16[16,16,5120]{2,1,0:T(8,128)(2,1)}), bf16[16,16,5120]{2,1,0:T(8,128)(2,1)}, u32[]{:S(2)}, u32[]{:S(2)}) %all-to-all-start.1) | async-done | bytes 2621472 | tf_op jit(solution)/shard_map/all_to_all | solution.py:43
  114.4 0.0 copy-done
  114.4 6.0 %convolution_convert_fusion = bf16[256,1024]{1,0:T(8,128)(2,1)} fusion(bf16[512,1024]{1,0:T(8,128)(2,1)S(1)} %copy-done, bf16[256,5120]{1,0:T(8,128)(2,1)} %bitcast.4, bf16[5120,512]{1,0:T(8,128)(2,1)} %param.10, f32[512]{0:T(512)S(1)} %fusion.11, f32[256]{0:T(256)S(1)} %reshape.122), kind=kOutput, calls=%fused_computation.6 | convolution fusion | flops 1611268096 | bytes 9440256 | tf_op jit(solution)/shard_map/dot_general | solution.py:50
  120.4 32.0 %all-to-all-start.2 = ((bf16[16,16,1024]{2,1,0:T(8,128)(2,1)}), bf16[16,16,1024]{2,1,0:T(8,128)(2,1)S(1)}, u32[]{:S(2)}, u32[]{:S(2)}) async-start(bf16[16,16,1024]{2,1,0:T(8,128)(2,1)} %bitcast.5), calls=%async_computation.2 | async-start | bytes 1048576 | tf_op jit(solution)/shard_map/all_to_all | solution.py:54
  152.4 0.0 copy-done.2
  152.4 14.4 %all-to-all-done.2 = bf16[16,16,1024]{2,1,0:T(8,128)(2,1)S(1)} async-done(((bf16[16,16,1024]{2,1,0:T(8,128)(2,1)}), bf16[16,16,1024]{2,1,0:T(8,128)(2,1)S(1)}, u32[]{:S(2)}, u32[]{:S(2)}) %all-to-all-start.2) | async-done | bytes 524320 | tf_op jit(solution)/shard_map/all_to_all | solution.py:54
  166.8 0.9 gather_fusion.1
  167.7 0.0 all-gather.2.cloned.1.call-done
  167.7 6.3 %fusion.3 = bf16[128,1024]{1,0:T(8,128)(2,1)} fusion(bf16[128,5120]{1,0:T(8,128)(2,1)S(1)} %copy-done.1, bf16[5120,1024]{1,0:T(8,128)(2,1)} %all-gather.2.cloned.1.call-done, bf16[128,1024]{1,0:T(8,128)(2,1)S(1)} %gather_fusion.1, f32[1024]{0:T(1024)S(1)} %convert_element_type.39), kind=kOutput, calls=%fused_computation.10 | convolution fusion | flops 1342832640 | bytes 12324864 | tf_op jit(solution)/shard_map/dot_general | solution.py:59
  (10 shorter events, 0.1 us)
Async XLA Ops:
  6.5 107.8 %copy-start = (bf16[512,1024]{1,0:T(8,128)(2,1)S(1)}, bf16[512,1024]{1,0:T(8,128)(2,1)}, u32[]{:S(2)}) copy-start(bf16[512,1024]{1,0:T(8,128)(2,1)} %param.11) | copy-start | bytes 3145732
  6.5 161.2 %all-gather.2.cloned.1.call-start = ((), (), s32[]{:S(2)}) async-start(), calls=%async_computation.3 | async-start | bytes 11141120 | tf_op jit(solution)/shard_map/all_gather | solution.py:58
  12.1 13.8 %all-to-all-start = ((bf16[16,1,16]{2,1,0:T(2,128)(2,1)}), bf16[16,1,16]{2,1,0:T(2,128)(2,1)S(1)}, u32[]{:S(2)}, u32[]{:S(2)}) async-start(bf16[16,1,16]{2,1,0:T(2,128)(2,1)} %all_to_all.16), calls=%async_computation | async-start | bytes 16384 | tf_op jit(solution)/shard_map/all_to_all | solution.py:44
  25.9 88.4 %all-to-all-start.1 = ((bf16[16,16,5120]{2,1,0:T(8,128)(2,1)}), bf16[16,16,5120]{2,1,0:T(8,128)(2,1)}, u32[]{:S(2)}, u32[]{:S(2)}) async-start(bf16[16,16,5120]{2,1,0:T(8,128)(2,1)} %bitcast.26), calls=%async_computation.1 | async-start | bytes 5242880 | tf_op jit(solution)/shard_map/all_to_all | solution.py:43
  114.4 38.0 %copy-start.2 = (bf16[1024]{0:T(1024)(128)(2,1)S(1)}, bf16[1024]{0:T(1024)(128)(2,1)}, u32[]{:S(2)}) copy-start(bf16[1024]{0:T(1024)(128)(2,1)} %param.9) | copy-start | bytes 6148
  120.4 47.4 %copy-start.1 = (bf16[128,5120]{1,0:T(8,128)(2,1)S(1)}, bf16[128,5120]{1,0:T(8,128)(2,1)}, u32[]{:S(2)}) copy-start(bf16[128,5120]{1,0:T(8,128)(2,1)} %param.7) | copy-start | bytes 3932164
  120.4 46.5 %all-to-all-start.2 = ((bf16[16,16,1024]{2,1,0:T(8,128)(2,1)}), bf16[16,16,1024]{2,1,0:T(8,128)(2,1)S(1)}, u32[]{:S(2)}, u32[]{:S(2)}) async-start(bf16[16,16,1024]{2,1,0:T(8,128)(2,1)} %bitcast.5), calls=%async_computation.2 | async-start | bytes 1048576 | tf_op jit(solution)/shard_map/all_to_all | solution.py:54
Sparse Core Ops, SparseCore 0:
  9.6 136.6 all-gather.1
where the time goes:
time: 181 us
  waiting for transfers between devices  100 us (55%)
  starting transfers between devices  44.1 us (24%)
  between operations  13.5 us (7%)
  matrix products  12.3 us (7%)
  local copies, waits for them, and re-layouts  9.73 us (5%)
    all_to_all x1, waiting for transfers between devices, per_device(): lax.all_to_all(outgoing, 'wide', split_axis=0, concat_axis=0, tiled=True)  83.6 us
    all_to_all x1, starting transfers between devices, per_device(): lax.all_to_all(adapter_update, 'wide', split_axis=0, concat_axis=0, tiled...  32 us
    all_to_all x1, waiting for transfers between devices, per_device(): lax.all_to_all(adapter_update, 'wide', split_axis=0, concat_axis=0, tiled...  14.4 us
    all_to_all x1, starting transfers between devices, per_device(): lax.all_to_all(labels, 'wide', split_axis=0, concat_axis=0, tiled=True)  7.39 us
    dot_general x1, matrix products, per_device(): base = jnp.dot(tokens, gathered, preferred_element_type=jnp.float32)  6.34 us
    dot_general x1, matrix products, per_device(): jnp.dot(shrink_output, expand_factors, preferred_element_type=jnp.float32)  6 us
    scatter x1, local copies, waits for them, and re-layouts, per_device(): jnp.zeros((slot_keepers * slot_capacity, width), jnp.bfloat16)  5.11 us
    all_to_all x1, starting transfers between devices, per_device(): lax.all_to_all(outgoing, 'wide', split_axis=0, concat_axis=0, tiled=True)  4.73 us
  transfers between devices with their start and end apart: 4, of which 3 were waited for; matrix products, arithmetic and copies ran while one was open for 9% of the time, Pallas kernels for 0%

commit v1 on v0

v1 whole, which is shorter than its diff:
```python
import functools

import jax
import jax.numpy as jnp
from jax import lax
from jax.experimental import pallas as pl
from jax.experimental.pallas import tpu as pltpu
from jax.sharding import PartitionSpec as P

ADAPTER_RANK = 16
LANES = 128
VMEM_LIMIT = 48 * 1024 * 1024
F32 = jnp.float32
BF16 = jnp.bfloat16


def _row_places(slot_ref, adapter_ref, adapters_held, capacity):
    adapters = slot_ref.shape[1]
    rows = adapter_ref.shape[1]
    held_bits = adapters_held.bit_length() - 1
    slots = slot_ref[...]
    high = jnp.broadcast_to((slots >> 6).astype(F32).astype(BF16), (8, adapters))
    low = jnp.broadcast_to((slots & 63).astype(F32).astype(BF16), (8, adapters))
    picks = lax.broadcasted_iota(jnp.int32, (adapters, rows), 0) == adapter_ref[...]
    picks = picks.astype(F32).astype(BF16)
    slot_high = jnp.dot(high, picks, preferred_element_type=F32)
    slot_low = jnp.dot(low, picks, preferred_element_type=F32)
    slot = (slot_high * 64.0 + slot_low)[:1].astype(jnp.int32)
    holder = slot >> held_bits
    local = slot & (adapters_held - 1)
    across = jnp.broadcast_to(holder.astype(F32), (rows, rows))
    earlier = lax.broadcasted_iota(jnp.int32, (rows, rows), 0) < lax.broadcasted_iota(
        jnp.int32, (rows, rows), 1
    )
    same = jnp.where(earlier & (across.T == across), 1.0, 0.0)
    rank = jnp.sum(same, axis=0, keepdims=True).astype(jnp.int32)
    return holder * capacity + rank, local


def _pack_kernel(adapters_held, capacity, slot_ref, adapter_ref, tokens_ref, out_ref, place_ref):
    rows, width = tokens_ref.shape
    places = out_ref.shape[0]
    place, local = _row_places(slot_ref, adapter_ref, adapters_held, capacity)
    place_ref[...] = jnp.broadcast_to(place, place_ref.shape)
    sits = lax.broadcasted_iota(jnp.int32, (places, rows), 0) == place
    labels = jnp.sum(
        jnp.where(sits, (local + 1).astype(F32), 0.0), axis=1, keepdims=True
    )
    chosen = sits.astype(F32).astype(BF16)
    step = 1024 if width % 1024 == 0 else width
    for start in range(0, width, step):
        out_ref[:, start : start + step] = jnp.dot(
            chosen, tokens_ref[:, start : start + step], preferred_element_type=F32
        ).astype(BF16)
    out_ref[:, width:] = jnp.broadcast_to(labels, (places, LANES)).astype(BF16)


def pack(slots, adapters, tokens, adapters_held, capacity, places):
    rows, width = tokens.shape
    return pl.pallas_call(
        functools.partial(_pack_kernel, adapters_held, capacity),
        out_shape=(
            jax.ShapeDtypeStruct((places, width + LANES), BF16),
            jax.ShapeDtypeStruct((8, rows), jnp.int32),
        ),
        compiler_params=pltpu.CompilerParams(vmem_limit_bytes=VMEM_LIMIT),
        cost_estimate=pl.CostEstimate(
            flops=2 * places * rows * width,
            bytes_accessed=2 * (rows + places) * width,
            transcendentals=0,
        ),
        name="pack_rows",
    )(slots, adapters, tokens)


def _adapter_kernel(rows_ref, label_ref, shrink_ref, expand_ref, out_ref, total_ref):
    step = pl.program_id(0)

    @pl.when(step == 0)
    def _():
        total_ref[...] = jnp.zeros_like(total_ref)

    total_ref[...] += jnp.dot(rows_ref[...], shrink_ref[...], preferred_element_type=F32)

    @pl.when(step == pl.num_programs(0) - 1)
    def _():
        places, ranks = total_ref.shape
        owner = lax.broadcasted_iota(jnp.int32, (places, ranks), 1) // ADAPTER_RANK + 1
        keep = label_ref[:, :1].astype(F32) == owner.astype(F32)
        shrunk = jnp.where(keep, total_ref[...], 0.0).astype(BF16)
        out_ref[...] = jnp.dot(shrunk, expand_ref[...], preferred_element_type=F32).astype(BF16)


def adapter_terms(arrived, shrink, expand):
    places = arrived.shape[0]
    width, ranks = shrink.shape
    columns = expand.shape[1]
    step = 1024
    return pl.pallas_call(
        _adapter_kernel,
        grid=(width // step,),
        in_specs=[
            pl.BlockSpec((places, step), lambda k: (0, k)),
            pl.BlockSpec((places, LANES), lambda k: (0, width // LANES)),
            pl.BlockSpec((step, ranks), lambda k: (k, 0)),
            pl.BlockSpec((ranks, columns), lambda k: (0, 0)),
        ],
        out_specs=pl.BlockSpec((places, columns), lambda k: (0, 0)),
        out_shape=jax.ShapeDtypeStruct((places, columns), BF16),
        scratch_shapes=[pltpu.VMEM((places, ranks), F32)],
        compiler_params=pltpu.CompilerParams(vmem_limit_bytes=VMEM_LIMIT),
        cost_estimate=pl.CostEstimate(
            flops=2 * places * ranks * (width + columns),
            bytes_accessed=2 * (places + ranks) * (width + columns),
            transcendentals=0,
        ),
        name="adapter_terms",
    )(arrived, arrived, shrink, expand)


def swap(x, axis, bit):
    size = lax.axis_size(axis)
    return lax.ppermute(x, axis, [(i, i ^ bit) for i in range(size)])


def gather_weights(weights):
    size = lax.axis_size("wide")
    half = weights.shape[0] // 2
    mine = lax.axis_index("parts") * half
    current = lax.dynamic_slice_in_dim(weights, mine, half, 0)
    marks = [(0, 0)]

    def grow(x, known, axis, bit):
        wide, parts = (bit, 0) if axis == "wide" else (0, bit)
        return (
            jnp.concatenate([x, swap(x, axis, bit)], axis=0),
            known + [(w ^ wide, p ^ parts) for w, p in known],
        )

    bit = size // 2
    while bit > 2:
        current, marks = grow(current, marks, "wide", bit)
        bit //= 2
    middle, cut = len(marks) // 2, current.shape[0] // 2
    pieces = []
    for x, known, order in (
        (current[:cut], marks[:middle], (("wide", 2), ("parts", 1))),
        (current[cut:], marks[middle:], (("parts", 1), ("wide", 2))),
    ):
        x, known = grow(x, known, *order[0])
        other, (axis, b) = swap(x, *order[1]), order[1]
        wide, parts = (b, 0) if axis == "wide" else (0, b)
        pieces += [(x, known), (other, [(w ^ wide, p ^ parts) for w, p in known])]
    pieces += [(swap(x, "wide", 1), [(w ^ 1, p) for w, p in known]) for x, known in pieces]
    return pieces


def _base_kernel(marks, me_ref, *refs):
    count = len(marks)
    pieces, tokens_ref, out_ref, held_ref = refs[:count], refs[count], refs[count + 1], refs[count + 2]
    wide, parts = me_ref[0], me_ref[1]
    rows = held_ref.shape[1]
    for piece, known in zip(pieces, marks, strict=True):
        for i, (w, p) in enumerate(known):
            place = (wide ^ w) * 2 + (parts ^ p)
            held_ref[place] = piece[i * rows : (i + 1) * rows, :]
    width, columns = tokens_ref.shape[1], out_ref.shape[1]
    together = 4
    depth = together * rows
    out_ref[...] = jnp.zeros_like(out_ref)

    @pl.loop(0, width // depth)
    def _(k):
        block = held_ref[pl.ds(k * together, together)].reshape(depth, columns)
        left = tokens_ref[:, pl.ds(pl.multiple_of(k * depth, LANES), depth)]
        out_ref[...] += jnp.dot(left, block, preferred_element_type=F32)


def base_product(tokens, pieces, rows):
    marks = [known for _, known in pieces]
    columns = pieces[0][0].shape[1]
    width = tokens.shape[1]
    me = jnp.stack([lax.axis_index("wide"), lax.axis_index("parts")]).astype(jnp.int32)
    vmem = pl.BlockSpec(memory_space=pltpu.VMEM)
    return pl.pallas_call(
        functools.partial(_base_kernel, marks),
        in_specs=[pl.BlockSpec(memory_space=pltpu.SMEM)] + [vmem] * (len(pieces) + 1),
        out_specs=vmem,
        out_shape=jax.ShapeDtypeStruct((tokens.shape[0], columns), F32),
        scratch_shapes=[pltpu.VMEM((width // rows, rows, columns), BF16)],
        compiler_params=pltpu.CompilerParams(vmem_limit_bytes=VMEM_LIMIT),
        cost_estimate=pl.CostEstimate(
            flops=2 * tokens.shape[0] * width * columns,
            bytes_accessed=2 * width * columns,
            transcendentals=0,
        ),
        name="base_product",
    )(me, *[x for x, _ in pieces], tokens)


def _finish_kernel(base_ref, bias_ref, returned_ref, place_ref, out_ref):
    places = returned_ref.shape[0]
    rows = base_ref.shape[0]
    sits = lax.broadcasted_iota(jnp.int32, (places, rows), 0) == place_ref[:1, :]
    chosen = sits.astype(F32).T.astype(BF16)
    terms = jnp.dot(chosen, returned_ref[...], preferred_element_type=F32)
    total = base_ref[...] + bias_ref[...].astype(F32) + 2.0 * terms
    out_ref[...] = total.astype(BF16)


def finish(base, bias, returned, place):
    return pl.pallas_call(
        _finish_kernel,
        out_shape=jax.ShapeDtypeStruct(base.shape, BF16),
        compiler_params=pltpu.CompilerParams(vmem_limit_bytes=VMEM_LIMIT),
        name="add_terms",
    )(base, bias, returned, place)


def per_device(
    tokens,
    key_weight_matrix,
    key_bias_vector,
    shrink_factors,
    expand_factors,
    adapter_slot_index,
    row_adapter_index,
):
    rows, width = tokens.shape
    holders = lax.axis_size("wide")
    capacity = 2 * rows // holders
    places = holders * capacity
    adapters_held = expand_factors.shape[0] // ADAPTER_RANK
    columns = expand_factors.shape[1]

    outgoing, place = pack(
        adapter_slot_index[None, :], row_adapter_index[None, :], tokens, adapters_held, capacity, places
    )
    arrived = lax.all_to_all(
        outgoing.reshape(holders, capacity, width + LANES), "wide", split_axis=0, concat_axis=0, tiled=True
    )
    half = key_weight_matrix.shape[0] // 2
    if half % 16 == 0 and (4 * half) % LANES == 0:
        base = base_product(tokens, gather_weights(key_weight_matrix), half)
    else:
        gathered = lax.all_gather(key_weight_matrix, "wide", axis=0, tiled=True)
        base = jnp.dot(tokens, gathered, preferred_element_type=F32)
    terms = adapter_terms(arrived.reshape(places, width + LANES), shrink_factors, expand_factors)
    returned = lax.all_to_all(
        terms.reshape(holders, capacity, columns), "wide", split_axis=0, concat_axis=0, tiled=True
    )
    return finish(base, key_bias_vector[None, :], returned.reshape(places, columns), place)


def solution(mesh):
    placed = (
        P(("parts", "wide"), None),
        P("wide", None),
        P(),
        P(None, ("parts", "wide")),
        P(("parts", "wide"), None),
        P("parts"),
        P(("parts", "wide")),
    )
    return jax.shard_map(
        per_device,
        mesh=mesh,
        in_specs=placed,
        out_specs=P(("parts", "wide"), None),
        check_vma=False,
    )
```

time: 181 us -> 178 us (0.983)
  waiting for transfers between devices: 100 us -> 132 us
  starting transfers between devices: 44.1 us -> 19.6 us
  Pallas kernels: 0 us -> 16 us
  between operations: 13.5 us -> 0.14 us
  matrix products: 12.3 us -> 0 us
    ppermute x0 -> x10, waiting for transfers between devices: none -> 126 us  [swap(): return lax.ppermute(x, axis, [(i, i ^ bit) for i in range(size)])]
    all_to_all x3 -> x2, waiting for transfers between devices: 99.3 us -> 6.19 us  [the longest x1 6.19 us: per_device(): lax.all_to_all(terms.reshape(holders, capacity, columns), 'wide', split_a...]
    all_to_all x3 -> x2, starting transfers between devices: 44.1 us -> 11.1 us  [the longest x1 7.38 us: per_device(): lax.all_to_all(outgoing.reshape(holders, capacity, width + LANES), 'wide'...]
    pallas_call x0 -> x4, Pallas kernels: none -> 16 us  [the longest x1 8.14 us: base_product(): pl.pallas_call(functools.partial(_base_kernel, marks), in_specs=[pl.Block...]
    dot_general x2 -> x0, matrix products: 12.3 us -> none  [the longest x1 6.34 us: per_device(): base = jnp.dot(tokens, gathered, preferred_element_type=jnp.float32)]
    ppermute x0 -> x10, starting transfers between devices: none -> 8.48 us  [swap(): return lax.ppermute(x, axis, [(i, i ^ bit) for i in range(size)])]
    unnamed x6 -> x17, local copies, waits for them, and re-layouts: 0.01 us -> 7.15 us
    scatter x2 -> x0, local copies, waits for them, and re-layouts: 6.45 us -> none  [the longest x1 5.11 us: per_device(): jnp.zeros((slot_keepers * slot_capacity, width), jnp.bfloat16)]
  transfers between devices with their start and end apart: 4 -> 12, of which waited for: 3 -> 6; matrix products, arithmetic and copies ran while one was open for 9% -> 2% of each run, Pallas kernels for 0% -> 8%
where the time goes in v1:
time: 178 us; the launch traced here: 177 us
  waiting for transfers between devices  132 us (74%)
  starting transfers between devices  19.6 us (11%)
  Pallas kernels  16 us (9%)
  local copies, waits for them, and re-layouts  8.13 us (5%)
    ppermute x10, waiting for transfers between devices, swap(): return lax.ppermute(x, axis, [(i, i ^ bit) for i in range(size)])  126 us
    ppermute x10, starting transfers between devices, swap(): return lax.ppermute(x, axis, [(i, i ^ bit) for i in range(size)])  8.48 us
    pallas_call x1, Pallas kernels, base_product(): pl.pallas_call(functools.partial(_base_kernel, marks), in_specs=[pl.Block...  8.14 us
    all_to_all x1, starting transfers between devices, per_device(): lax.all_to_all(outgoing.reshape(holders, capacity, width + LANES), 'wide'...  7.38 us
    unnamed x17, local copies, waits for them, and re-layouts  7.15 us
    all_to_all x1, waiting for transfers between devices, per_device(): lax.all_to_all(terms.reshape(holders, capacity, columns), 'wide', split_a...  6.19 us
    pallas_call x1, Pallas kernels, adapter_terms(): pl.pallas_call(_adapter_kernel, grid=(width // step,), in_specs=[pl.Block...  5.76 us
    all_to_all x1, starting transfers between devices, per_device(): lax.all_to_all(terms.reshape(holders, capacity, columns), 'wide', split_a...  3.76 us
  transfers between devices with their start and end apart: 12, of which 6 were waited for; matrix products, arithmetic and copies ran while one was open for 2% of the time, Pallas kernels for 8%

profile of v1, /device:TPU:0, one launch (start us, length us, event | category | flops | bytes accessed | tf_op | source)
XLA Modules:
  0.0 177.1 jit_solution(1108495560551651504)
XLA Ops:
  0.0 1.4 copy-done.1
  1.4 0.7 copy-done.5
  2.7 1.1 pack_rows.1
  3.8 1.5 copy-done.2
  5.4 7.4 %all-to-all-start = ((bf16[16,16,5248]{2,1,0:T(8,128)(2,1)}), bf16[16,16,5248]{2,1,0:T(8,128)(2,1)S(1)}, u32[]{:S(2)}, u32[]{:S(2)}) async-start(bf16[16,16,5248]{2,1,0:T(8,128)(2,1)} %bitcast.10), calls=%async_computation | async-start | bytes 5373952 | tf_op jit(solution)/shard_map/all_to_all | solution.py:239
  12.8 2.9 %collective-permute-start = (bf16[160,1024]{1,0:T(8,128)(2,1)S(1)}, bf16[160,1024]{1,0:T(8,128)(2,1)S(1)}, u32[]{:S(2)}, u32[]{:S(2)}) collective-permute-start(bf16[160,1024]{1,0:T(8,128)(2,1)S(1)} %constant_dynamic-slice_fusion), channel_id=1, source_target_pairs={{0,8},{1,9},{2,10},{3,11},{4,12},{5,13},{6,14},{7,15},{8,0},{9,1},... | collective-permute-start | bytes 983048 | tf_op jit(solution)/shard_map/ppermute | solution.py:123
  15.7 72.9 %collective-permute-done = bf16[160,1024]{1,0:T(8,128)(2,1)S(1)} collective-permute-done((bf16[160,1024]{1,0:T(8,128)(2,1)S(1)}, bf16[160,1024]{1,0:T(8,128)(2,1)S(1)}, u32[]{:S(2)}, u32[]{:S(2)}) %collective-permute-start) | collective-permute-done | bytes 327712 | tf_op jit(solution)/shard_map/ppermute | solution.py:123
  88.7 1.5 collective-permute-start.1
  90.2 14.7 %collective-permute-done.3 = bf16[320,1024]{1,0:T(8,128)(2,1)S(1)} collective-permute-done((bf16[320,1024]{1,0:T(8,128)(2,1)S(1)}, bf16[320,1024]{1,0:T(8,128)(2,1)S(1)}, u32[]{:S(2)}, u32[]{:S(2)}) %collective-permute-start.3) | collective-permute-done | bytes 655392 | tf_op jit(solution)/shard_map/ppermute | solution.py:123
  104.9 1.5 collective-permute-start.4
  106.4 1.2 pad_maximum_fusion.refs_0_
  108.1 0.9 constant_dynamic-update-slice_fusion.1
  109.0 13.6 %collective-permute-done.4 = bf16[320,1024]{1,0:T(8,128)(2,1)S(1)} collective-permute-done((bf16[320,1024]{1,0:T(8,128)(2,1)S(1)}, bf16[320,1024]{1,0:T(8,128)(2,1)S(1)}, u32[]{:S(2)}, u32[]{:S(2)}) %collective-permute-start.4) | collective-permute-done | bytes 655392 | tf_op jit(solution)/shard_map/ppermute | solution.py:123
  122.6 0.9 constant_dynamic-update-slice_fusion.refs_2_
  123.5 1.5 collective-permute-start.5
  125.5 23.0 %collective-permute-done.2.refs_1_ = bf16[640,1024]{1,0:T(8,128)(2,1)} collective-permute-done((bf16[640,1024]{1,0:T(8,128)(2,1)}, bf16[640,1024]{1,0:T(8,128)(2,1)}, u32[]{:S(2)}, u32[]{:S(2)}) %collective-permute-start.2) | collective-permute-done | bytes 1310752 | tf_op jit(solution)/shard_map/ppermute | solution.py:123
  148.5 1.6 collective-permute-done.5.refs_3_
  150.1 1.2 copy-done.4
  151.3 5.8 %adapter_terms.1 = bf16[256,1024]{1,0:T(8,128)(2,1)S(1)} custom-call(bf16[256,5248]{1,0:T(8,128)(2,1)S(1)} %bitcast.8, bf16[256,5248]{1,0:T(8,128)(2,1)S(1)} %bitcast.9, bf16[5120,512]{1,0:T(8,128)(2,1)} %shrink_ref.1, bf16[512,1024]{1,0:T(8,128)(2,1)S(1)} %copy-done.4), custom_call_target="tpu_custom_call" | custom-call | flops 1610612736 | bytes 9437184 | tf_op jit(solution)/shard_map/adapter_terms/pallas_call | solution.py:99
  157.1 0.8 copy-done.3
  157.9 3.8 %all-to-all-start.1 = ((bf16[16,16,1024]{2,1,0:T(8,128)(2,1)}), bf16[16,16,1024]{2,1,0:T(8,128)(2,1)S(1)}, u32[]{:S(2)}, u32[]{:S(2)}) async-start(bf16[16,16,1024]{2,1,0:T(8,128)(2,1)} %bitcast.11), calls=%async_computation.1 | async-start | bytes 1048576 | tf_op jit(solution)/shard_map/all_to_all | solution.py:249
  161.8 8.1 %base_product.1.base_ref = f32[128,1024]{1,0:T(8,128)S(1)} custom-call(s32[2]{0:T(128)S(1)} %pad_add_fusion.me_ref, bf16[640,1024]{1,0:T(8,128)(2,1)} %pad_maximum_fusion.refs_0_, bf16[640,1024]{1,0:T(8,128)(2,1)} %collective-permute-done.2.refs_1_, bf16[640,1024]{1,0:T(8,128)(2,1)} %constant_dynamic-update-slice_fusion.refs_2_, ...), custom_call_target="tpu_custom_call" | custom-call | flops 1342177280 | bytes 10485760 | tf_op jit(solution)/shard_map/base_product/pallas_call | solution.py:185
  169.9 6.2 %all-to-all-done.1 = bf16[16,16,1024]{2,1,0:T(8,128)(2,1)S(1)} async-done(((bf16[16,16,1024]{2,1,0:T(8,128)(2,1)}), bf16[16,16,1024]{2,1,0:T(8,128)(2,1)S(1)}, u32[]{:S(2)}, u32[]{:S(2)}) %all-to-all-start.1) | async-done | bytes 524320 | tf_op jit(solution)/shard_map/all_to_all | solution.py:249
  176.1 1.0 add_terms.1
  (27 shorter events, 2.0 us)
Async XLA Ops:
  0.0 12.8 %copy-start = (bf16[320,1024]{1,0:T(8,128)(2,1)S(1)}, bf16[320,1024]{1,0:T(8,128)(2,1)}, u32[]{:S(2)}) copy-start(bf16[320,1024]{1,0:T(8,128)(2,1)} %param.8) | copy-start | bytes 1966084
  0.0 1.4 copy-start.1
  1.4 0.7 copy-start.5
  2.1 0.7 copy-start.6
  3.8 1.5 copy-start.2
  5.4 144.7 %all-to-all-start = ((bf16[16,16,5248]{2,1,0:T(8,128)(2,1)}), bf16[16,16,5248]{2,1,0:T(8,128)(2,1)S(1)}, u32[]{:S(2)}, u32[]{:S(2)}) async-start(bf16[16,16,5248]{2,1,0:T(8,128)(2,1)} %bitcast.10), calls=%async_computation | async-start | bytes 5373952 | tf_op jit(solution)/shard_map/all_to_all | solution.py:239
  12.8 75.7 %collective-permute-start = (bf16[160,1024]{1,0:T(8,128)(2,1)S(1)}, bf16[160,1024]{1,0:T(8,128)(2,1)S(1)}, u32[]{:S(2)}, u32[]{:S(2)}) collective-permute-start(bf16[160,1024]{1,0:T(8,128)(2,1)S(1)} %constant_dynamic-slice_fusion), channel_id=1, source_target_pairs={{0,8},{1,9},{2,10},{3,11},{4,12},{5,13},{6,14},{7,15},{8,0},{9,1},... | collective-permute-start | bytes 983048 | tf_op jit(solution)/shard_map/ppermute | solution.py:123
  88.6 16.3 %collective-permute-start.3 = (bf16[320,1024]{1,0:T(8,128)(2,1)S(1)}, bf16[320,1024]{1,0:T(8,128)(2,1)S(1)}, u32[]{:S(2)}, u32[]{:S(2)}) collective-permute-start(bf16[320,1024]{1,0:T(8,128)(2,1)S(1)} %pad_maximum_fusion.1), channel_id=1, source_target_pairs={{0,4},{1,5},{2,6},{3,7},{4,0},{5,1},{6,2},{7,3},{8,12},{9,13},{10,... | collective-permute-start | bytes 1966088 | tf_op jit(solution)/shard_map/ppermute | solution.py:123
  88.7 17.8 %collective-permute-start.1 = (bf16[320,1024]{1,0:T(8,128)(2,1)S(1)}, bf16[320,1024]{1,0:T(8,128)(2,1)S(1)}, u32[]{:S(2)}, u32[]{:S(2)}) collective-permute-start(bf16[320,1024]{1,0:T(8,128)(2,1)S(1)} %pad_maximum_fusion.1), channel_id=1, source_target_pairs={{0,2},{1,3},{2,0},{3,1},{4,6},{5,7},{6,4},{7,5},{8,10},{9,11},{10,... | collective-permute-start | bytes 1966088 | tf_op jit(solution)/shard_map/ppermute | solution.py:123
  104.9 17.7 %collective-permute-start.4 = (bf16[320,1024]{1,0:T(8,128)(2,1)S(1)}, bf16[320,1024]{1,0:T(8,128)(2,1)S(1)}, u32[]{:S(2)}, u32[]{:S(2)}) collective-permute-start(bf16[320,1024]{1,0:T(8,128)(2,1)S(1)} %collective-permute-done.3), channel_id=1, source_target_pairs={{0,16},{16,0},{1,17},{17,1},{2,18},{18,2},{3,19},{19,3},{4,20},{20... | collective-permute-start | bytes 1966088 | tf_op jit(solution)/shard_map/ppermute | solution.py:123
  107.6 40.9 %collective-permute-start.2 = (bf16[640,1024]{1,0:T(8,128)(2,1)}, bf16[640,1024]{1,0:T(8,128)(2,1)}, u32[]{:S(2)}, u32[]{:S(2)}) collective-permute-start(bf16[640,1024]{1,0:T(8,128)(2,1)} %pad_maximum_fusion.refs_0_), channel_id=1, source_target_pairs={{0,16},{16,0},{1,17},{17,1},{2,18},{18,2},{3,19},{19,3},{4,20},{20... | collective-permute-start | bytes 3932168 | tf_op jit(solution)/shard_map/ppermute | solution.py:123
  123.5 26.5 %collective-permute-start.5 = (bf16[640,1024]{1,0:T(8,128)(2,1)}, bf16[640,1024]{1,0:T(8,128)(2,1)}, u32[]{:S(2)}, u32[]{:S(2)}) collective-permute-start(bf16[640,1024]{1,0:T(8,128)(2,1)} %constant_dynamic-update-slice_fusion.refs_2_), channel_id=1, source_target_pairs={{0,2},{1,3},{2,0},{3,1},{4,6},{5,7},{6,4},{7,5},{8,10},{9,11},{10,... | collective-permute-start | bytes 3932168 | tf_op jit(solution)/shard_map/ppermute | solution.py:123
  125.0 36.7 %collective-permute-start.6 = (bf16[640,1024]{1,0:T(8,128)(2,1)}, bf16[640,1024]{1,0:T(8,128)(2,1)}, u32[]{:S(2)}, u32[]{:S(2)}) collective-permute-start(bf16[640,1024]{1,0:T(8,128)(2,1)} %pad_maximum_fusion.refs_0_), channel_id=1, source_target_pairs={{0,1},{1,0},{2,3},{3,2},{4,5},{5,4},{6,7},{7,6},{8,9},{9,8},{10,11... | collective-permute-start | bytes 3932168 | tf_op jit(solution)/shard_map/ppermute | solution.py:123
  125.0 36.7 %collective-permute-start.8 = (bf16[640,1024]{1,0:T(8,128)(2,1)}, bf16[640,1024]{1,0:T(8,128)(2,1)}, u32[]{:S(2)}, u32[]{:S(2)}) collective-permute-start(bf16[640,1024]{1,0:T(8,128)(2,1)} %constant_dynamic-update-slice_fusion.refs_2_), channel_id=1, source_target_pairs={{0,1},{1,0},{2,3},{3,2},{4,5},{5,4},{6,7},{7,6},{8,9},{9,8},{10,11... | collective-permute-start | bytes 3932168 | tf_op jit(solution)/shard_map/ppermute | solution.py:123
  148.5 13.3 %collective-permute-start.7 = (bf16[640,1024]{1,0:T(8,128)(2,1)}, bf16[640,1024]{1,0:T(8,128)(2,1)}, u32[]{:S(2)}, u32[]{:S(2)}) collective-permute-start(bf16[640,1024]{1,0:T(8,128)(2,1)} %collective-permute-done.2.refs_1_), channel_id=1, source_target_pairs={{0,1},{1,0},{2,3},{3,2},{4,5},{5,4},{6,7},{7,6},{8,9},{9,8},{10,11... | collective-permute-start | bytes 3932168 | tf_op jit(solution)/shard_map/ppermute | solution.py:123
  150.1 11.7 %collective-permute-start.9 = (bf16[640,1024]{1,0:T(8,128)(2,1)}, bf16[640,1024]{1,0:T(8,128)(2,1)}, u32[]{:S(2)}, u32[]{:S(2)}) collective-permute-start(bf16[640,1024]{1,0:T(8,128)(2,1)} %collective-permute-done.5.refs_3_), channel_id=1, source_target_pairs={{0,1},{1,0},{2,3},{3,2},{4,5},{5,4},{6,7},{7,6},{8,9},{9,8},{10,11... | collective-permute-start | bytes 3932168 | tf_op jit(solution)/shard_map/ppermute | solution.py:123
  150.1 1.2 copy-start.4
  151.3 10.3 %copy-start.7 = (bf16[1024]{0:T(1024)(128)(2,1)S(1)}, bf16[1024]{0:T(1024)(128)(2,1)}, u32[]{:S(2)}) copy-start(bf16[1024]{0:T(1024)(128)(2,1)} %param.9) | copy-start | bytes 6148
  157.1 0.8 copy-start.3
  157.9 18.2 %all-to-all-start.1 = ((bf16[16,16,1024]{2,1,0:T(8,128)(2,1)}), bf16[16,16,1024]{2,1,0:T(8,128)(2,1)S(1)}, u32[]{:S(2)}, u32[]{:S(2)}) async-start(bf16[16,16,1024]{2,1,0:T(8,128)(2,1)} %bitcast.11), calls=%async_computation.1 | async-start | bytes 1048576 | tf_op jit(solution)/shard_map/all_to_all | solution.py:249

commit v2 on v1

--- a/solution.py
+++ b/solution.py
@@ -37,6 +37,10 @@
     return holder * capacity + rank, local
 
 
+def _step(width):
+    return 1280 if width % 1280 == 0 else width
+
+
 def _pack_kernel(adapters_held, capacity, slot_ref, adapter_ref, tokens_ref, out_ref, place_ref):
     rows, width = tokens_ref.shape
     places = out_ref.shape[0]
@@ -47,7 +51,7 @@
         jnp.where(sits, (local + 1).astype(F32), 0.0), axis=1, keepdims=True
     )
     chosen = sits.astype(F32).astype(BF16)
-    step = 1024 if width % 1024 == 0 else width
+    step = _step(width)
     for start in range(0, width, step):
         out_ref[:, start : start + step] = jnp.dot(
             chosen, tokens_ref[:, start : start + step], preferred_element_type=F32
@@ -123,8 +127,7 @@
     return lax.ppermute(x, axis, [(i, i ^ bit) for i in range(size)])
 
 
-def gather_weights(weights):
-    size = lax.axis_size("wide")
+def gather_weights(weights, size):
     half = weights.shape[0] // 2
     mine = lax.axis_index("parts") * half
     current = lax.dynamic_slice_in_dim(weights, mine, half, 0)
@@ -155,49 +158,6 @@
     return pieces
 
 
-def _base_kernel(marks, me_ref, *refs):
-    count = len(marks)
-    pieces, tokens_ref, out_ref, held_ref = refs[:count], refs[count], refs[count + 1], refs[count + 2]
-    wide, parts = me_ref[0], me_ref[1]
-    rows = held_ref.shape[1]
-    for piece, known in zip(pieces, marks, strict=True):
-        for i, (w, p) in enumerate(known):
-            place = (wide ^ w) * 2 + (parts ^ p)
-            held_ref[place] = piece[i * rows : (i + 1) * rows, :]
-    width, columns = tokens_ref.shape[1], out_ref.shape[1]
-    together = 4
-    depth = together * rows
-    out_ref[...] = jnp.zeros_like(out_ref)
-
-    @pl.loop(0, width // depth)
-    def _(k):
-        block = held_ref[pl.ds(k * together, together)].reshape(depth, columns)
-        left = tokens_ref[:, pl.ds(pl.multiple_of(k * depth, LANES), depth)]
-        out_ref[...] += jnp.dot(left, block, preferred_element_type=F32)
-
-
-def base_product(tokens, pieces, rows):
-    marks = [known for _, known in pieces]
-    columns = pieces[0][0].shape[1]
-    width = tokens.shape[1]
-    me = jnp.stack([lax.axis_index("wide"), lax.axis_index("parts")]).astype(jnp.int32)
-    vmem = pl.BlockSpec(memory_space=pltpu.VMEM)
-    return pl.pallas_call(
-        functools.partial(_base_kernel, marks),
-        in_specs=[pl.BlockSpec(memory_space=pltpu.SMEM)] + [vmem] * (len(pieces) + 1),
-        out_specs=vmem,
-        out_shape=jax.ShapeDtypeStruct((tokens.shape[0], columns), F32),
-        scratch_shapes=[pltpu.VMEM((width // rows, rows, columns), BF16)],
-        compiler_params=pltpu.CompilerParams(vmem_limit_bytes=VMEM_LIMIT),
-        cost_estimate=pl.CostEstimate(
-            flops=2 * tokens.shape[0] * width * columns,
-            bytes_accessed=2 * width * columns,
-            transcendentals=0,
-        ),
-        name="base_product",
-    )(me, *[x for x, _ in pieces], tokens)
-
-
 def _finish_kernel(base_ref, bias_ref, returned_ref, place_ref, out_ref):
     places = returned_ref.shape[0]
     rows = base_ref.shape[0]
@@ -215,6 +175,243 @@
         compiler_params=pltpu.CompilerParams(vmem_limit_bytes=VMEM_LIMIT),
         name="add_terms",
     )(base, bias, returned, place)
+
+
+def _pack_direct_kernel(adapters_held, capacity, me_ref, slot_ref, adapter_ref, tokens_ref, out_ref, place_ref):
+    rows, width = tokens_ref.shape
+    places = out_ref.shape[0]
+    place, _ = _row_places(slot_ref, adapter_ref, adapters_held, capacity)
+    place_ref[...] = jnp.broadcast_to(place, place_ref.shape)
+    sits = lax.broadcasted_iota(jnp.int32, (places, rows), 0) == place
+    chosen = sits.astype(F32).astype(BF16)
+    step = _step(width)
+    for start in range(0, width, step):
+        out_ref[:, start : start + step] = jnp.dot(
+            chosen, tokens_ref[:, start : start + step], preferred_element_type=F32
+        ).astype(BF16)
+
+
+def pack_direct(half_index, slots, adapters, tokens, adapters_held, capacity, places):
+    rows, width = tokens.shape[0], tokens.shape[1] // 2
+    adapters_all = slots.shape[1]
+    return pl.pallas_call(
+        functools.partial(_pack_direct_kernel, adapters_held, capacity),
+        grid_spec=pltpu.PrefetchScalarGridSpec(
+            num_scalar_prefetch=1,
+            grid=(1,),
+            in_specs=[
+                pl.BlockSpec((1, adapters_all), lambda i, me: (0, 0)),
+                pl.BlockSpec((1, rows), lambda i, me: (0, 0)),
+                pl.BlockSpec((rows, width), lambda i, me: (0, me[0])),
+            ],
+            out_specs=[
+                pl.BlockSpec((places, width), lambda i, me: (0, 0)),
+                pl.BlockSpec((8, rows), lambda i, me: (0, 0)),
+            ],
+        ),
+        out_shape=(
+            jax.ShapeDtypeStruct((places, width), BF16),
+            jax.ShapeDtypeStruct((8, rows), jnp.int32),
+        ),
+        compiler_params=pltpu.CompilerParams(vmem_limit_bytes=VMEM_LIMIT),
+        cost_estimate=pl.CostEstimate(
+            flops=2 * places * rows * width,
+            bytes_accessed=2 * (rows + places) * width,
+            transcendentals=0,
+        ),
+        name="pack_direct",
+    )(half_index, slots, adapters, tokens)
+
+
+def _pack_route_kernel(
+    adapters_held, capacity, me_ref, slot_ref, own_ref, other_ref, far_ref, came_ref, out_ref
+):
+    rows, width = far_ref.shape
+    places = out_ref.shape[0]
+    first = me_ref[0] * (places // 2)
+    at = lax.broadcasted_iota(jnp.int32, (places, rows), 0)
+    holder = at // (2 * capacity)
+    rank = at % (2 * capacity)
+    chosen, labels = [], 0.0
+    for adapter_ref, shift in ((own_ref, 0), (other_ref, capacity)):
+        place, local = _row_places(slot_ref, adapter_ref, adapters_held, capacity)
+        here = (rank >= shift) & (rank < shift + capacity)
+        sits = here & (first + holder * capacity + rank - shift == place)
+        labels += jnp.sum(jnp.where(sits, (local + 1).astype(F32), 0.0), axis=1, keepdims=True)
+        chosen.append(sits.astype(F32).astype(BF16))
+    step = _step(width)
+    for start in range(0, width, step):
+        cut = slice(start, start + step)
+        out_ref[:, cut] = (
+            jnp.dot(chosen[0], far_ref[:, cut], preferred_element_type=F32)
+            + jnp.dot(chosen[1], came_ref[:, cut], preferred_element_type=F32)
+        ).astype(BF16)
+    out_ref[:, width:] = jnp.broadcast_to(labels, (places, LANES)).astype(BF16)
+
+
+def pack_route(half_index, slots, own, other, far, came, adapters_held, capacity, places):
+    rows, width = far.shape
+    vmem = pl.BlockSpec(memory_space=pltpu.VMEM)
+    return pl.pallas_call(
+        functools.partial(_pack_route_kernel, adapters_held, capacity),
+        in_specs=[pl.BlockSpec(memory_space=pltpu.SMEM)] + [vmem] * 5,
+        out_specs=vmem,
+        out_shape=jax.ShapeDtypeStruct((places, width + LANES), BF16),
+        compiler_params=pltpu.CompilerParams(vmem_limit_bytes=VMEM_LIMIT),
+        cost_estimate=pl.CostEstimate(
+            flops=4 * places * rows * width,
+            bytes_accessed=2 * (2 * rows + places) * width,
+            transcendentals=0,
+        ),
+        name="pack_route",
+    )(half_index, slots, own, other, far, came)
+
+
+def _split_adapter_kernel(me_ref, direct_ref, routed_ref, shrink_ref, expand_ref, out_ref):
+    senders, capacity, width = direct_ref.shape
+    ranks = expand_ref.shape[0]
+    half = senders // 2
+    me = me_ref[0]
+    rows = half * capacity
+    for mirror in (0, 1):
+        block = me if mirror == 0 else 1 - me
+        direct = direct_ref[pl.ds(block * half, half)].reshape(rows, width)
+        cut = slice(mirror * capacity, (mirror + 1) * capacity)
+        routed = routed_ref[:, cut, :width].reshape(rows, width)
+        label = routed_ref[:, cut, width:].reshape(rows, LANES)[:, :1].astype(F32)
+        at = pl.multiple_of(block * width, LANES)
+        past = pl.multiple_of((1 - block) * width, LANES)
+        total = jnp.dot(direct, shrink_ref[pl.ds(at, width), :], preferred_element_type=F32)
+        total += jnp.dot(routed, shrink_ref[pl.ds(past, width), :], preferred_element_type=F32)
+        owner = lax.broadcasted_iota(jnp.int32, (rows, ranks), 1) // ADAPTER_RANK + 1
+        shrunk = jnp.where(label == owner.astype(F32), total, 0.0).astype(BF16)
+        terms = jnp.dot(shrunk, expand_ref[...], preferred_element_type=F32).astype(BF16)
+        out_ref[pl.ds(block * half, half)] = terms.reshape(half, capacity, terms.shape[1])
+
+
+def split_adapter_terms(half_index, direct, routed, shrink, expand):
+    senders, capacity, _ = direct.shape
+    places = senders * capacity
+    width, ranks = shrink.shape
+    columns = expand.shape[1]
+    vmem = pl.BlockSpec(memory_space=pltpu.VMEM)
+    return pl.pallas_call(
+        _split_adapter_kernel,
+        in_specs=[pl.BlockSpec(memory_space=pltpu.SMEM)] + [vmem] * 4,
+        out_specs=vmem,
+        out_shape=jax.ShapeDtypeStruct((senders, capacity, columns), BF16),
+        compiler_params=pltpu.CompilerParams(vmem_limit_bytes=VMEM_LIMIT),
+        cost_estimate=pl.CostEstimate(
+            flops=2 * places * ranks * (width + columns),
+            bytes_accessed=2 * (places + ranks) * (width + columns),
+            transcendentals=0,
+        ),
+        name="adapter_terms",
+    )(half_index, direct, routed, shrink, expand)
+
+
+def _half_base_kernel(marks, me_ref, *refs):
+    count = len(marks)
+    pieces = refs[:count]
+    tokens_ref, came_ref, own_ref, other_ref, held_ref, left_ref = refs[count:]
+    parts, inside, half_index = me_ref[0], me_ref[1], me_ref[2]
+    rows = held_ref.shape[1]
+    for piece, known in zip(pieces, marks, strict=True):
+        for i, (w, p) in enumerate(known):
+            held_ref[(inside ^ w) * 2 + (parts ^ p)] = piece[i * rows : (i + 1) * rows, :]
+    own_rows, width = came_ref.shape
+    columns = own_ref.shape[1]
+    left_ref[:own_rows, :] = tokens_ref[:, pl.ds(pl.multiple_of(half_index * width, LANES), width)]
+    left_ref[own_rows:, :] = came_ref[...]
+    step = 256 if columns % 256 == 0 else columns
+
+    for start in range(0, columns, step):
+        block = held_ref[:, :, start : start + step].reshape(width, step)
+        product = jnp.dot(left_ref[...], block, preferred_element_type=F32)
+        own_ref[:, start : start + step] = product[:own_rows]
+        other_ref[:, start : start + step] = product[own_rows:].astype(BF16)
+
+
+def half_base_product(me, tokens, came, pieces, rows):
+    marks = [known for _, known in pieces]
+    columns = pieces[0][0].shape[1]
+    own_rows, width = came.shape
+    vmem = pl.BlockSpec(memory_space=pltpu.VMEM)
+    return pl.pallas_call(
+        functools.partial(_half_base_kernel, marks),
+        in_specs=[pl.BlockSpec(memory_space=pltpu.SMEM)] + [vmem] * (len(pieces) + 2),
+        out_specs=(vmem, vmem),
+        out_shape=(
+            jax.ShapeDtypeStruct((own_rows, columns), F32),
+            jax.ShapeDtypeStruct((own_rows, columns), BF16),
+        ),
+        scratch_shapes=[
+            pltpu.VMEM((width // rows, rows, columns), BF16),
+            pltpu.VMEM((2 * own_rows, width), BF16),
+        ],
+        compiler_params=pltpu.CompilerParams(vmem_limit_bytes=VMEM_LIMIT),
+        cost_estimate=pl.CostEstimate(
+            flops=4 * own_rows * width * columns,
+            bytes_accessed=2 * width * columns,
+            transcendentals=0,
+        ),
+        name="half_base_product",
+    )(me, *[x for x, _ in pieces], tokens, came)
+
+
+def _split_finish_kernel(own_ref, other_ref, bias_ref, returned_ref, place_ref, out_ref):
+    places = returned_ref.shape[0]
+    rows = own_ref.shape[0]
+    sits = lax.broadcasted_iota(jnp.int32, (places, rows), 0) == place_ref[:1, :]
+    chosen = sits.astype(F32).T.astype(BF16)
+    terms = jnp.dot(chosen, returned_ref[...], preferred_element_type=F32)
+    total = own_ref[...] + other_ref[...].astype(F32) + bias_ref[...].astype(F32) + 2.0 * terms
+    out_ref[...] = total.astype(BF16)
+
+
+def split_finish(own, other, bias, returned, place):
+    return pl.pallas_call(
+        _split_finish_kernel,
+        out_shape=jax.ShapeDtypeStruct(own.shape, BF16),
+        compiler_params=pltpu.CompilerParams(vmem_limit_bytes=VMEM_LIMIT),
+        name="add_terms",
+    )(own, other, bias, returned, place)
+
+
+def split_plan(tokens, weights, bias, shrink, expand, slots, adapters, adapters_held, capacity):
+    rows, width = tokens.shape
+    holders = lax.axis_size("wide")
+    half = holders // 2
+    places = holders * capacity
+    columns = expand.shape[1]
+    wide, parts = lax.axis_index("wide"), lax.axis_index("parts")
+    half_index = wide // half
+    me = half_index[None].astype(jnp.int32)
+
+    far = lax.dynamic_slice_in_dim(tokens, (1 - half_index) * (width // 2), width // 2, 1)
+    came = swap(far, "wide", half)
+    other_adapters = swap(adapters, "wide", half)
+    outgoing, place = pack_direct(me, slots, adapters, tokens, adapters_held, capacity, places)
+    direct = lax.all_to_all(
+        outgoing.reshape(holders, capacity, width // 2), "wide", split_axis=0, concat_axis=0, tiled=True
+    )
+    pieces = gather_weights(weights, half)
+    inside = pack_route(me, slots, adapters, other_adapters, far, came, adapters_held, capacity, places)
+    groups = [list(range(half)), list(range(half, holders))]
+    routed = lax.all_to_all(
+        inside.reshape(half, 2 * capacity, width // 2 + LANES),
+        "wide",
+        split_axis=0,
+        concat_axis=0,
+        tiled=True,
+        axis_index_groups=groups,
+    )
+    who = jnp.stack([parts, wide % half, half_index]).astype(jnp.int32)
+    own, other = half_base_product(who, tokens, came, pieces, weights.shape[0] // 2)
+    other = swap(other, "wide", half)
+    terms = split_adapter_terms(me, direct, routed, shrink, expand)
+    returned = lax.all_to_all(terms, "wide", split_axis=0, concat_axis=0, tiled=True)
+    return split_finish(own, other, bias, returned.reshape(places, columns), place)
 
 
 def per_device(
@@ -233,23 +430,23 @@
     adapters_held = expand_factors.shape[0] // ADAPTER_RANK
     columns = expand_factors.shape[1]
 
-    outgoing, place = pack(
-        adapter_slot_index[None, :], row_adapter_index[None, :], tokens, adapters_held, capacity, places
-    )
+    slots, adapters, bias = adapter_slot_index[None, :], row_adapter_index[None, :], key_bias_vector[None, :]
+    half = key_weight_matrix.shape[0] // 2
+    if holders >= 8 and capacity % 16 == 0 and half % 16 == 0 and width % (2 * LANES) == 0:
+        return split_plan(
+            tokens, key_weight_matrix, bias, shrink_factors, expand_factors, slots, adapters, adapters_held, capacity
+        )
+    outgoing, place = pack(slots, adapters, tokens, adapters_held, capacity, places)
     arrived = lax.all_to_all(
         outgoing.reshape(holders, capacity, width + LANES), "wide", split_axis=0, concat_axis=0, tiled=True
     )
-    half = key_weight_matrix.shape[0] // 2
-    if half % 16 == 0 and (4 * half) % LANES == 0:
-        base = base_product(tokens, gather_weights(key_weight_matrix), half)
-    else:
-        gathered = lax.all_gather(key_weight_matrix, "wide", axis=0, tiled=True)
-        base = jnp.dot(tokens, gathered, preferred_element_type=F32)
+    gathered = lax.all_gather(key_weight_matrix, "wide", axis=0, tiled=True)
+    base = jnp.dot(tokens, gathered, preferred_element_type=F32)
     terms = adapter_terms(arrived.reshape(places, width + LANES), shrink_factors, expand_factors)
     returned = lax.all_to_all(
         terms.reshape(holders, capacity, columns), "wide", split_axis=0, concat_axis=0, tiled=True
     )
-    return finish(base, key_bias_vector[None, :], returned.reshape(places, columns), place)
+    return finish(base, bias, returned.reshape(places, columns), place)
 
 
 def solution(mesh):

time: 178 us -> 167 us (0.938)
  waiting for transfers between devices: 132 us -> 116 us
  starting transfers between devices: 19.6 us -> 28.3 us
  Pallas kernels: 16 us -> 13.4 us
    ppermute x10 -> x12, waiting for transfers between devices: 126 us -> 116 us  [swap(): return lax.ppermute(x, axis, [(i, i ^ bit) for i in range(size)])]
    all_to_all x2 -> x3, waiting for transfers between devices: 6.19 us -> 0.01 us  [the longest x1 0.01 us: split_plan(): lax.all_to_all(outgoing.reshape(holders, capacity, width // 2), 'wide', s...]
    ppermute x10 -> x12, starting transfers between devices: 8.48 us -> 13.7 us  [swap(): return lax.ppermute(x, axis, [(i, i ^ bit) for i in range(size)])]
    all_to_all x2 -> x3, starting transfers between devices: 11.1 us -> 14.7 us  [the longest x1 7.51 us: split_plan(): lax.all_to_all(outgoing.reshape(holders, capacity, width // 2), 'wide', s...]
    pallas_call x4 -> x5, Pallas kernels: 16 us -> 13.4 us  [the longest x1 4.91 us: half_base_product(): pl.pallas_call(functools.partial(_half_base_kernel, marks), in_specs=[pl....]
    unnamed x17 -> x25, local copies, waits for them, and re-layouts: 7.15 us -> 6.6 us
  transfers between devices with their start and end apart: 12 -> 15, of which waited for: 6 -> 6; matrix products, arithmetic and copies ran while one was open for 2% -> 2% of each run, Pallas kernels for 8% -> 7%
where the time goes in v2:
time: 167 us; the launch traced here: 166 us
  waiting for transfers between devices  116 us (69%)
  starting transfers between devices  28.3 us (17%)
  Pallas kernels  13.4 us (8%)
  local copies, waits for them, and re-layouts  7.41 us (4%)
    ppermute x12, waiting for transfers between devices, swap(): return lax.ppermute(x, axis, [(i, i ^ bit) for i in range(size)])  116 us
    ppermute x12, starting transfers between devices, swap(): return lax.ppermute(x, axis, [(i, i ^ bit) for i in range(size)])  13.7 us
    all_to_all x1, starting transfers between devices, split_plan(): lax.all_to_all(outgoing.reshape(holders, capacity, width // 2), 'wide', s...  7.51 us
    unnamed x25, local copies, waits for them, and re-layouts  6.6 us
    pallas_call x1, Pallas kernels, half_base_product(): pl.pallas_call(functools.partial(_half_base_kernel, marks), in_specs=[pl....  4.91 us
    pallas_call x1, Pallas kernels, split_adapter_terms(): pl.pallas_call(_split_adapter_kernel, in_specs=[pl.BlockSpec(memory_space...  4.51 us
    all_to_all x1, starting transfers between devices, split_plan(): lax.all_to_all(inside.reshape(half, 2 * capacity, width // 2 + LANES), 'w...  3.57 us
    all_to_all x1, starting transfers between devices, split_plan(): lax.all_to_all(terms, 'wide', split_axis=0, concat_axis=0, tiled=True)  3.57 us
  transfers between devices with their start and end apart: 15, of which 6 were waited for; matrix products, arithmetic and copies ran while one was open for 2% of the time, Pallas kernels for 7%

profile of v2, /device:TPU:0, one launch (start us, length us, event | category | flops | bytes accessed | tf_op | source)
XLA Modules:
  0.0 166.5 jit_solution(2242226649002562837)
XLA Ops:
  0.0 1.4 copy-done.1
  3.5 1.1 copy-done.5
  4.6 7.5 %all-to-all-start = ((bf16[16,16,2560]{2,1,0:T(8,128)(2,1)}), bf16[16,16,2560]{2,1,0:T(8,128)(2,1)S(1)}, u32[]{:S(2)}, u32[]{:S(2)}) async-start(bf16[16,16,2560]{2,1,0:T(8,128)(2,1)} %bitcast.9), calls=%async_computation | async-start | bytes 2621440 | tf_op jit(solution)/shard_map/all_to_all | solution.py:395
  12.2 2.9 %collective-permute-start.9 = (bf16[128,2560]{1,0:T(8,128)(2,1)S(1)}, bf16[128,2560]{1,0:T(8,128)(2,1)S(1)}, u32[]{:S(2)}, u32[]{:S(2)}) collective-permute-start(bf16[128,2560]{1,0:T(8,128)(2,1)S(1)} %constant_dynamic-slice_fusion.far_ref), channel_id=1, source_target_pairs={{0,8},{1,9},{2,10},{3,11},{4,12},{5,13},{6,14},{7,15},{8,0},{9,1},... | collective-permute-start | bytes 1966088 | tf_op jit(solution)/shard_map/ppermute | solution.py:127
  15.6 56.9 %collective-permute-done.11.other_ref = s32[1,128]{1,0:T(1,128)S(1)} collective-permute-done((s32[1,128]{1,0:T(1,128)S(1)}, s32[1,128]{1,0:T(1,128)S(1)}, u32[]{:S(2)}, u32[]{:S(2)}) %collective-permute-start.11) | collective-permute-done | bytes 544 | tf_op jit(solution)/shard_map/ppermute | solution.py:127
  72.5 2.3 %pack_route.1 = bf16[256,2688]{1,0:T(8,128)(2,1)} custom-call(s32[1]{0:T(128)} %bitcast.2.me_ref, s32[1,512]{1,0:T(1,128)S(1)} %bitcast.11, s32[1,128]{1,0:T(1,128)S(1)} %bitcast.14, s32[1,128]{1,0:T(1,128)S(1)} %collective-permute-done.11.other_ref, bf16[128,2560]{1,0:T(8,128)(2,1)S(1)} %constant_dynamic-slice_fusion.far_ref, ...), custom_call_target="tpu_custom_call" | custom-call | flops 335544320 | bytes 2621440 | tf_op jit(solution)/shard_map/pack_route/pallas_call | solution.py:255
  74.7 3.6 %all-to-all-start.1 = ((bf16[8,32,2688]{2,1,0:T(8,128)(2,1)}), bf16[8,32,2688]{2,1,0:T(8,128)(2,1)S(1)}, u32[]{:S(2)}, u32[]{:S(2)}) async-start(bf16[8,32,2688]{2,1,0:T(8,128)(2,1)} %bitcast.6), calls=%async_computation.1 | async-start | bytes 2752512 | tf_op jit(solution)/shard_map/all_to_all | solution.py:401
  78.4 2.0 %collective-permute-start.2 = (bf16[160,1024]{1,0:T(8,128)(2,1)S(1)}, bf16[160,1024]{1,0:T(8,128)(2,1)S(1)}, u32[]{:S(2)}, u32[]{:S(2)}) collective-permute-start(bf16[160,1024]{1,0:T(8,128)(2,1)S(1)} %constant_dynamic-slice_fusion.1), channel_id=1, source_target_pairs={{0,4},{1,5},{2,6},{3,7},{4,0},{5,1},{6,2},{7,3},{8,12},{9,13},{10,... | collective-permute-start | bytes 983048 | tf_op jit(solution)/shard_map/ppermute | solution.py:127
  80.4 1.5 collective-permute-start
  81.8 21.4 %collective-permute-done.2 = bf16[160,1024]{1,0:T(8,128)(2,1)S(1)} collective-permute-done((bf16[160,1024]{1,0:T(8,128)(2,1)S(1)}, bf16[160,1024]{1,0:T(8,128)(2,1)S(1)}, u32[]{:S(2)}, u32[]{:S(2)}) %collective-permute-start.2) | collective-permute-done | bytes 327712 | tf_op jit(solution)/shard_map/ppermute | solution.py:127
  103.2 1.5 collective-permute-start.3
  104.7 0.9 pad_maximum_fusion.refs_0_
  106.9 7.0 %collective-permute-done.3 = bf16[160,1024]{1,0:T(8,128)(2,1)S(1)} collective-permute-done((bf16[160,1024]{1,0:T(8,128)(2,1)S(1)}, bf16[160,1024]{1,0:T(8,128)(2,1)S(1)}, u32[]{:S(2)}, u32[]{:S(2)}) %collective-permute-start.3) | collective-permute-done | bytes 327712 | tf_op jit(solution)/shard_map/ppermute | solution.py:127
  114.6 1.5 collective-permute-start.4
  116.6 10.1 %collective-permute-done.1.refs_1_ = bf16[320,1024]{1,0:T(8,128)(2,1)} collective-permute-done((bf16[320,1024]{1,0:T(8,128)(2,1)}, bf16[320,1024]{1,0:T(8,128)(2,1)}, u32[]{:S(2)}, u32[]{:S(2)}) %collective-permute-start.1) | collective-permute-done | bytes 655392 | tf_op jit(solution)/shard_map/ppermute | solution.py:127
  126.6 2.3 %collective-permute-done.4.refs_3_ = bf16[320,1024]{1,0:T(8,128)(2,1)} collective-permute-done((bf16[320,1024]{1,0:T(8,128)(2,1)}, bf16[320,1024]{1,0:T(8,128)(2,1)}, u32[]{:S(2)}, u32[]{:S(2)}) %collective-permute-start.4) | collective-permute-done | bytes 655392 | tf_op jit(solution)/shard_map/ppermute | solution.py:127
  128.9 1.2 copy-done.6
  130.2 4.5 %adapter_terms.1 = bf16[16,16,1024]{2,1,0:T(8,128)(2,1)S(1)} custom-call(s32[1]{0:T(128)} %bitcast.2.me_ref, bf16[16,16,2560]{2,1,0:T(8,128)(2,1)S(1)} %all-to-all-done.direct_ref, bf16[8,32,2688]{2,1,0:T(8,128)(2,1)S(1)} %all-to-all-done.1.routed_ref, bf16[5120,512]{1,0:T(8,128)(2,1)} %shrink_ref.1, bf16[512,1024]{1,0:T(8,128)(2,1)S(1)} %copy-done.6), custom_call_target="tpu_custom_call" | custom-call | flops 1610612736 | bytes 9437184 | tf_op jit(solution)/shard_map/adapter_terms/pallas_call | solution.py:298
  134.7 0.8 copy-done.4
  135.5 3.6 %all-to-all-start.2 = ((bf16[16,16,1024]{2,1,0:T(8,128)(2,1)}), bf16[16,16,1024]{2,1,0:T(8,128)(2,1)S(1)}, u32[]{:S(2)}, u32[]{:S(2)}) async-start(bf16[16,16,1024]{2,1,0:T(8,128)(2,1)} %copy-done.4), calls=%async_computation.2 | async-start | bytes 1048576 | tf_op jit(solution)/shard_map/all_to_all | solution.py:413
  139.2 4.9 %half_base_product.1 = (f32[128,1024]{1,0:T(8,128)S(1)}, bf16[128,1024]{1,0:T(8,128)(2,1)S(1)}) custom-call(s32[3]{0:T(128)S(1)} %pad_add_fusion.me_ref, bf16[320,1024]{1,0:T(8,128)(2,1)} %pad_maximum_fusion.refs_0_, bf16[320,1024]{1,0:T(8,128)(2,1)} %collective-permute-done.1.refs_1_, bf16[320,1024]{1,0:T(8,128)(2,1)} %constant_dynamic-update-slice_fusion.refs_2_, ...), custom_call_target="tpu_custom_call" | custom-call | flops 1342177280 | bytes 5242880 | tf_op jit(solution)/shard_map/half_base_product/pallas_call | solution.py:340
  144.1 2.8 %collective-permute-start.10 = (bf16[128,1024]{1,0:T(8,128)(2,1)S(1)}, bf16[128,1024]{1,0:T(8,128)(2,1)S(1)}, u32[]{:S(2)}, u32[]{:S(2)}) collective-permute-start(bf16[128,1024]{1,0:T(8,128)(2,1)S(1)} %get-tuple-element.10), channel_id=1, source_target_pairs={{0,8},{1,9},{2,10},{3,11},{4,12},{5,13},{6,14},{7,15},{8,0},{9,1},... | collective-permute-start | bytes 786440 | tf_op jit(solution)/shard_map/ppermute | solution.py:127
  146.9 18.6 %collective-permute-done.10.other_ref = bf16[128,1024]{1,0:T(8,128)(2,1)S(1)} collective-permute-done((bf16[128,1024]{1,0:T(8,128)(2,1)S(1)}, bf16[128,1024]{1,0:T(8,128)(2,1)S(1)}, u32[]{:S(2)}, u32[]{:S(2)}) %collective-permute-start.10) | collective-permute-done | bytes 262176 | tf_op jit(solution)/shard_map/ppermute | solution.py:127
  165.5 1.0 add_terms.1
  (42 shorter events, 5.3 us)
Async XLA Ops:
  0.0 78.3 %copy-start = (bf16[320,1024]{1,0:T(8,128)(2,1)S(1)}, bf16[320,1024]{1,0:T(8,128)(2,1)}, u32[]{:S(2)}) copy-start(bf16[320,1024]{1,0:T(8,128)(2,1)} %param.8) | copy-start | bytes 1966084
  0.0 1.4 copy-start.1
  3.5 1.1 copy-start.5
  4.6 7.6 %copy-start.2 = (bf16[128,5120]{1,0:T(8,128)(2,1)S(1)}, bf16[128,5120]{1,0:T(8,128)(2,1)}, u32[]{:S(2)}) copy-start(bf16[128,5120]{1,0:T(8,128)(2,1)} %tokens_ref.1) | copy-start | bytes 3932164
  4.6 70.2 %all-to-all-start = ((bf16[16,16,2560]{2,1,0:T(8,128)(2,1)}), bf16[16,16,2560]{2,1,0:T(8,128)(2,1)S(1)}, u32[]{:S(2)}, u32[]{:S(2)}) async-start(bf16[16,16,2560]{2,1,0:T(8,128)(2,1)} %bitcast.9), calls=%async_computation | async-start | bytes 2621440 | tf_op jit(solution)/shard_map/all_to_all | solution.py:395
  12.1 3.0 %copy-start.10 = (s32[128]{0:T(128)S(1)}, s32[128]{0:T(128)}, u32[]{:S(2)}) copy-start(s32[128]{0:T(128)} %param.13) | copy-start | bytes 1540
  12.1 60.4 %copy-start.8 = (s32[512]{0:T(512)S(1)}, s32[512]{0:T(512)}, u32[]{:S(2)}) copy-start(s32[512]{0:T(512)} %param.12) | copy-start | bytes 6148
  12.2 60.3 %collective-permute-start.9 = (bf16[128,2560]{1,0:T(8,128)(2,1)S(1)}, bf16[128,2560]{1,0:T(8,128)(2,1)S(1)}, u32[]{:S(2)}, u32[]{:S(2)}) collective-permute-start(bf16[128,2560]{1,0:T(8,128)(2,1)S(1)} %constant_dynamic-slice_fusion.far_ref), channel_id=1, source_target_pairs={{0,8},{1,9},{2,10},{3,11},{4,12},{5,13},{6,14},{7,15},{8,0},{9,1},... | collective-permute-start | bytes 1966088 | tf_op jit(solution)/shard_map/ppermute | solution.py:127
  15.1 57.4 %collective-permute-start.11 = (s32[1,128]{1,0:T(1,128)S(1)}, s32[1,128]{1,0:T(1,128)S(1)}, u32[]{:S(2)}, u32[]{:S(2)}) collective-permute-start(s32[1,128]{1,0:T(1,128)S(1)} %bitcast.13), channel_id=1, source_target_pairs={{0,8},{1,9},{2,10},{3,11},{4,12},{5,13},{6,14},{7,15},{8,0},{9,1},... | collective-permute-start | bytes 1544 | tf_op jit(solution)/shard_map/ppermute | solution.py:127
  72.5 2.3 %copy-start.3 = (bf16[128,2560]{1,0:T(8,128)(2,1)}, bf16[128,2560]{1,0:T(8,128)(2,1)S(1)}, u32[]{:S(2)}) copy-start(bf16[128,2560]{1,0:T(8,128)(2,1)S(1)} %collective-permute-done.9.refs_9_.came_ref) | copy-start | bytes 1966084
  74.7 54.2 %all-to-all-start.1 = ((bf16[8,32,2688]{2,1,0:T(8,128)(2,1)}), bf16[8,32,2688]{2,1,0:T(8,128)(2,1)S(1)}, u32[]{:S(2)}, u32[]{:S(2)}) async-start(bf16[8,32,2688]{2,1,0:T(8,128)(2,1)} %bitcast.6), calls=%async_computation.1 | async-start | bytes 2752512 | tf_op jit(solution)/shard_map/all_to_all | solution.py:401
  78.4 24.9 %collective-permute-start.2 = (bf16[160,1024]{1,0:T(8,128)(2,1)S(1)}, bf16[160,1024]{1,0:T(8,128)(2,1)S(1)}, u32[]{:S(2)}, u32[]{:S(2)}) collective-permute-start(bf16[160,1024]{1,0:T(8,128)(2,1)S(1)} %constant_dynamic-slice_fusion.1), channel_id=1, source_target_pairs={{0,4},{1,5},{2,6},{3,7},{4,0},{5,1},{6,2},{7,3},{8,12},{9,13},{10,... | collective-permute-start | bytes 983048 | tf_op jit(solution)/shard_map/ppermute | solution.py:127
  80.4 24.4 %collective-permute-start = (bf16[160,1024]{1,0:T(8,128)(2,1)S(1)}, bf16[160,1024]{1,0:T(8,128)(2,1)S(1)}, u32[]{:S(2)}, u32[]{:S(2)}) collective-permute-start(bf16[160,1024]{1,0:T(8,128)(2,1)S(1)} %constant_dynamic-slice_fusion.1), channel_id=1, source_target_pairs={{0,2},{1,3},{2,0},{3,1},{4,6},{5,7},{6,4},{7,5},{8,10},{9,11},{10,... | collective-permute-start | bytes 983048 | tf_op jit(solution)/shard_map/ppermute | solution.py:127
  103.2 10.6 %collective-permute-start.3 = (bf16[160,1024]{1,0:T(8,128)(2,1)S(1)}, bf16[160,1024]{1,0:T(8,128)(2,1)S(1)}, u32[]{:S(2)}, u32[]{:S(2)}) collective-permute-start(bf16[160,1024]{1,0:T(8,128)(2,1)S(1)} %collective-permute-done.2), channel_id=1, source_target_pairs={{0,16},{16,0},{1,17},{17,1},{2,18},{18,2},{3,19},{19,3},{4,20},{20... | collective-permute-start | bytes 983048 | tf_op jit(solution)/shard_map/ppermute | solution.py:127
  105.6 21.0 %collective-permute-start.1 = (bf16[320,1024]{1,0:T(8,128)(2,1)}, bf16[320,1024]{1,0:T(8,128)(2,1)}, u32[]{:S(2)}, u32[]{:S(2)}) collective-permute-start(bf16[320,1024]{1,0:T(8,128)(2,1)} %pad_maximum_fusion.refs_0_), channel_id=1, source_target_pairs={{0,16},{16,0},{1,17},{17,1},{2,18},{18,2},{3,19},{19,3},{4,20},{20... | collective-permute-start | bytes 1966088 | tf_op jit(solution)/shard_map/ppermute | solution.py:127
  114.6 14.3 %collective-permute-start.4 = (bf16[320,1024]{1,0:T(8,128)(2,1)}, bf16[320,1024]{1,0:T(8,128)(2,1)}, u32[]{:S(2)}, u32[]{:S(2)}) collective-permute-start(bf16[320,1024]{1,0:T(8,128)(2,1)} %constant_dynamic-update-slice_fusion.refs_2_), channel_id=1, source_target_pairs={{0,2},{1,3},{2,0},{3,1},{4,6},{5,7},{6,4},{7,5},{8,10},{9,11},{10,... | collective-permute-start | bytes 1966088 | tf_op jit(solution)/shard_map/ppermute | solution.py:127
  116.1 23.1 %collective-permute-start.5 = (bf16[320,1024]{1,0:T(8,128)(2,1)}, bf16[320,1024]{1,0:T(8,128)(2,1)}, u32[]{:S(2)}, u32[]{:S(2)}) collective-permute-start(bf16[320,1024]{1,0:T(8,128)(2,1)} %pad_maximum_fusion.refs_0_), channel_id=1, source_target_pairs={{0,1},{1,0},{2,3},{3,2},{4,5},{5,4},{6,7},{7,6},{8,9},{9,8},{10,11... | collective-permute-start | bytes 1966088 | tf_op jit(solution)/shard_map/ppermute | solution.py:127
  116.1 23.1 %collective-permute-start.7 = (bf16[320,1024]{1,0:T(8,128)(2,1)}, bf16[320,1024]{1,0:T(8,128)(2,1)}, u32[]{:S(2)}, u32[]{:S(2)}) collective-permute-start(bf16[320,1024]{1,0:T(8,128)(2,1)} %constant_dynamic-update-slice_fusion.refs_2_), channel_id=1, source_target_pairs={{0,1},{1,0},{2,3},{3,2},{4,5},{5,4},{6,7},{7,6},{8,9},{9,8},{10,11... | collective-permute-start | bytes 1966088 | tf_op jit(solution)/shard_map/ppermute | solution.py:127
  126.6 12.5 %collective-permute-start.6 = (bf16[320,1024]{1,0:T(8,128)(2,1)}, bf16[320,1024]{1,0:T(8,128)(2,1)}, u32[]{:S(2)}, u32[]{:S(2)}) collective-permute-start(bf16[320,1024]{1,0:T(8,128)(2,1)} %collective-permute-done.1.refs_1_), channel_id=1, source_target_pairs={{0,1},{1,0},{2,3},{3,2},{4,5},{5,4},{6,7},{7,6},{8,9},{9,8},{10,11... | collective-permute-start | bytes 1966088 | tf_op jit(solution)/shard_map/ppermute | solution.py:127
  128.9 10.3 %collective-permute-start.8 = (bf16[320,1024]{1,0:T(8,128)(2,1)}, bf16[320,1024]{1,0:T(8,128)(2,1)}, u32[]{:S(2)}, u32[]{:S(2)}) collective-permute-start(bf16[320,1024]{1,0:T(8,128)(2,1)} %collective-permute-done.4.refs_3_), channel_id=1, source_target_pairs={{0,1},{1,0},{2,3},{3,2},{4,5},{5,4},{6,7},{7,6},{8,9},{9,8},{10,11... | collective-permute-start | bytes 1966088 | tf_op jit(solution)/shard_map/ppermute | solution.py:127
  128.9 1.2 copy-start.6
  135.5 30.0 %all-to-all-start.2 = ((bf16[16,16,1024]{2,1,0:T(8,128)(2,1)}), bf16[16,16,1024]{2,1,0:T(8,128)(2,1)S(1)}, u32[]{:S(2)}, u32[]{:S(2)}) async-start(bf16[16,16,1024]{2,1,0:T(8,128)(2,1)} %copy-done.4), calls=%async_computation.2 | async-start | bytes 1048576 | tf_op jit(solution)/shard_map/all_to_all | solution.py:413
  139.2 7.8 %copy-start.11 = (bf16[1024]{0:T(1024)(128)(2,1)S(1)}, bf16[1024]{0:T(1024)(128)(2,1)}, u32[]{:S(2)}) copy-start(bf16[1024]{0:T(1024)(128)(2,1)} %param.9) | copy-start | bytes 6148
  144.1 21.4 %collective-permute-start.10 = (bf16[128,1024]{1,0:T(8,128)(2,1)S(1)}, bf16[128,1024]{1,0:T(8,128)(2,1)S(1)}, u32[]{:S(2)}, u32[]{:S(2)}) collective-permute-start(bf16[128,1024]{1,0:T(8,128)(2,1)S(1)} %get-tuple-element.10), channel_id=1, source_target_pairs={{0,8},{1,9},{2,10},{3,11},{4,12},{5,13},{6,14},{7,15},{8,0},{9,1},... | collective-permute-start | bytes 786440 | tf_op jit(solution)/shard_map/ppermute | solution.py:127
  (3 other events, 2.1 us)

commit v3 on v1

v3 whole, which is shorter than its diff:
```python
import functools

import jax
import jax.numpy as jnp
from jax import lax
from jax.experimental import pallas as pl
from jax.experimental.pallas import tpu as pltpu
from jax.sharding import PartitionSpec as P

ADAPTER_RANK = 16
LANES = 128
VMEM_LIMIT = 48 * 1024 * 1024
BASE_PRODUCT = 22 * 10**9
BASE_SUM = 20 * 10**9
F32 = jnp.float32
BF16 = jnp.bfloat16


def _in_team(wide, quarter):
    return wide // (2 * quarter) * quarter + wide % quarter


def _from_team(number, team, quarter):
    return number // quarter * (2 * quarter) + team * quarter + number % quarter


def _row_places(slot_ref, adapter_ref, adapters_held, capacity):
    adapters = slot_ref.shape[1]
    rows = adapter_ref.shape[1]
    held_bits = adapters_held.bit_length() - 1
    slots = slot_ref[...]
    high = jnp.broadcast_to((slots >> 6).astype(F32).astype(BF16), (8, adapters))
    low = jnp.broadcast_to((slots & 63).astype(F32).astype(BF16), (8, adapters))
    picks = lax.broadcasted_iota(jnp.int32, (adapters, rows), 0) == adapter_ref[...]
    picks = picks.astype(F32).astype(BF16)
    slot_high = jnp.dot(high, picks, preferred_element_type=F32)
    slot_low = jnp.dot(low, picks, preferred_element_type=F32)
    slot = (slot_high * 64.0 + slot_low)[:1].astype(jnp.int32)
    holder = slot >> held_bits
    local = slot & (adapters_held - 1)
    across = jnp.broadcast_to(holder.astype(F32), (rows, rows))
    earlier = lax.broadcasted_iota(jnp.int32, (rows, rows), 0) < lax.broadcasted_iota(
        jnp.int32, (rows, rows), 1
    )
    same = jnp.where(earlier & (across.T == across), 1.0, 0.0)
    rank = jnp.sum(same, axis=0, keepdims=True).astype(jnp.int32)
    return holder * capacity + rank, local


def _pack_kernel(adapters_held, capacity, slot_ref, adapter_ref, tokens_ref, out_ref, chosen_ref):
    rows, width = tokens_ref.shape
    places = out_ref.shape[0]
    place, local = _row_places(slot_ref, adapter_ref, adapters_held, capacity)
    sits = lax.broadcasted_iota(jnp.int32, (places, rows), 0) == place
    labels = jnp.sum(
        jnp.where(sits, (local + 1).astype(F32), 0.0), axis=1, keepdims=True
    )
    chosen = sits.astype(F32).astype(BF16)
    chosen_ref[...] = sits.astype(F32).T.astype(BF16)
    step = 1280 if width % 1280 == 0 else width
    for start in range(0, width, step):
        out_ref[:, start : start + step] = jnp.dot(
            chosen, tokens_ref[:, start : start + step], preferred_element_type=F32
        ).astype(BF16)
    out_ref[:, width:] = jnp.broadcast_to(labels, (places, LANES)).astype(BF16)


def pack(slots, adapters, tokens, adapters_held, capacity, places):
    rows, width = tokens.shape
    return pl.pallas_call(
        functools.partial(_pack_kernel, adapters_held, capacity),
        out_shape=(
            jax.ShapeDtypeStruct((places, width + LANES), BF16),
            jax.ShapeDtypeStruct((rows, places), BF16),
        ),
        compiler_params=pltpu.CompilerParams(vmem_limit_bytes=VMEM_LIMIT),
        cost_estimate=pl.CostEstimate(
            flops=2 * places * rows * width,
            bytes_accessed=2 * (rows + places) * width,
            transcendentals=0,
        ),
        name="pack_rows",
    )(slots, adapters, tokens)


def _adapter_kernel(rows_ref, shrink_ref, expand_ref, out_ref):
    places, ranks = rows_ref.shape[0], expand_ref.shape[0]
    width = shrink_ref.shape[0]
    total = jnp.dot(rows_ref[:, :width], shrink_ref[...], preferred_element_type=F32)
    owner = lax.broadcasted_iota(jnp.int32, (places, ranks), 1) // ADAPTER_RANK + 1
    keep = rows_ref[:, width : width + 1].astype(F32) == owner.astype(F32)
    shrunk = jnp.where(keep, total, 0.0).astype(BF16)
    out_ref[...] = jnp.dot(shrunk, expand_ref[...], preferred_element_type=F32).astype(BF16)


def adapter_terms(arrived, shrink, expand):
    places = arrived.shape[0]
    width, ranks = shrink.shape
    columns = expand.shape[1]
    return pl.pallas_call(
        _adapter_kernel,
        out_shape=jax.ShapeDtypeStruct((places, columns), BF16),
        compiler_params=pltpu.CompilerParams(vmem_limit_bytes=VMEM_LIMIT),
        cost_estimate=pl.CostEstimate(
            flops=2 * places * ranks * (width + columns),
            bytes_accessed=2 * (places + ranks) * (width + columns),
            transcendentals=0,
        ),
        name="adapter_terms",
    )(arrived, shrink, expand)


def swap(x, axis, bit):
    size = lax.axis_size(axis)
    return lax.ppermute(x, axis, [(i, i ^ bit) for i in range(size)])


def gather_weights(weights, quarter, came):
    half = weights.shape[0] // 2
    mine = lax.axis_index("parts") * half
    current = lax.dynamic_slice_in_dim(weights, mine, half, 0)
    marks = [(0, 0)]

    def grow(x, known, axis, bit):
        number, parts = (bit, 0) if axis == "wide" else (0, bit)
        across = _from_team(bit, 0, quarter) if axis == "wide" else bit
        return (
            jnp.concatenate([x, swap(x, axis, across)], axis=0),
            known + [(w ^ number, p ^ parts) for w, p in known],
        )

    bit = quarter
    while bit > 2:
        current, marks = grow(current, marks, "wide", bit)
        bit //= 2
    current, _ = lax.optimization_barrier((current, came))
    middle, cut = len(marks) // 2, current.shape[0] // 2
    pieces = []
    for x, known, order in (
        (current[:cut], marks[:middle], (("wide", 2), ("parts", 1))),
        (current[cut:], marks[middle:], (("parts", 1), ("wide", 2))),
    ):
        for axis, bit in order:
            x, known = grow(x, known, axis, bit)
        pieces += [(x, known), (swap(x, "wide", 1), [(w ^ 1, p) for w, p in known])]
    return pieces


def _base_kernel(marks, me_ref, *refs):
    count = len(marks)
    pieces = refs[:count]
    tokens_ref, came_ref, own_ref, other_ref, held_ref, left_ref = refs[count:]
    team, inside, parts = me_ref[0], me_ref[1], me_ref[2]
    rows = held_ref.shape[1]
    for piece, known in zip(pieces, marks, strict=True):
        for i, (w, p) in enumerate(known):
            held_ref[(inside ^ w) * 2 + (parts ^ p)] = piece[i * rows : (i + 1) * rows, :]
    own_rows, width = came_ref.shape
    columns = own_ref.shape[1]
    depth = width // 2
    for upper in (0, 1):
        block = pl.ds(pl.multiple_of((2 * upper + team) * depth, LANES), depth)
        left_ref[:own_rows, upper * depth : (upper + 1) * depth] = tokens_ref[:, block]
    left_ref[own_rows:, :] = came_ref[...]
    step = 256 if columns % 256 == 0 else columns

    for start in range(0, columns, step):
        block = held_ref[:, :, start : start + step].reshape(width, step)
        product = jnp.dot(left_ref[...], block, preferred_element_type=F32)
        own_ref[:, start : start + step] = product[:own_rows]
        other_ref[:, start : start + step] = product[own_rows:].astype(BF16)


def base_product(me, tokens, came, pieces, rows):
    marks = [known for _, known in pieces]
    columns = pieces[0][0].shape[1]
    own_rows, width = came.shape
    vmem = pl.BlockSpec(memory_space=pltpu.VMEM)
    return pl.pallas_call(
        functools.partial(_base_kernel, marks),
        in_specs=[pl.BlockSpec(memory_space=pltpu.SMEM)] + [vmem] * (len(pieces) + 2),
        out_specs=(vmem, vmem),
        out_shape=(
            jax.ShapeDtypeStruct((own_rows, columns), F32),
            jax.ShapeDtypeStruct((own_rows, columns), BF16),
        ),
        scratch_shapes=[
            pltpu.VMEM((width // rows, rows, columns), BF16),
            pltpu.VMEM((2 * own_rows, width), BF16),
        ],
        compiler_params=pltpu.CompilerParams(vmem_limit_bytes=VMEM_LIMIT),
        cost_estimate=pl.CostEstimate(
            flops=BASE_PRODUCT,
            bytes_accessed=2 * width * columns,
            transcendentals=0,
        ),
        name="base_product",
    )(me, *[x for x, _ in pieces], tokens, came)


def _base_sum_kernel(own_ref, other_ref, bias_ref, out_ref):
    out_ref[...] = own_ref[...] + other_ref[...].astype(F32) + bias_ref[...].astype(F32)


def base_sum(own, other, bias):
    return pl.pallas_call(
        _base_sum_kernel,
        out_shape=jax.ShapeDtypeStruct(own.shape, F32),
        cost_estimate=pl.CostEstimate(flops=BASE_SUM, bytes_accessed=10 * own.size, transcendentals=0),
        name="base_sum",
    )(own, other, bias)


def _add_terms_kernel(base_ref, returned_ref, chosen_ref, out_ref):
    terms = jnp.dot(chosen_ref[...], returned_ref[...], preferred_element_type=F32)
    out_ref[...] = (base_ref[...] + 2.0 * terms).astype(BF16)


def add_terms(base, returned, chosen):
    return pl.pallas_call(
        _add_terms_kernel,
        out_shape=jax.ShapeDtypeStruct(base.shape, BF16),
        name="add_terms",
    )(base, returned, chosen)


def per_device(
    tokens,
    key_weight_matrix,
    key_bias_vector,
    shrink_factors,
    expand_factors,
    adapter_slot_index,
    row_adapter_index,
):
    rows, width = tokens.shape
    holders = lax.axis_size("wide")
    capacity = 2 * rows // holders
    places = holders * capacity
    adapters_held = expand_factors.shape[0] // ADAPTER_RANK
    columns = expand_factors.shape[1]

    slots, adapters, bias = adapter_slot_index[None, :], row_adapter_index[None, :], key_bias_vector[None, :]
    outgoing, chosen = pack(slots, adapters, tokens, adapters_held, capacity, places)
    arrived = lax.all_to_all(
        outgoing.reshape(holders, capacity, width + LANES), "wide", split_axis=0, concat_axis=0, tiled=True
    )
    half = key_weight_matrix.shape[0] // 2
    if holders >= 8 and half % 16 == 0 and width % (4 * LANES) == 0:
        quarter, depth = holders // 4, width // 4
        wide, parts = lax.axis_index("wide"), lax.axis_index("parts")
        team = wide // quarter % 2
        far = [lax.dynamic_slice_in_dim(tokens, (2 * upper + 1 - team) * depth, depth, 1) for upper in (0, 1)]
        came = swap(jnp.concatenate(far, axis=1), "wide", quarter)
        pieces = gather_weights(key_weight_matrix, quarter, came)
        me = jnp.stack([team, _in_team(wide, quarter), parts]).astype(jnp.int32)
        own, other = base_product(me, tokens, came, pieces, half)
        arrived, other = lax.optimization_barrier((arrived, other))
        base = base_sum(own, swap(other, "wide", quarter), bias)
    else:
        gathered = lax.all_gather(key_weight_matrix, "wide", axis=0, tiled=True)
        base = jnp.dot(tokens, gathered, preferred_element_type=F32) + bias.astype(F32)
    terms = adapter_terms(arrived.reshape(places, width + LANES), shrink_factors, expand_factors)
    returned = lax.all_to_all(
        terms.reshape(holders, capacity, columns), "wide", split_axis=0, concat_axis=0, tiled=True
    )
    return add_terms(base, returned.reshape(places, columns), chosen)


def solution(mesh):
    placed = (
        P(("parts", "wide"), None),
        P("wide", None),
        P(),
        P(None, ("parts", "wide")),
        P(("parts", "wide"), None),
        P("parts"),
        P(("parts", "wide")),
    )
    return jax.shard_map(
        per_device,
        mesh=mesh,
        in_specs=placed,
        out_specs=P(("parts", "wide"), None),
        check_vma=False,
    )
```

time: 178 us -> 114 us (0.64)
  waiting for transfers between devices: 132 us -> 68 us
  other arithmetic: 1.3 us -> 4.5 us
  starting transfers between devices: 19.6 us -> 17.4 us
    ppermute x10 -> x9, waiting for transfers between devices: 126 us -> 55.5 us  [swap(): return lax.ppermute(x, axis, [(i, i ^ bit) for i in range(size)])]
    all_to_all x1, waiting for transfers between devices: 6.19 us -> 12.5 us  [per_device(): lax.all_to_all(terms.reshape(holders, capacity, columns), 'wide', split_a...]
    all_to_all x1, starting transfers between devices: 7.38 us -> 3.73 us  [per_device(): lax.all_to_all(outgoing.reshape(holders, capacity, width + LANES), 'wide'...]
    pallas_call x1, Pallas kernels: 8.14 us -> 4.91 us  [base_product(): pl.pallas_call(functools.partial(_base_kernel, marks), in_specs=[pl.Block...]
    concatenate x2 -> x6, other arithmetic: 1.23 us -> 4.43 us  [the longest x5 3.54 us: grow(): jnp.concatenate([x, swap(x, axis, across)], axis=0)]
    pallas_call x2 -> x3, Pallas kernels: 6.74 us -> 8.49 us  [the longest x1 4.35 us: adapter_terms(): pl.pallas_call(_adapter_kernel, out_shape=jax.ShapeDtypeStruct((places, c...]
    unnamed x17 -> x24, local copies, waits for them, and re-layouts: 7.15 us -> 6.51 us
    ppermute x10 -> x9, starting transfers between devices: 8.48 us -> 8.31 us  [swap(): return lax.ppermute(x, axis, [(i, i ^ bit) for i in range(size)])]
  transfers between devices with their start and end apart: 12 -> 11, of which waited for: 6 -> 8; matrix products, arithmetic and copies ran while one was open for 2% -> 4% of each run, Pallas kernels for 8% -> 11%
where the time goes in v3:
time: 114 us
  waiting for transfers between devices  68 us (60%)
  starting transfers between devices  17.4 us (15%)
  Pallas kernels  14.5 us (13%)
  local copies, waits for them, and re-layouts  9.08 us (8%)
  other arithmetic  4.5 us (4%)
    ppermute x9, waiting for transfers between devices, swap(): return lax.ppermute(x, axis, [(i, i ^ bit) for i in range(size)])  55.5 us
    all_to_all x1, waiting for transfers between devices, per_device(): lax.all_to_all(terms.reshape(holders, capacity, columns), 'wide', split_a...  12.5 us
    ppermute x9, starting transfers between devices, swap(): return lax.ppermute(x, axis, [(i, i ^ bit) for i in range(size)])  8.31 us
    unnamed x24, local copies, waits for them, and re-layouts  6.51 us
    all_to_all x1, starting transfers between devices, per_device(): lax.all_to_all(terms.reshape(holders, capacity, columns), 'wide', split_a...  5.32 us
    pallas_call x1, Pallas kernels, base_product(): pl.pallas_call(functools.partial(_base_kernel, marks), in_specs=[pl.Block...  4.91 us
    pallas_call x1, Pallas kernels, adapter_terms(): pl.pallas_call(_adapter_kernel, out_shape=jax.ShapeDtypeStruct((places, c...  4.35 us
    all_to_all x1, starting transfers between devices, per_device(): lax.all_to_all(outgoing.reshape(holders, capacity, width + LANES), 'wide'...  3.73 us
  transfers between devices with their start and end apart: 11, of which 8 were waited for; matrix products, arithmetic and copies ran while one was open for 4% of the time, Pallas kernels for 11%

profile of v3, /device:TPU:0, one launch (start us, length us, event | category | flops | bytes accessed | tf_op | source)
XLA Modules:
  0.0 113.6 jit_solution(1330833763268951109)
XLA Ops:
  0.0 1.2 %constant_dynamic-slice_fusion.1 = (bf16[128,1280]{1,0:T(8,128)(2,1)S(1)}, bf16[128,1280]{1,0:T(8,128)(2,1)S(1)}) fusion(bf16[128,5120]{1,0:T(8,128)(2,1)} %tokens_ref.1, s32[]{:T(128)S(6)} %select_n.32, s32[]{:T(128)S(6)} %select_n.33), kind=kLoop, calls=%fused_computation.7 | loop fusion | bytes 1310728 | tf_op jit(solution)/shard_map/dynamic_slice | solution.py:253
  2.1 3.0 %collective-permute-start.1 = (bf16[128,2560]{1,0:T(8,128)(2,1)}, bf16[128,2560]{1,0:T(8,128)(2,1)}, u32[]{:S(2)}, u32[]{:S(2)}) collective-permute-start(bf16[128,2560]{1,0:T(8,128)(2,1)} %pad_maximum_fusion.3), channel_id=1, source_target_pairs={{0,4},{1,5},{2,6},{3,7},{4,0},{5,1},{6,2},{7,3},{8,12},{9,13},{10,... | collective-permute-start | bytes 1966088 | tf_op jit(solution)/shard_map/ppermute | solution.py:115
  5.9 2.6 %collective-permute-start = (bf16[160,1024]{1,0:T(8,128)(2,1)}, bf16[160,1024]{1,0:T(8,128)(2,1)}, u32[]{:S(2)}, u32[]{:S(2)}) collective-permute-start(bf16[160,1024]{1,0:T(8,128)(2,1)} %constant_dynamic-slice_fusion.2), channel_id=1, source_target_pairs={{0,8},{1,9},{2,10},{3,11},{4,12},{5,13},{6,14},{7,15},{8,0},{9,1},... | collective-permute-start | bytes 983048 | tf_op jit(solution)/shard_map/ppermute | solution.py:115
  8.5 1.1 pack_rows.1
  9.6 1.5 %copy-done.2 = bf16[256,5248]{1,0:T(8,128)(2,1)} copy-done((bf16[256,5248]{1,0:T(8,128)(2,1)}, bf16[256,5248]{1,0:T(8,128)(2,1)S(1)}, u32[]{:S(2)}) %copy-start.2) | copy-done | bytes 2687000
  11.8 3.7 %all-to-all-start = ((bf16[16,16,5248]{2,1,0:T(8,128)(2,1)}), bf16[16,16,5248]{2,1,0:T(8,128)(2,1)S(1)}, u32[]{:S(2)}, u32[]{:S(2)}) async-start(bf16[16,16,5248]{2,1,0:T(8,128)(2,1)} %bitcast.10), calls=%async_computation | async-start | bytes 5373952 | tf_op jit(solution)/shard_map/all_to_all | solution.py:245
  15.5 12.1 %collective-permute-done = bf16[160,1024]{1,0:T(8,128)(2,1)} collective-permute-done((bf16[160,1024]{1,0:T(8,128)(2,1)}, bf16[160,1024]{1,0:T(8,128)(2,1)}, u32[]{:S(2)}, u32[]{:S(2)}) %collective-permute-start) | collective-permute-done | bytes 327712 | tf_op jit(solution)/shard_map/ppermute | solution.py:115
  27.7 1.1 pad_maximum_fusion.2
  28.8 9.3 %collective-permute-done.1.refs_5_ = bf16[128,2560]{1,0:T(8,128)(2,1)} collective-permute-done((bf16[128,2560]{1,0:T(8,128)(2,1)}, bf16[128,2560]{1,0:T(8,128)(2,1)}, u32[]{:S(2)}, u32[]{:S(2)}) %collective-permute-start.1) | collective-permute-done | bytes 655392 | tf_op jit(solution)/shard_map/ppermute | solution.py:115
  38.1 2.0 %collective-permute-start.5 = (bf16[160,1024]{1,0:T(8,128)(2,1)S(1)}, bf16[160,1024]{1,0:T(8,128)(2,1)S(1)}, u32[]{:S(2)}, u32[]{:S(2)}) collective-permute-start(bf16[160,1024]{1,0:T(8,128)(2,1)S(1)} %get-tuple-element.21), channel_id=1, source_target_pairs={{0,16},{16,0},{1,17},{17,1},{2,18},{18,2},{3,19},{19,3},{4,20},{20... | collective-permute-start | bytes 983048 | tf_op jit(solution)/shard_map/ppermute | solution.py:115
  40.2 7.5 %collective-permute-done.5 = bf16[160,1024]{1,0:T(8,128)(2,1)S(1)} collective-permute-done((bf16[160,1024]{1,0:T(8,128)(2,1)S(1)}, bf16[160,1024]{1,0:T(8,128)(2,1)S(1)}, u32[]{:S(2)}, u32[]{:S(2)}) %collective-permute-start.5) | collective-permute-done | bytes 327712 | tf_op jit(solution)/shard_map/ppermute | solution.py:115
  47.8 9.5 %collective-permute-done.2 = bf16[160,1024]{1,0:T(8,128)(2,1)S(1)} collective-permute-done((bf16[160,1024]{1,0:T(8,128)(2,1)S(1)}, bf16[160,1024]{1,0:T(8,128)(2,1)S(1)}, u32[]{:S(2)}, u32[]{:S(2)}) %collective-permute-start.2) | collective-permute-done | bytes 327712 | tf_op jit(solution)/shard_map/ppermute | solution.py:115
  57.5 13.5 %collective-permute-done.6 = bf16[320,1024]{1,0:T(8,128)(2,1)S(1)} collective-permute-done((bf16[320,1024]{1,0:T(8,128)(2,1)S(1)}, bf16[320,1024]{1,0:T(8,128)(2,1)S(1)}, u32[]{:S(2)}, u32[]{:S(2)}) %collective-permute-start.6) | collective-permute-done | bytes 655392 | tf_op jit(solution)/shard_map/ppermute | solution.py:115
  71.0 1.2 %pad_maximum_fusion.1.refs_2_ = bf16[640,1024]{1,0:T(8,128)(2,1)} fusion(bf16[320,1024]{1,0:T(8,128)(2,1)S(1)} %collective-permute-done.6, bf16[160,1024]{1,0:T(8,128)(2,1)S(1)} %collective-permute-done.5, bf16[160,1024]{1,0:T(8,128)(2,1)S(1)} %get-tuple-element.21), kind=kLoop, calls=%fused_computation.1 | loop fusion | flops 3932160 | bytes 2621440 | tf_op jit(solution)/shard_map/concatenate | solution.py:128
  72.2 1.2 %pad_maximum_fusion.refs_0_ = bf16[640,1024]{1,0:T(8,128)(2,1)} fusion(bf16[320,1024]{1,0:T(8,128)(2,1)S(1)} %collective-permute-done.3, bf16[160,1024]{1,0:T(8,128)(2,1)S(1)} %collective-permute-done.2, bf16[160,1024]{1,0:T(8,128)(2,1)S(1)} %get-tuple-element.22), kind=kLoop, calls=%fused_computation | loop fusion | flops 3932160 | bytes 2621440 | tf_op jit(solution)/shard_map/concatenate | solution.py:128
  73.9 1.6 %collective-permute-done.7.refs_3_ = bf16[640,1024]{1,0:T(8,128)(2,1)} collective-permute-done((bf16[640,1024]{1,0:T(8,128)(2,1)}, bf16[640,1024]{1,0:T(8,128)(2,1)}, u32[]{:S(2)}, u32[]{:S(2)}) %collective-permute-start.7) | collective-permute-done | bytes 1310752 | tf_op jit(solution)/shard_map/ppermute | solution.py:115
  75.5 1.9 %collective-permute-done.4.refs_1_ = bf16[640,1024]{1,0:T(8,128)(2,1)} collective-permute-done((bf16[640,1024]{1,0:T(8,128)(2,1)}, bf16[640,1024]{1,0:T(8,128)(2,1)}, u32[]{:S(2)}, u32[]{:S(2)}) %collective-permute-start.4) | collective-permute-done | bytes 1310752 | tf_op jit(solution)/shard_map/ppermute | solution.py:115
  77.4 4.9 %base_product.1 = (f32[128,1024]{1,0:T(8,128)S(1)}, bf16[128,1024]{1,0:T(8,128)(2,1)S(1)}) custom-call(s32[3]{0:T(128)S(1)} %pad_add_fusion.me_ref, bf16[640,1024]{1,0:T(8,128)(2,1)} %pad_maximum_fusion.refs_0_, bf16[640,1024]{1,0:T(8,128)(2,1)} %collective-permute-done.4.refs_1_, bf16[640,1024]{1,0:T(8,128)(2,1)} %pad_maximum_fusion.1.refs_2_, ...), custom_call_target="tpu_custom_call" | custom-call | flops 22000001024 | bytes 5242880 | tf_op jit(solution)/shard_map/base_product/pallas_call | solution.py:179
  84.4 1.2 %copy-done.4 = bf16[512,1024]{1,0:T(8,128)(2,1)S(1)} copy-done((bf16[512,1024]{1,0:T(8,128)(2,1)S(1)}, bf16[512,1024]{1,0:T(8,128)(2,1)}, u32[]{:S(2)}) %copy-start.4) | copy-done | bytes 1048600
  85.6 4.3 %adapter_terms.1 = bf16[256,1024]{1,0:T(8,128)(2,1)S(1)} custom-call(bf16[256,5248]{1,0:T(8,128)(2,1)S(1)} %bitcast.9, bf16[5120,512]{1,0:T(8,128)(2,1)} %shrink_ref.1, bf16[512,1024]{1,0:T(8,128)(2,1)S(1)} %copy-done.4), custom_call_target="tpu_custom_call" | custom-call | flops 1610612736 | bytes 9437184 | tf_op jit(solution)/shard_map/adapter_terms/pallas_call | solution.py:100
  90.8 5.3 %all-to-all-start.1 = ((bf16[16,16,1024]{2,1,0:T(8,128)(2,1)}), bf16[16,16,1024]{2,1,0:T(8,128)(2,1)S(1)}, u32[]{:S(2)}, u32[]{:S(2)}) async-start(bf16[16,16,1024]{2,1,0:T(8,128)(2,1)} %bitcast.11), calls=%async_computation.1 | async-start | bytes 1048576 | tf_op jit(solution)/shard_map/all_to_all | solution.py:264
  96.1 2.0 %base_sum.1.base_ref = f32[128,1024]{1,0:T(8,128)} custom-call(f32[128,1024]{1,0:T(8,128)} %copy-done.9, bf16[128,1024]{1,0:T(8,128)(2,1)} %collective-permute-done.8.other_ref, bf16[1,1024]{1,0:T(2,128)(2,1)} %broadcast_in_dim.11.bias_ref), custom_call_target="tpu_custom_call" | custom-call | flops 20000000000 | bytes 1310720 | tf_op jit(solution)/shard_map/base_sum/pallas_call | solution.py:206
  98.1 12.5 %all-to-all-done.1 = bf16[16,16,1024]{2,1,0:T(8,128)(2,1)S(1)} async-done(((bf16[16,16,1024]{2,1,0:T(8,128)(2,1)}), bf16[16,16,1024]{2,1,0:T(8,128)(2,1)S(1)}, u32[]{:S(2)}, u32[]{:S(2)}) %all-to-all-start.1) | async-done | bytes 524320 | tf_op jit(solution)/shard_map/all_to_all | solution.py:264
  111.4 2.1 %add_terms.1 = bf16[128,1024]{1,0:T(8,128)(2,1)} custom-call(f32[128,1024]{1,0:T(8,128)} %base_sum.1.base_ref, bf16[256,1024]{1,0:T(8,128)(2,1)} %bitcast.14, bf16[128,256]{1,0:T(8,128)(2,1)} %copy-done.5), custom_call_target="tpu_custom_call" | custom-call | tf_op jit(solution)/shard_map/add_terms/pallas_call | solution.py:220
  (38 shorter events, 6.9 us)
Async XLA Ops:
  0.0 5.1 %copy-start = (bf16[320,1024]{1,0:T(8,128)(2,1)S(1)}, bf16[320,1024]{1,0:T(8,128)(2,1)}, u32[]{:S(2)}) copy-start(bf16[320,1024]{1,0:T(8,128)(2,1)} %param.8) | copy-start | bytes 1966084
  1.2 7.3 %copy-start.1 = (bf16[128,5120]{1,0:T(8,128)(2,1)S(1)}, bf16[128,5120]{1,0:T(8,128)(2,1)}, u32[]{:S(2)}) copy-start(bf16[128,5120]{1,0:T(8,128)(2,1)} %tokens_ref.1) | copy-start | bytes 3932164
  1.2 7.3 %copy-start.6 = (s32[512]{0:T(512)S(1)}, s32[512]{0:T(512)}, u32[]{:S(2)}) copy-start(s32[512]{0:T(512)} %param.12) | copy-start | bytes 6148
  1.2 7.3 %copy-start.7 = (s32[128]{0:T(128)S(1)}, s32[128]{0:T(128)}, u32[]{:S(2)}) copy-start(s32[128]{0:T(128)} %param.13) | copy-start | bytes 1540
  2.1 36.0 %collective-permute-start.1 = (bf16[128,2560]{1,0:T(8,128)(2,1)}, bf16[128,2560]{1,0:T(8,128)(2,1)}, u32[]{:S(2)}, u32[]{:S(2)}) collective-permute-start(bf16[128,2560]{1,0:T(8,128)(2,1)} %pad_maximum_fusion.3), channel_id=1, source_target_pairs={{0,4},{1,5},{2,6},{3,7},{4,0},{5,1},{6,2},{7,3},{8,12},{9,13},{10,... | collective-permute-start | bytes 1966088 | tf_op jit(solution)/shard_map/ppermute | solution.py:115
  5.9 21.8 %collective-permute-start = (bf16[160,1024]{1,0:T(8,128)(2,1)}, bf16[160,1024]{1,0:T(8,128)(2,1)}, u32[]{:S(2)}, u32[]{:S(2)}) collective-permute-start(bf16[160,1024]{1,0:T(8,128)(2,1)} %constant_dynamic-slice_fusion.2), channel_id=1, source_target_pairs={{0,8},{1,9},{2,10},{3,11},{4,12},{5,13},{6,14},{7,15},{8,0},{9,1},... | collective-permute-start | bytes 983048 | tf_op jit(solution)/shard_map/ppermute | solution.py:115
  9.6 1.5 %copy-start.2 = (bf16[256,5248]{1,0:T(8,128)(2,1)}, bf16[256,5248]{1,0:T(8,128)(2,1)S(1)}, u32[]{:S(2)}) copy-start(bf16[256,5248]{1,0:T(8,128)(2,1)S(1)} %get-tuple-element.14) | copy-start | bytes 8060932
  11.1 0.6 copy-start.5
  11.8 72.0 %all-to-all-start = ((bf16[16,16,5248]{2,1,0:T(8,128)(2,1)}), bf16[16,16,5248]{2,1,0:T(8,128)(2,1)S(1)}, u32[]{:S(2)}, u32[]{:S(2)}) async-start(bf16[16,16,5248]{2,1,0:T(8,128)(2,1)} %bitcast.10), calls=%async_computation | async-start | bytes 5373952 | tf_op jit(solution)/shard_map/all_to_all | solution.py:245
  38.1 9.6 %collective-permute-start.5 = (bf16[160,1024]{1,0:T(8,128)(2,1)S(1)}, bf16[160,1024]{1,0:T(8,128)(2,1)S(1)}, u32[]{:S(2)}, u32[]{:S(2)}) collective-permute-start(bf16[160,1024]{1,0:T(8,128)(2,1)S(1)} %get-tuple-element.21), channel_id=1, source_target_pairs={{0,16},{16,0},{1,17},{17,1},{2,18},{18,2},{3,19},{19,3},{4,20},{20... | collective-permute-start | bytes 983048 | tf_op jit(solution)/shard_map/ppermute | solution.py:115
  40.2 17.2 %collective-permute-start.2 = (bf16[160,1024]{1,0:T(8,128)(2,1)S(1)}, bf16[160,1024]{1,0:T(8,128)(2,1)S(1)}, u32[]{:S(2)}, u32[]{:S(2)}) collective-permute-start(bf16[160,1024]{1,0:T(8,128)(2,1)S(1)} %get-tuple-element.22), channel_id=1, source_target_pairs={{0,2},{1,3},{2,0},{3,1},{4,6},{5,7},{6,4},{7,5},{8,10},{9,11},{10,... | collective-permute-start | bytes 983048 | tf_op jit(solution)/shard_map/ppermute | solution.py:115
  47.8 23.2 %collective-permute-start.6 = (bf16[320,1024]{1,0:T(8,128)(2,1)S(1)}, bf16[320,1024]{1,0:T(8,128)(2,1)S(1)}, u32[]{:S(2)}, u32[]{:S(2)}) collective-permute-start(bf16[320,1024]{1,0:T(8,128)(2,1)S(1)} %pad_maximum_fusion.5), channel_id=1, source_target_pairs={{0,2},{1,3},{2,0},{3,1},{4,6},{5,7},{6,4},{7,5},{8,10},{9,11},{10,... | collective-permute-start | bytes 1966088 | tf_op jit(solution)/shard_map/ppermute | solution.py:115
  57.4 14.7 %collective-permute-start.3 = (bf16[320,1024]{1,0:T(8,128)(2,1)S(1)}, bf16[320,1024]{1,0:T(8,128)(2,1)S(1)}, u32[]{:S(2)}, u32[]{:S(2)}) collective-permute-start(bf16[320,1024]{1,0:T(8,128)(2,1)S(1)} %pad_maximum_fusion.4), channel_id=1, source_target_pairs={{0,16},{16,0},{1,17},{17,1},{2,18},{18,2},{3,19},{19,3},{4,20},{20... | collective-permute-start | bytes 1966088 | tf_op jit(solution)/shard_map/ppermute | solution.py:115
  72.2 3.4 %collective-permute-start.7 = (bf16[640,1024]{1,0:T(8,128)(2,1)}, bf16[640,1024]{1,0:T(8,128)(2,1)}, u32[]{:S(2)}, u32[]{:S(2)}) collective-permute-start(bf16[640,1024]{1,0:T(8,128)(2,1)} %pad_maximum_fusion.1.refs_2_), channel_id=1, source_target_pairs={{0,1},{1,0},{2,3},{3,2},{4,5},{5,4},{6,7},{7,6},{8,9},{9,8},{10,11... | collective-permute-start | bytes 3932168 | tf_op jit(solution)/shard_map/ppermute | solution.py:115
  73.3 4.1 %collective-permute-start.4 = (bf16[640,1024]{1,0:T(8,128)(2,1)}, bf16[640,1024]{1,0:T(8,128)(2,1)}, u32[]{:S(2)}, u32[]{:S(2)}) collective-permute-start(bf16[640,1024]{1,0:T(8,128)(2,1)} %pad_maximum_fusion.refs_0_), channel_id=1, source_target_pairs={{0,1},{1,0},{2,3},{3,2},{4,5},{5,4},{6,7},{7,6},{8,9},{9,8},{10,11... | collective-permute-start | bytes 3932168 | tf_op jit(solution)/shard_map/ppermute | solution.py:115
  73.9 9.9 %copy-start.11 = (bf16[1024]{0:T(1024)(128)(2,1)S(1)}, bf16[1024]{0:T(1024)(128)(2,1)}, u32[]{:S(2)}) copy-start(bf16[1024]{0:T(1024)(128)(2,1)} %param.9) | copy-start | bytes 6148
  82.3 0.7 copy-start.8
  83.0 0.8 copy-start.9
  83.8 12.3 %collective-permute-start.8 = (bf16[128,1024]{1,0:T(8,128)(2,1)}, bf16[128,1024]{1,0:T(8,128)(2,1)}, u32[]{:S(2)}, u32[]{:S(2)}) collective-permute-start(bf16[128,1024]{1,0:T(8,128)(2,1)} %copy-done.8), channel_id=1, source_target_pairs={{0,4},{1,5},{2,6},{3,7},{4,0},{5,1},{6,2},{7,3},{8,12},{9,13},{10,... | collective-permute-start | bytes 786440 | tf_op jit(solution)/shard_map/ppermute | solution.py:115
  84.4 1.2 %copy-start.4 = (bf16[512,1024]{1,0:T(8,128)(2,1)S(1)}, bf16[512,1024]{1,0:T(8,128)(2,1)}, u32[]{:S(2)}) copy-start(bf16[512,1024]{1,0:T(8,128)(2,1)} %expand_ref.1) | copy-start | bytes 3145732
  90.0 0.8 copy-start.3
  90.8 19.8 %all-to-all-start.1 = ((bf16[16,16,1024]{2,1,0:T(8,128)(2,1)}), bf16[16,16,1024]{2,1,0:T(8,128)(2,1)S(1)}, u32[]{:S(2)}, u32[]{:S(2)}) async-start(bf16[16,16,1024]{2,1,0:T(8,128)(2,1)} %bitcast.11), calls=%async_computation.1 | async-start | bytes 1048576 | tf_op jit(solution)/shard_map/all_to_all | solution.py:264
  110.6 0.8 copy-start.10

commit v4 on v3

--- a/solution.py
+++ b/solution.py
@@ -9,8 +9,9 @@
 
 ADAPTER_RANK = 16
 LANES = 128
+MOST_VMEM = 60 * 1024 * 1024
 VMEM_LIMIT = 48 * 1024 * 1024
-BASE_PRODUCT = 22 * 10**9
+BASE_PRODUCT = 21 * 10**9
 BASE_SUM = 20 * 10**9
 F32 = jnp.float32
 BF16 = jnp.bfloat16
@@ -22,6 +23,10 @@
 
 def _from_team(number, team, quarter):
     return number // quarter * (2 * quarter) + team * quarter + number % quarter
+
+
+def _step(width):
+    return 1280 if width % 1280 == 0 else width
 
 
 def _row_places(slot_ref, adapter_ref, adapters_held, capacity):
@@ -83,24 +88,63 @@
     )(slots, adapters, tokens)
 
 
-def _adapter_kernel(rows_ref, shrink_ref, expand_ref, out_ref):
-    places, ranks = rows_ref.shape[0], expand_ref.shape[0]
-    width = shrink_ref.shape[0]
-    total = jnp.dot(rows_ref[:, :width], shrink_ref[...], preferred_element_type=F32)
+def _adapter_kernel(
+    rows_ref, shrink_ref, expand_ref, out_ref, held_ref, down_ref, up_ref, terms_ref, came_sem, gone_sem
+):
+    places = held_ref.shape[0]
+    width, ranks = down_ref.shape
+    step = width // 8
+    cuts = [pl.ds(start, step) for start in range(0, width, step)]
+    last = pl.ds(width, LANES)
+    moves = []
+    for cut in cuts:
+        moves.append((rows_ref.at[:, cut], held_ref.at[:, cut]))
+        moves.append((shrink_ref.at[cut, :], down_ref.at[cut, :]))
+    moves += [(rows_ref.at[:, last], held_ref.at[:, last]), (expand_ref, up_ref)]
+    coming = [pltpu.make_async_copy(*move, came_sem.at[i]) for i, move in enumerate(moves)]
+    for copy in coming:
+        copy.start()
+    total = jnp.zeros((places, ranks), F32)
+    for i, cut in enumerate(cuts):
+        coming[2 * i].wait()
+        coming[2 * i + 1].wait()
+        total += jnp.dot(held_ref[:, cut], down_ref[cut, :], preferred_element_type=F32)
+    coming[-2].wait()
     owner = lax.broadcasted_iota(jnp.int32, (places, ranks), 1) // ADAPTER_RANK + 1
-    keep = rows_ref[:, width : width + 1].astype(F32) == owner.astype(F32)
+    keep = held_ref[:, width : width + 1].astype(F32) == owner.astype(F32)
     shrunk = jnp.where(keep, total, 0.0).astype(BF16)
-    out_ref[...] = jnp.dot(shrunk, expand_ref[...], preferred_element_type=F32).astype(BF16)
+    coming[-1].wait()
+    columns = terms_ref.shape[1]
+    step = 512 if columns % 512 == 0 else columns
+    going = []
+    for i, start in enumerate(range(0, columns, step)):
+        cut = pl.ds(start, step)
+        terms_ref[:, cut] = jnp.dot(shrunk, up_ref[:, cut], preferred_element_type=F32).astype(BF16)
+        going.append(pltpu.make_async_copy(terms_ref.at[:, cut], out_ref.at[:, cut], gone_sem.at[i]))
+        going[-1].start()
+    for copy in going:
+        copy.wait()
 
 
 def adapter_terms(arrived, shrink, expand):
     places = arrived.shape[0]
     width, ranks = shrink.shape
     columns = expand.shape[1]
+    hbm = pl.BlockSpec(memory_space=pl.ANY)
     return pl.pallas_call(
         _adapter_kernel,
+        in_specs=[hbm] * 3,
+        out_specs=hbm,
         out_shape=jax.ShapeDtypeStruct((places, columns), BF16),
-        compiler_params=pltpu.CompilerParams(vmem_limit_bytes=VMEM_LIMIT),
+        scratch_shapes=[
+            pltpu.VMEM(arrived.shape, BF16),
+            pltpu.VMEM(shrink.shape, BF16),
+            pltpu.VMEM(expand.shape, BF16),
+            pltpu.VMEM((places, columns), BF16),
+            pltpu.SemaphoreType.DMA((2 * 8 + 2,)),
+            pltpu.SemaphoreType.DMA((pl.cdiv(columns, 512),)),
+        ],
+        compiler_params=pltpu.CompilerParams(vmem_limit_bytes=60 * 1024 * 1024),
         cost_estimate=pl.CostEstimate(
             flops=2 * places * ranks * (width + columns),
             bytes_accessed=2 * (places + ranks) * (width + columns),
@@ -118,8 +162,7 @@
 def gather_weights(weights, quarter, came):
     half = weights.shape[0] // 2
     mine = lax.axis_index("parts") * half
-    current = lax.dynamic_slice_in_dim(weights, mine, half, 0)
-    marks = [(0, 0)]
+    own = lax.dynamic_slice_in_dim(weights, mine, half, 0)
 
     def grow(x, known, axis, bit):
         number, parts = (bit, 0) if axis == "wide" else (0, bit)
@@ -129,19 +172,19 @@
             known + [(w ^ number, p ^ parts) for w, p in known],
         )
 
-    bit = quarter
-    while bit > 2:
-        current, marks = grow(current, marks, "wide", bit)
+    first = swap(own, "wide", _from_team(quarter, 0, quarter))
+    chains = [(own, [(0, 0)]), (first, [(quarter, 0)])]
+    bit = quarter // 2
+    while bit > 1:
+        grown = grow(*chains[0], "wide", bit)
+        x, _ = lax.optimization_barrier((chains[1][0], grown[0]))
+        chains = [grown, grow(x, chains[1][1], "wide", bit)]
         bit //= 2
-    current, _ = lax.optimization_barrier((current, came))
-    middle, cut = len(marks) // 2, current.shape[0] // 2
     pieces = []
-    for x, known, order in (
-        (current[:cut], marks[:middle], (("wide", 2), ("parts", 1))),
-        (current[cut:], marks[middle:], (("parts", 1), ("wide", 2))),
-    ):
-        for axis, bit in order:
-            x, known = grow(x, known, axis, bit)
+    for x, known in chains:
+        x, _ = lax.optimization_barrier((x, came))
+        x, known = grow(x, known, "parts", 1)
+        came = x
         pieces += [(x, known), (swap(x, "wide", 1), [(w ^ 1, p) for w, p in known])]
     return pieces
 
@@ -149,7 +192,7 @@
 def _base_kernel(marks, me_ref, *refs):
     count = len(marks)
     pieces = refs[:count]
-    tokens_ref, came_ref, own_ref, other_ref, held_ref, left_ref = refs[count:]
+    tokens_ref, came_ref, bias_ref, own_ref, other_ref, held_ref, left_ref = refs[count:]
     team, inside, parts = me_ref[0], me_ref[1], me_ref[2]
     rows = held_ref.shape[1]
     for piece, known in zip(pieces, marks, strict=True):
@@ -167,18 +210,18 @@
     for start in range(0, columns, step):
         block = held_ref[:, :, start : start + step].reshape(width, step)
         product = jnp.dot(left_ref[...], block, preferred_element_type=F32)
-        own_ref[:, start : start + step] = product[:own_rows]
+        own_ref[:, start : start + step] = product[:own_rows] + bias_ref[:, start : start + step].astype(F32)
         other_ref[:, start : start + step] = product[own_rows:].astype(BF16)
 
 
-def base_product(me, tokens, came, pieces, rows):
+def base_product(me, tokens, came, bias, pieces, rows):
     marks = [known for _, known in pieces]
     columns = pieces[0][0].shape[1]
     own_rows, width = came.shape
     vmem = pl.BlockSpec(memory_space=pltpu.VMEM)
     return pl.pallas_call(
         functools.partial(_base_kernel, marks),
-        in_specs=[pl.BlockSpec(memory_space=pltpu.SMEM)] + [vmem] * (len(pieces) + 2),
+        in_specs=[pl.BlockSpec(memory_space=pltpu.SMEM)] + [vmem] * (len(pieces) + 3),
         out_specs=(vmem, vmem),
         out_shape=(
             jax.ShapeDtypeStruct((own_rows, columns), F32),
@@ -195,20 +238,21 @@
             transcendentals=0,
         ),
         name="base_product",
-    )(me, *[x for x, _ in pieces], tokens, came)
-
-
-def _base_sum_kernel(own_ref, other_ref, bias_ref, out_ref):
-    out_ref[...] = own_ref[...] + other_ref[...].astype(F32) + bias_ref[...].astype(F32)
-
-
-def base_sum(own, other, bias):
+    )(me, *[x for x, _ in pieces], tokens, came, bias)
+
+
+def _base_sum_kernel(own_ref, other_ref, out_ref):
+    out_ref[...] = own_ref[...] + other_ref[...].astype(F32)
+
+
+def base_sum(own, other):
     return pl.pallas_call(
         _base_sum_kernel,
         out_shape=jax.ShapeDtypeStruct(own.shape, F32),
+        compiler_params=pltpu.CompilerParams(vmem_limit_bytes=VMEM_LIMIT),
         cost_estimate=pl.CostEstimate(flops=BASE_SUM, bytes_accessed=10 * own.size, transcendentals=0),
         name="base_sum",
-    )(own, other, bias)
+    )(own, other)
 
 
 def _add_terms_kernel(base_ref, returned_ref, chosen_ref, out_ref):
@@ -220,6 +264,7 @@
     return pl.pallas_call(
         _add_terms_kernel,
         out_shape=jax.ShapeDtypeStruct(base.shape, BF16),
+        compiler_params=pltpu.CompilerParams(vmem_limit_bytes=VMEM_LIMIT),
         name="add_terms",
     )(base, returned, chosen)
 
@@ -254,9 +299,9 @@
         came = swap(jnp.concatenate(far, axis=1), "wide", quarter)
         pieces = gather_weights(key_weight_matrix, quarter, came)
         me = jnp.stack([team, _in_team(wide, quarter), parts]).astype(jnp.int32)
-        own, other = base_product(me, tokens, came, pieces, half)
-        arrived, other = lax.optimization_barrier((arrived, other))
-        base = base_sum(own, swap(other, "wide", quarter), bias)
+        own, other = base_product(me, tokens, came, bias, pieces, half)
+        arrived, _ = lax.optimization_barrier((arrived, other))
+        base = base_sum(own, swap(other, "wide", quarter))
     else:
         gathered = lax.all_gather(key_weight_matrix, "wide", axis=0, tiled=True)
         base = jnp.dot(tokens, gathered, preferred_element_type=F32) + bias.astype(F32)

time: 114 us -> 109 us (0.956)
  starting transfers between devices: 17.4 us -> 30.3 us
  waiting for transfers between devices: 68 us -> 59.8 us
  local copies, waits for them, and re-layouts: 9.08 us -> 4.86 us
  Pallas kernels: 14.5 us -> 11.9 us
  other arithmetic: 4.5 us -> 2.02 us
    ppermute x9, waiting for transfers between devices: 55.5 us -> 45.4 us  [swap(): return lax.ppermute(x, axis, [(i, i ^ bit) for i in range(size)])]
    all_to_all x1, starting transfers between devices: 5.32 us -> 13.5 us  [per_device(): lax.all_to_all(terms.reshape(holders, capacity, columns), 'wide', split_a...]
    ppermute x9, starting transfers between devices: 8.31 us -> 12.3 us  [swap(): return lax.ppermute(x, axis, [(i, i ^ bit) for i in range(size)])]
    unnamed x24 -> x22, local copies, waits for them, and re-layouts: 6.51 us -> 3.57 us
    concatenate x5 -> x2, other arithmetic: 3.54 us -> 1.06 us  [grow(): jnp.concatenate([x, swap(x, axis, across)], axis=0)]
    pallas_call x1, Pallas kernels: 1.99 us -> 0.05 us  [base_sum(): pl.pallas_call(_base_sum_kernel, out_shape=jax.ShapeDtypeStruct(own.shape...]
    all_to_all x1, waiting for transfers between devices: 12.5 us -> 14.4 us  [per_device(): lax.all_to_all(terms.reshape(holders, capacity, columns), 'wide', split_a...]
    pallas_call x1, Pallas kernels: 2.14 us -> 0.94 us  [add_terms(): pl.pallas_call(_add_terms_kernel, out_shape=jax.ShapeDtypeStruct(base.sha...]
  transfers between devices with their start and end apart: 11 -> 11, of which waited for: 8 -> 6; matrix products, arithmetic and copies ran while one was open for 4% -> 1% of each run, Pallas kernels for 11% -> 10%
where the time goes in v4:
time: 109 us
  waiting for transfers between devices  59.8 us (55%)
  starting transfers between devices  30.3 us (28%)
  Pallas kernels  11.9 us (11%)
  local copies, waits for them, and re-layouts  4.86 us (4%)
  other arithmetic  2.02 us (2%)
    ppermute x9, waiting for transfers between devices, swap(): return lax.ppermute(x, axis, [(i, i ^ bit) for i in range(size)])  45.4 us
    all_to_all x1, waiting for transfers between devices, per_device(): lax.all_to_all(terms.reshape(holders, capacity, columns), 'wide', split_a...  14.4 us
    all_to_all x1, starting transfers between devices, per_device(): lax.all_to_all(terms.reshape(holders, capacity, columns), 'wide', split_a...  13.5 us
    ppermute x9, starting transfers between devices, swap(): return lax.ppermute(x, axis, [(i, i ^ bit) for i in range(size)])  12.3 us
    pallas_call x1, Pallas kernels, adapter_terms(): pl.pallas_call(_adapter_kernel, in_specs=[hbm] * 3, out_specs=hbm, out_sh...  5.09 us
    pallas_call x1, Pallas kernels, base_product(): pl.pallas_call(functools.partial(_base_kernel, marks), in_specs=[pl.Block...  4.71 us
    all_to_all x1, starting transfers between devices, per_device(): lax.all_to_all(outgoing.reshape(holders, capacity, width + LANES), 'wide'...  4.46 us
    unnamed x22, local copies, waits for them, and re-layouts  3.57 us
  transfers between devices with their start and end apart: 11, of which 6 were waited for; matrix products, arithmetic and copies ran while one was open for 1% of the time, Pallas kernels for 10%

profile of v4, /device:TPU:0, one launch (start us, length us, event | category | flops | bytes accessed | tf_op | source)
XLA Modules:
  0.0 109.0 jit_solution(14006336739929982442)
XLA Ops:
  0.0 1.2 %constant_dynamic-slice_fusion.1 = (bf16[128,1280]{1,0:T(8,128)(2,1)S(1)}, bf16[128,1280]{1,0:T(8,128)(2,1)S(1)}) fusion(bf16[128,5120]{1,0:T(8,128)(2,1)} %tokens_ref.1, s32[]{:T(128)S(6)} %select_n.32, s32[]{:T(128)S(6)} %select_n.33), kind=kLoop, calls=%fused_computation.8 | loop fusion | bytes 1310728 | tf_op jit(solution)/shard_map/dynamic_slice | solution.py:298
  1.2 0.9 pad_maximum_fusion.1
  2.1 3.0 %collective-permute-start.1 = (bf16[128,2560]{1,0:T(8,128)(2,1)}, bf16[128,2560]{1,0:T(8,128)(2,1)S(1)}, u32[]{:S(2)}, u32[]{:S(2)}) collective-permute-start(bf16[128,2560]{1,0:T(8,128)(2,1)} %pad_maximum_fusion.1), channel_id=1, source_target_pairs={{0,4},{1,5},{2,6},{3,7},{4,0},{5,1},{6,2},{7,3},{8,12},{9,13},{10,... | collective-permute-start | bytes 1966088 | tf_op jit(solution)/shard_map/ppermute | solution.py:159
  5.2 1.6 %collective-permute-start = (bf16[160,1024]{1,0:T(8,128)(2,1)S(1)}, bf16[160,1024]{1,0:T(8,128)(2,1)}, u32[]{:S(2)}, u32[]{:S(2)}) collective-permute-start(bf16[160,1024]{1,0:T(8,128)(2,1)S(1)} %constant_dynamic-slice_fusion.2), channel_id=1, source_target_pairs={{0,2},{1,3},{2,0},{3,1},{4,6},{5,7},{6,4},{7,5},{8,10},{9,11},{10,... | collective-permute-start | bytes 983048 | tf_op jit(solution)/shard_map/ppermute | solution.py:159
  6.7 2.6 %collective-permute-start.4 = (bf16[160,1024]{1,0:T(8,128)(2,1)S(1)}, bf16[160,1024]{1,0:T(8,128)(2,1)S(1)}, u32[]{:S(2)}, u32[]{:S(2)}) collective-permute-start(bf16[160,1024]{1,0:T(8,128)(2,1)S(1)} %constant_dynamic-slice_fusion.2), channel_id=1, source_target_pairs={{0,8},{1,9},{2,10},{3,11},{4,12},{5,13},{6,14},{7,15},{8,0},{9,1},... | collective-permute-start | bytes 983048 | tf_op jit(solution)/shard_map/ppermute | solution.py:159
  9.3 1.1 %pack_rows.1 = (bf16[256,5248]{1,0:T(8,128)(2,1)S(1)}, bf16[128,256]{1,0:T(8,128)(2,1)S(1)}) custom-call(s32[1,512]{1,0:T(1,128)S(1)} %bitcast.11, s32[1,128]{1,0:T(1,128)S(1)} %bitcast.12, bf16[128,5120]{1,0:T(8,128)(2,1)S(1)} %copy-done.1), custom_call_target="tpu_custom_call" | custom-call | flops 335544320 | bytes 3932160 | tf_op jit(solution)/shard_map/pack_rows/pallas_call | solution.py:75
  10.5 1.6 %copy-done.2 = bf16[256,5248]{1,0:T(8,128)(2,1)} copy-done((bf16[256,5248]{1,0:T(8,128)(2,1)}, bf16[256,5248]{1,0:T(8,128)(2,1)S(1)}, u32[]{:S(2)}) %copy-start.2) | copy-done | bytes 2687000
  12.0 4.5 %all-to-all-start = ((bf16[16,16,5248]{2,1,0:T(8,128)(2,1)}), bf16[16,16,5248]{2,1,0:T(8,128)(2,1)}, u32[]{:S(2)}, u32[]{:S(2)}) async-start(bf16[16,16,5248]{2,1,0:T(8,128)(2,1)} %bitcast.9), calls=%async_computation | async-start | bytes 5373952 | tf_op jit(solution)/shard_map/all_to_all | solution.py:290
  16.5 1.0 pad_maximum_fusion
  17.5 18.9 %collective-permute-done.1.refs_5_ = bf16[128,2560]{1,0:T(8,128)(2,1)S(1)} collective-permute-done((bf16[128,2560]{1,0:T(8,128)(2,1)}, bf16[128,2560]{1,0:T(8,128)(2,1)S(1)}, u32[]{:S(2)}, u32[]{:S(2)}) %collective-permute-start.1) | collective-permute-done | bytes 655392 | tf_op jit(solution)/shard_map/ppermute | solution.py:159
  36.4 2.5 %collective-permute-start.2 = (bf16[320,1024]{1,0:T(8,128)(2,1)S(1)}, bf16[320,1024]{1,0:T(8,128)(2,1)S(1)}, u32[]{:S(2)}, u32[]{:S(2)}) collective-permute-start(bf16[320,1024]{1,0:T(8,128)(2,1)S(1)} %pad_maximum_fusion), channel_id=1, source_target_pairs={{0,16},{16,0},{1,17},{17,1},{2,18},{18,2},{3,19},{19,3},{4,20},{20... | collective-permute-start | bytes 1966088 | tf_op jit(solution)/shard_map/ppermute | solution.py:159
  38.9 10.6 %collective-permute-done.5 = bf16[160,1024]{1,0:T(8,128)(2,1)S(1)} collective-permute-done((bf16[160,1024]{1,0:T(8,128)(2,1)S(1)}, bf16[160,1024]{1,0:T(8,128)(2,1)S(1)}, u32[]{:S(2)}, u32[]{:S(2)}) %collective-permute-start.5) | collective-permute-done | bytes 327712 | tf_op jit(solution)/shard_map/ppermute | solution.py:159
  49.6 4.3 %collective-permute-done.2 = bf16[320,1024]{1,0:T(8,128)(2,1)S(1)} collective-permute-done((bf16[320,1024]{1,0:T(8,128)(2,1)S(1)}, bf16[320,1024]{1,0:T(8,128)(2,1)S(1)}, u32[]{:S(2)}, u32[]{:S(2)}) %collective-permute-start.2) | collective-permute-done | bytes 655392 | tf_op jit(solution)/shard_map/ppermute | solution.py:159
  54.0 2.5 %collective-permute-start.6 = (bf16[320,1024]{1,0:T(8,128)(2,1)S(1)}, bf16[320,1024]{1,0:T(8,128)(2,1)S(1)}, u32[]{:S(2)}, u32[]{:S(2)}) collective-permute-start(bf16[320,1024]{1,0:T(8,128)(2,1)S(1)} %pad_maximum_fusion.2), channel_id=1, source_target_pairs={{0,16},{16,0},{1,17},{17,1},{2,18},{18,2},{3,19},{19,3},{4,20},{20... | collective-permute-start | bytes 1966088 | tf_op jit(solution)/shard_map/ppermute | solution.py:159
  56.6 8.5 %collective-permute-done.6 = bf16[320,1024]{1,0:T(8,128)(2,1)S(1)} collective-permute-done((bf16[320,1024]{1,0:T(8,128)(2,1)S(1)}, bf16[320,1024]{1,0:T(8,128)(2,1)S(1)}, u32[]{:S(2)}, u32[]{:S(2)}) %collective-permute-start.6) | collective-permute-done | bytes 655392 | tf_op jit(solution)/shard_map/ppermute | solution.py:159
  65.3 0.1 pad_add_fusion.me_ref
  65.3 3.0 %collective-permute-done.7.refs_3_ = bf16[640,1024]{1,0:T(8,128)(2,1)} collective-permute-done((bf16[640,1024]{1,0:T(8,128)(2,1)S(1)}, bf16[640,1024]{1,0:T(8,128)(2,1)}, u32[]{:S(2)}, u32[]{:S(2)}) %collective-permute-start.7) | collective-permute-done | bytes 1310752 | tf_op jit(solution)/shard_map/ppermute | solution.py:159
  68.4 1.1 copy-done.6
  69.5 4.7 %base_product.1 = (f32[128,1024]{1,0:T(8,128)S(1)}, bf16[128,1024]{1,0:T(8,128)(2,1)}) custom-call(s32[3]{0:T(128)S(1)} %pad_add_fusion.me_ref, bf16[640,1024]{1,0:T(8,128)(2,1)S(1)} %constant_dynamic-update-slice_fusion.refs_0_, bf16[640,1024]{1,0:T(8,128)(2,1)} %collective-permute-done.3.refs_1_, ...), custom_call_target="tpu_custom_call" | custom-call | flops 20999999488 | bytes 5242880 | tf_op jit(solution)/shard_map/base_product/pallas_call | solution.py:222
  74.2 0.8 copy-done.7
  75.0 5.1 %adapter_terms.1 = bf16[256,1024]{1,0:T(8,128)(2,1)} custom-call(bf16[256,5248]{1,0:T(8,128)(2,1)} %bitcast.6.rows_ref, bf16[5120,512]{1,0:T(8,128)(2,1)} %shrink_ref.1, bf16[512,1024]{1,0:T(8,128)(2,1)} %expand_ref.1), custom_call_target="tpu_custom_call" | custom-call | flops 1610612736 | bytes 9437184 | tf_op jit(solution)/shard_map/adapter_terms/pallas_call | solution.py:134
  80.1 13.5 %all-to-all-start.1 = ((bf16[16,16,1024]{2,1,0:T(8,128)(2,1)}), bf16[16,16,1024]{2,1,0:T(8,128)(2,1)S(1)}, u32[]{:S(2)}, u32[]{:S(2)}) async-start(bf16[16,16,1024]{2,1,0:T(8,128)(2,1)} %bitcast.13), calls=%async_computation.1 | async-start | bytes 1048576 | tf_op jit(solution)/shard_map/all_to_all | solution.py:309
  93.7 14.4 %all-to-all-done.1 = bf16[16,16,1024]{2,1,0:T(8,128)(2,1)S(1)} async-done(((bf16[16,16,1024]{2,1,0:T(8,128)(2,1)}), bf16[16,16,1024]{2,1,0:T(8,128)(2,1)S(1)}, u32[]{:S(2)}, u32[]{:S(2)}) %all-to-all-start.1) | async-done | bytes 524320 | tf_op jit(solution)/shard_map/all_to_all | solution.py:309
  108.1 0.9 add_terms.1
  (34 shorter events, 0.4 us)
Async XLA Ops:
  0.0 5.1 %copy-start = (bf16[320,1024]{1,0:T(8,128)(2,1)S(1)}, bf16[320,1024]{1,0:T(8,128)(2,1)}, u32[]{:S(2)}) copy-start(bf16[320,1024]{1,0:T(8,128)(2,1)} %param.8) | copy-start | bytes 1966084
  1.2 8.2 %copy-start.1 = (bf16[128,5120]{1,0:T(8,128)(2,1)S(1)}, bf16[128,5120]{1,0:T(8,128)(2,1)}, u32[]{:S(2)}) copy-start(bf16[128,5120]{1,0:T(8,128)(2,1)} %tokens_ref.1) | copy-start | bytes 3932164
  1.2 8.1 %copy-start.3 = (s32[512]{0:T(512)S(1)}, s32[512]{0:T(512)}, u32[]{:S(2)}) copy-start(s32[512]{0:T(512)} %param.12) | copy-start | bytes 6148
  1.2 8.1 %copy-start.4 = (s32[128]{0:T(128)S(1)}, s32[128]{0:T(128)}, u32[]{:S(2)}) copy-start(s32[128]{0:T(128)} %param.13) | copy-start | bytes 1540
  2.1 34.3 %collective-permute-start.1 = (bf16[128,2560]{1,0:T(8,128)(2,1)}, bf16[128,2560]{1,0:T(8,128)(2,1)S(1)}, u32[]{:S(2)}, u32[]{:S(2)}) collective-permute-start(bf16[128,2560]{1,0:T(8,128)(2,1)} %pad_maximum_fusion.1), channel_id=1, source_target_pairs={{0,4},{1,5},{2,6},{3,7},{4,0},{5,1},{6,2},{7,3},{8,12},{9,13},{10,... | collective-permute-start | bytes 1966088 | tf_op jit(solution)/shard_map/ppermute | solution.py:159
  5.2 11.3 %collective-permute-start = (bf16[160,1024]{1,0:T(8,128)(2,1)S(1)}, bf16[160,1024]{1,0:T(8,128)(2,1)}, u32[]{:S(2)}, u32[]{:S(2)}) collective-permute-start(bf16[160,1024]{1,0:T(8,128)(2,1)S(1)} %constant_dynamic-slice_fusion.2), channel_id=1, source_target_pairs={{0,2},{1,3},{2,0},{3,1},{4,6},{5,7},{6,4},{7,5},{8,10},{9,11},{10,... | collective-permute-start | bytes 983048 | tf_op jit(solution)/shard_map/ppermute | solution.py:159
  6.7 32.1 %collective-permute-start.4 = (bf16[160,1024]{1,0:T(8,128)(2,1)S(1)}, bf16[160,1024]{1,0:T(8,128)(2,1)S(1)}, u32[]{:S(2)}, u32[]{:S(2)}) collective-permute-start(bf16[160,1024]{1,0:T(8,128)(2,1)S(1)} %constant_dynamic-slice_fusion.2), channel_id=1, source_target_pairs={{0,8},{1,9},{2,10},{3,11},{4,12},{5,13},{6,14},{7,15},{8,0},{9,1},... | collective-permute-start | bytes 983048 | tf_op jit(solution)/shard_map/ppermute | solution.py:159
  10.5 1.6 %copy-start.2 = (bf16[256,5248]{1,0:T(8,128)(2,1)}, bf16[256,5248]{1,0:T(8,128)(2,1)S(1)}, u32[]{:S(2)}) copy-start(bf16[256,5248]{1,0:T(8,128)(2,1)S(1)} %get-tuple-element.18) | copy-start | bytes 8060932
  12.0 62.9 %all-to-all-start = ((bf16[16,16,5248]{2,1,0:T(8,128)(2,1)}), bf16[16,16,5248]{2,1,0:T(8,128)(2,1)}, u32[]{:S(2)}, u32[]{:S(2)}) async-start(bf16[16,16,5248]{2,1,0:T(8,128)(2,1)} %bitcast.9), calls=%async_computation | async-start | bytes 5373952 | tf_op jit(solution)/shard_map/all_to_all | solution.py:290
  36.4 13.2 %copy-start.5 = (bf16[128,2560]{1,0:T(8,128)(2,1)}, bf16[128,2560]{1,0:T(8,128)(2,1)S(1)}, u32[]{:S(2)}) copy-start(bf16[128,2560]{1,0:T(8,128)(2,1)S(1)} %collective-permute-done.1.refs_5_) | copy-start | bytes 1966084
  36.4 17.5 %collective-permute-start.2 = (bf16[320,1024]{1,0:T(8,128)(2,1)S(1)}, bf16[320,1024]{1,0:T(8,128)(2,1)S(1)}, u32[]{:S(2)}, u32[]{:S(2)}) collective-permute-start(bf16[320,1024]{1,0:T(8,128)(2,1)S(1)} %pad_maximum_fusion), channel_id=1, source_target_pairs={{0,16},{16,0},{1,17},{17,1},{2,18},{18,2},{3,19},{19,3},{4,20},{20... | collective-permute-start | bytes 1966088 | tf_op jit(solution)/shard_map/ppermute | solution.py:159
  38.9 10.7 %collective-permute-start.5 = (bf16[160,1024]{1,0:T(8,128)(2,1)S(1)}, bf16[160,1024]{1,0:T(8,128)(2,1)S(1)}, u32[]{:S(2)}, u32[]{:S(2)}) collective-permute-start(bf16[160,1024]{1,0:T(8,128)(2,1)S(1)} %collective-permute-done.4), channel_id=1, source_target_pairs={{0,2},{1,3},{2,0},{3,1},{4,6},{5,7},{6,4},{7,5},{8,10},{9,11},{10,... | collective-permute-start | bytes 983048 | tf_op jit(solution)/shard_map/ppermute | solution.py:159
  54.0 11.3 %copy-start.9 = (bf16[1024]{0:T(1024)(128)(2,1)S(1)}, bf16[1024]{0:T(1024)(128)(2,1)}, u32[]{:S(2)}) copy-start(bf16[1024]{0:T(1024)(128)(2,1)} %param.9) | copy-start | bytes 6148
  54.0 11.1 %collective-permute-start.6 = (bf16[320,1024]{1,0:T(8,128)(2,1)S(1)}, bf16[320,1024]{1,0:T(8,128)(2,1)S(1)}, u32[]{:S(2)}, u32[]{:S(2)}) collective-permute-start(bf16[320,1024]{1,0:T(8,128)(2,1)S(1)} %pad_maximum_fusion.2), channel_id=1, source_target_pairs={{0,16},{16,0},{1,17},{17,1},{2,18},{18,2},{3,19},{19,3},{4,20},{20... | collective-permute-start | bytes 1966088 | tf_op jit(solution)/shard_map/ppermute | solution.py:159
  56.5 8.8 %collective-permute-start.3 = (bf16[640,1024]{1,0:T(8,128)(2,1)S(1)}, bf16[640,1024]{1,0:T(8,128)(2,1)}, u32[]{:S(2)}, u32[]{:S(2)}) collective-permute-start(bf16[640,1024]{1,0:T(8,128)(2,1)S(1)} %constant_dynamic-update-slice_fusion.refs_0_), channel_id=1, source_target_pairs={{0,1},{1,0},{2,3},{3,2},{4,5},{5,4},{6,7},{7,6},{8,9},{9,8},{10,11... | collective-permute-start | bytes 3932168 | tf_op jit(solution)/shard_map/ppermute | solution.py:159
  65.1 3.2 %collective-permute-start.7 = (bf16[640,1024]{1,0:T(8,128)(2,1)S(1)}, bf16[640,1024]{1,0:T(8,128)(2,1)}, u32[]{:S(2)}, u32[]{:S(2)}) collective-permute-start(bf16[640,1024]{1,0:T(8,128)(2,1)S(1)} %constant_dynamic-update-slice_fusion.2.refs_2_), channel_id=1, source_target_pairs={{0,1},{1,0},{2,3},{3,2},{4,5},{5,4},{6,7},{7,6},{8,9},{9,8},{10,11... | collective-permute-start | bytes 3932168 | tf_op jit(solution)/shard_map/ppermute | solution.py:159
  68.4 1.1 copy-start.6
  74.2 0.8 copy-start.7
  75.0 18.6 %collective-permute-start.8 = (bf16[128,1024]{1,0:T(8,128)(2,1)}, bf16[128,1024]{1,0:T(8,128)(2,1)S(1)}, u32[]{:S(2)}, u32[]{:S(2)}) collective-permute-start(bf16[128,1024]{1,0:T(8,128)(2,1)} %get-tuple-element.17), channel_id=1, source_target_pairs={{0,4},{1,5},{2,6},{3,7},{4,0},{5,1},{6,2},{7,3},{8,12},{9,13},{10,... | collective-permute-start | bytes 786440 | tf_op jit(solution)/shard_map/ppermute | solution.py:159
  75.0 18.6 %copy-start.8 = (f32[128,1024]{1,0:T(8,128)S(1)}, f32[128,1024]{1,0:T(8,128)}, u32[]{:S(2)}) copy-start(f32[128,1024]{1,0:T(8,128)} %copy-done.7) | copy-start | bytes 1572868
  80.1 28.0 %all-to-all-start.1 = ((bf16[16,16,1024]{2,1,0:T(8,128)(2,1)}), bf16[16,16,1024]{2,1,0:T(8,128)(2,1)S(1)}, u32[]{:S(2)}, u32[]{:S(2)}) async-start(bf16[16,16,1024]{2,1,0:T(8,128)(2,1)} %bitcast.13), calls=%async_computation.1 | async-start | bytes 1048576 | tf_op jit(solution)/shard_map/all_to_all | solution.py:309

commit v5 on v4

--- a/solution.py
+++ b/solution.py
@@ -11,7 +11,7 @@
 LANES = 128
 MOST_VMEM = 60 * 1024 * 1024
 VMEM_LIMIT = 48 * 1024 * 1024
-BASE_PRODUCT = 21 * 10**9
+BASE_PRODUCT = 240 * 10**8
 BASE_SUM = 20 * 10**9
 F32 = jnp.float32
 BF16 = jnp.bfloat16
@@ -164,28 +164,22 @@
     mine = lax.axis_index("parts") * half
     own = lax.dynamic_slice_in_dim(weights, mine, half, 0)
 
-    def grow(x, known, axis, bit):
-        number, parts = (bit, 0) if axis == "wide" else (0, bit)
-        across = _from_team(bit, 0, quarter) if axis == "wide" else bit
-        return (
-            jnp.concatenate([x, swap(x, axis, across)], axis=0),
-            known + [(w ^ number, p ^ parts) for w, p in known],
-        )
-
-    first = swap(own, "wide", _from_team(quarter, 0, quarter))
-    chains = [(own, [(0, 0)]), (first, [(quarter, 0)])]
-    bit = quarter // 2
-    while bit > 1:
-        grown = grow(*chains[0], "wide", bit)
-        x, _ = lax.optimization_barrier((chains[1][0], grown[0]))
-        chains = [grown, grow(x, chains[1][1], "wide", bit)]
-        bit //= 2
+    def across(x, axis, bit):
+        return swap(x, axis, _from_team(bit, 0, quarter) if axis == "wide" else bit)
+
+    upper, lower = quarter, quarter // 2
+    far = across(own, "wide", upper)
+    near = across(own, "wide", lower)
+    near_x = [across(x, "parts", 1) for x in (own, near)]
+    held = jnp.concatenate([own, near] + near_x, axis=0)
+    far, *_ = lax.optimization_barrier((far, near))
+    far = jnp.concatenate([far, across(far, "wide", lower)], axis=0)
+    far, *_ = lax.optimization_barrier((far, came, *near_x))
+    far = jnp.concatenate([far, across(far, "parts", 1)], axis=0)
     pieces = []
-    for x, known in chains:
-        x, _ = lax.optimization_barrier((x, came))
-        x, known = grow(x, known, "parts", 1)
-        came = x
-        pieces += [(x, known), (swap(x, "wide", 1), [(w ^ 1, p) for w, p in known])]
+    for x, bit in ((held, 0), (far, upper)):
+        known = [(bit ^ w, p) for p in (0, 1) for w in (0, lower)]
+        pieces += [(x, known), (across(x, "wide", 1), [(w ^ 1, p) for w, p in known])]
     return pieces
 
 
@@ -291,7 +285,7 @@
         outgoing.reshape(holders, capacity, width + LANES), "wide", split_axis=0, concat_axis=0, tiled=True
     )
     half = key_weight_matrix.shape[0] // 2
-    if holders >= 8 and half % 16 == 0 and width % (4 * LANES) == 0:
+    if holders == 16 and half % 16 == 0 and width % (4 * LANES) == 0:
         quarter, depth = holders // 4, width // 4
         wide, parts = lax.axis_index("wide"), lax.axis_index("parts")
         team = wide // quarter % 2

time: 109 us -> 105 us (0.963)
  starting transfers between devices: 30.3 us -> 27 us
  waiting for transfers between devices: 59.8 us -> 58 us
  other arithmetic: 2.02 us -> 0.26 us
  Pallas kernels: 11.9 us -> 13.5 us
    ppermute x9 -> x10, waiting for transfers between devices: 45.4 us -> 40.1 us  [swap(): return lax.ppermute(x, axis, [(i, i ^ bit) for i in range(size)])]
    all_to_all x1, waiting for transfers between devices: 0.01 us -> 3.49 us  [per_device(): lax.all_to_all(outgoing.reshape(holders, capacity, width + LANES), 'wide'...]
    all_to_all x1, starting transfers between devices: 13.5 us -> 10 us  [per_device(): lax.all_to_all(terms.reshape(holders, capacity, columns), 'wide', split_a...]
    pallas_call x1, Pallas kernels: 1.11 us -> 2.68 us  [pack(): pl.pallas_call(functools.partial(_pack_kernel, adapters_held, capacity),...]
    unnamed x22 -> x19, local copies, waits for them, and re-layouts: 3.57 us -> 3.95 us
    ppermute x9 -> x10, starting transfers between devices: 12.3 us -> 12.5 us  [swap(): return lax.ppermute(x, axis, [(i, i ^ bit) for i in range(size)])]
  transfers between devices with their start and end apart: 11 -> 12, of which waited for: 6 -> 7; matrix products, arithmetic and copies ran while one was open for 1% -> 2% of each run, Pallas kernels for 10% -> 12%
where the time goes in v5:
time: 105 us; the launch traced here: 104 us
  waiting for transfers between devices  58 us (55%)
  starting transfers between devices  27 us (26%)
  Pallas kernels  13.5 us (13%)
  local copies, waits for them, and re-layouts  5.23 us (5%)
    ppermute x10, waiting for transfers between devices, swap(): return lax.ppermute(x, axis, [(i, i ^ bit) for i in range(size)])  40.1 us
    all_to_all x1, waiting for transfers between devices, per_device(): lax.all_to_all(terms.reshape(holders, capacity, columns), 'wide', split_a...  14.4 us
    ppermute x10, starting transfers between devices, swap(): return lax.ppermute(x, axis, [(i, i ^ bit) for i in range(size)])  12.5 us
    all_to_all x1, starting transfers between devices, per_device(): lax.all_to_all(terms.reshape(holders, capacity, columns), 'wide', split_a...  10 us
    pallas_call x1, Pallas kernels, adapter_terms(): pl.pallas_call(_adapter_kernel, in_specs=[hbm] * 3, out_specs=hbm, out_sh...  5.09 us
    pallas_call x1, Pallas kernels, base_product(): pl.pallas_call(functools.partial(_base_kernel, marks), in_specs=[pl.Block...  4.71 us
    all_to_all x1, starting transfers between devices, per_device(): lax.all_to_all(outgoing.reshape(holders, capacity, width + LANES), 'wide'...  4.46 us
    unnamed x19, local copies, waits for them, and re-layouts  3.95 us
  transfers between devices with their start and end apart: 12, of which 7 were waited for; matrix products, arithmetic and copies ran while one was open for 2% of the time, Pallas kernels for 12%

profile of v5, /device:TPU:0, one launch (start us, length us, event | category | flops | bytes accessed | tf_op | source)
XLA Modules:
  0.0 104.2 jit_solution(5314577472987753413)
XLA Ops:
  0.0 1.1 %copy-done = bf16[320,1024]{1,0:T(8,128)(2,1)S(1)} copy-done((bf16[320,1024]{1,0:T(8,128)(2,1)S(1)}, bf16[320,1024]{1,0:T(8,128)(2,1)}, u32[]{:S(2)}) %copy-start) | copy-done | bytes 655384
  1.1 4.1 %collective-permute-start.4 = (bf16[160,1024]{1,0:T(8,128)(2,1)S(1)}, bf16[160,1024]{1,0:T(8,128)(2,1)S(1)}, u32[]{:S(2)}, u32[]{:S(2)}) collective-permute-start(bf16[160,1024]{1,0:T(8,128)(2,1)S(1)} %constant_dynamic-slice_fusion.2), channel_id=1, source_target_pairs={{0,8},{1,9},{2,10},{3,11},{4,12},{5,13},{6,14},{7,15},{8,0},{9,1},... | collective-permute-start | bytes 983048 | tf_op jit(solution)/shard_map/ppermute | solution.py:159
  5.2 1.5 %collective-permute-start = (bf16[160,1024]{1,0:T(8,128)(2,1)S(1)}, bf16[160,1024]{1,0:T(8,128)(2,1)S(1)}, u32[]{:S(2)}, u32[]{:S(2)}) collective-permute-start(bf16[160,1024]{1,0:T(8,128)(2,1)S(1)} %constant_dynamic-slice_fusion.2), channel_id=1, source_target_pairs={{0,2},{1,3},{2,0},{3,1},{4,6},{5,7},{6,4},{7,5},{8,10},{9,11},{10,... | collective-permute-start | bytes 983048 | tf_op jit(solution)/shard_map/ppermute | solution.py:159
  6.7 1.2 %constant_dynamic-slice_fusion.1 = (bf16[128,1280]{1,0:T(8,128)(2,1)S(1)}, bf16[128,1280]{1,0:T(8,128)(2,1)S(1)}) fusion(bf16[128,5120]{1,0:T(8,128)(2,1)} %tokens_ref.1, s32[]{:T(128)S(6)} %select_n.32, s32[]{:T(128)S(6)} %select_n.33), kind=kLoop, calls=%fused_computation.6 | loop fusion | bytes 1310728 | tf_op jit(solution)/shard_map/dynamic_slice | solution.py:292
  8.0 1.6 %collective-permute-start.6 = (bf16[128,2560]{1,0:T(8,128)(2,1)S(1)}, bf16[128,2560]{1,0:T(8,128)(2,1)S(1)}, u32[]{:S(2)}, u32[]{:S(2)}) collective-permute-start(bf16[128,2560]{1,0:T(8,128)(2,1)S(1)} %pad_maximum_fusion.2), channel_id=1, source_target_pairs={{0,4},{1,5},{2,6},{3,7},{4,0},{5,1},{6,2},{7,3},{8,12},{9,13},{10,... | collective-permute-start | bytes 1966088 | tf_op jit(solution)/shard_map/ppermute | solution.py:159
  9.7 2.7 %pack_rows.1 = (bf16[256,5248]{1,0:T(8,128)(2,1)}, bf16[128,256]{1,0:T(8,128)(2,1)S(1)}) custom-call(s32[1,512]{1,0:T(1,128)S(1)} %bitcast.10, s32[1,128]{1,0:T(1,128)S(1)} %bitcast.11, bf16[128,5120]{1,0:T(8,128)(2,1)S(1)} %copy-done.1), custom_call_target="tpu_custom_call" | custom-call | flops 335544320 | bytes 3932160 | tf_op jit(solution)/shard_map/pack_rows/pallas_call | solution.py:75
  12.3 4.5 %all-to-all-start = ((bf16[16,16,5248]{2,1,0:T(8,128)(2,1)}), bf16[16,16,5248]{2,1,0:T(8,128)(2,1)}, u32[]{:S(2)}, u32[]{:S(2)}) async-start(bf16[16,16,5248]{2,1,0:T(8,128)(2,1)} %bitcast.5), calls=%async_computation | async-start | bytes 5373952 | tf_op jit(solution)/shard_map/all_to_all | solution.py:284
  16.8 3.2 %collective-permute-done.4 = bf16[160,1024]{1,0:T(8,128)(2,1)S(1)} collective-permute-done((bf16[160,1024]{1,0:T(8,128)(2,1)S(1)}, bf16[160,1024]{1,0:T(8,128)(2,1)S(1)}, u32[]{:S(2)}, u32[]{:S(2)}) %collective-permute-start.4) | collective-permute-done | bytes 327712 | tf_op jit(solution)/shard_map/ppermute | solution.py:159
  20.1 1.6 %collective-permute-start.5 = (bf16[160,1024]{1,0:T(8,128)(2,1)S(1)}, bf16[160,1024]{1,0:T(8,128)(2,1)S(1)}, u32[]{:S(2)}, u32[]{:S(2)}) collective-permute-start(bf16[160,1024]{1,0:T(8,128)(2,1)S(1)} %collective-permute-done.4), channel_id=1, source_target_pairs={{0,2},{1,3},{2,0},{3,1},{4,6},{5,7},{6,4},{7,5},{8,10},{9,11},{10,... | collective-permute-start | bytes 983048 | tf_op jit(solution)/shard_map/ppermute | solution.py:159
  21.6 1.5 %collective-permute-start.1 = (bf16[160,1024]{1,0:T(8,128)(2,1)S(1)}, bf16[160,1024]{1,0:T(8,128)(2,1)S(1)}, u32[]{:S(2)}, u32[]{:S(2)}) collective-permute-start(bf16[160,1024]{1,0:T(8,128)(2,1)S(1)} %constant_dynamic-slice_fusion.2), channel_id=1, source_target_pairs={{0,16},{16,0},{1,17},{17,1},{2,18},{18,2},{3,19},{19,3},{4,20},{20... | collective-permute-start | bytes 983048 | tf_op jit(solution)/shard_map/ppermute | solution.py:159
  23.7 15.3 %collective-permute-done.5 = bf16[160,1024]{1,0:T(8,128)(2,1)S(1)} collective-permute-done((bf16[160,1024]{1,0:T(8,128)(2,1)S(1)}, bf16[160,1024]{1,0:T(8,128)(2,1)S(1)}, u32[]{:S(2)}, u32[]{:S(2)}) %collective-permute-start.5) | collective-permute-done | bytes 327712 | tf_op jit(solution)/shard_map/ppermute | solution.py:159
  39.0 7.0 %collective-permute-done.6.refs_5_ = bf16[128,2560]{1,0:T(8,128)(2,1)S(1)} collective-permute-done((bf16[128,2560]{1,0:T(8,128)(2,1)S(1)}, bf16[128,2560]{1,0:T(8,128)(2,1)S(1)}, u32[]{:S(2)}, u32[]{:S(2)}) %collective-permute-start.6) | collective-permute-done | bytes 655392 | tf_op jit(solution)/shard_map/ppermute | solution.py:159
  46.0 0.9 copy-done.4
  46.9 1.5 %collective-permute-start.7 = (bf16[320,1024]{1,0:T(8,128)(2,1)S(1)}, bf16[320,1024]{1,0:T(8,128)(2,1)S(1)}, u32[]{:S(2)}, u32[]{:S(2)}) collective-permute-start(bf16[320,1024]{1,0:T(8,128)(2,1)S(1)} %pad_maximum_fusion.1), channel_id=1, source_target_pairs={{0,16},{16,0},{1,17},{17,1},{2,18},{18,2},{3,19},{19,3},{4,20},{20... | collective-permute-start | bytes 1966088 | tf_op jit(solution)/shard_map/ppermute | solution.py:159
  48.7 11.5 %collective-permute-done.7 = bf16[320,1024]{1,0:T(8,128)(2,1)S(1)} collective-permute-done((bf16[320,1024]{1,0:T(8,128)(2,1)S(1)}, bf16[320,1024]{1,0:T(8,128)(2,1)S(1)}, u32[]{:S(2)}, u32[]{:S(2)}) %collective-permute-start.7) | collective-permute-done | bytes 655392 | tf_op jit(solution)/shard_map/ppermute | solution.py:159
  60.5 3.0 %collective-permute-done.8.refs_3_ = bf16[640,1024]{1,0:T(8,128)(2,1)} collective-permute-done((bf16[640,1024]{1,0:T(8,128)(2,1)S(1)}, bf16[640,1024]{1,0:T(8,128)(2,1)}, u32[]{:S(2)}, u32[]{:S(2)}) %collective-permute-start.8) | collective-permute-done | bytes 1310752 | tf_op jit(solution)/shard_map/ppermute | solution.py:159
  63.5 1.1 %copy-done.5 = bf16[128,2560]{1,0:T(8,128)(2,1)S(1)} copy-done((bf16[128,2560]{1,0:T(8,128)(2,1)S(1)}, bf16[128,2560]{1,0:T(8,128)(2,1)}, u32[]{:S(2)}) %copy-start.5) | copy-done | bytes 655384
  64.6 4.7 %base_product.1 = (f32[128,1024]{1,0:T(8,128)S(1)}, bf16[128,1024]{1,0:T(8,128)(2,1)}) custom-call(s32[3]{0:T(128)S(1)} %pad_add_fusion.me_ref, bf16[640,1024]{1,0:T(8,128)(2,1)S(1)} %pad_maximum_fusion.refs_0_, bf16[640,1024]{1,0:T(8,128)(2,1)} %collective-permute-done.3.refs_1_, bf16[640,1024]{1,0:T(8,128)(2,1)S(1)} %constant_dynamic-update-slice_fusion.refs_2_, ...), custom_call_target="tpu_custom_call" | custom-call | flops 24000000000 | bytes 5242880 | tf_op jit(solution)/shard_map/base_product/pallas_call | solution.py:216
  69.3 0.8 copy-done.6
  70.1 3.5 %all-to-all-done = bf16[16,16,5248]{2,1,0:T(8,128)(2,1)} async-done(((bf16[16,16,5248]{2,1,0:T(8,128)(2,1)}), bf16[16,16,5248]{2,1,0:T(8,128)(2,1)}, u32[]{:S(2)}, u32[]{:S(2)}) %all-to-all-start) | async-done | bytes 2687008 | tf_op jit(solution)/shard_map/all_to_all | solution.py:284
  73.6 5.1 %adapter_terms.1 = bf16[256,1024]{1,0:T(8,128)(2,1)} custom-call(bf16[256,5248]{1,0:T(8,128)(2,1)} %bitcast.6.rows_ref, bf16[5120,512]{1,0:T(8,128)(2,1)} %shrink_ref.1, bf16[512,1024]{1,0:T(8,128)(2,1)} %expand_ref.1), custom_call_target="tpu_custom_call" | custom-call | flops 1610612736 | bytes 9437184 | tf_op jit(solution)/shard_map/adapter_terms/pallas_call | solution.py:134
  78.7 10.0 %all-to-all-start.1 = ((bf16[16,16,1024]{2,1,0:T(8,128)(2,1)}), bf16[16,16,1024]{2,1,0:T(8,128)(2,1)S(1)}, u32[]{:S(2)}, u32[]{:S(2)}) async-start(bf16[16,16,1024]{2,1,0:T(8,128)(2,1)} %bitcast.12), calls=%async_computation.1 | async-start | bytes 1048576 | tf_op jit(solution)/shard_map/all_to_all | solution.py:303
  88.8 14.4 %all-to-all-done.1 = bf16[16,16,1024]{2,1,0:T(8,128)(2,1)S(1)} async-done(((bf16[16,16,1024]{2,1,0:T(8,128)(2,1)}), bf16[16,16,1024]{2,1,0:T(8,128)(2,1)S(1)}, u32[]{:S(2)}, u32[]{:S(2)}) %all-to-all-start.1) | async-done | bytes 524320 | tf_op jit(solution)/shard_map/all_to_all | solution.py:303
  103.2 0.9 add_terms.1
  (32 shorter events, 1.1 us)
Async XLA Ops:
  0.0 1.1 %copy-start = (bf16[320,1024]{1,0:T(8,128)(2,1)S(1)}, bf16[320,1024]{1,0:T(8,128)(2,1)}, u32[]{:S(2)}) copy-start(bf16[320,1024]{1,0:T(8,128)(2,1)} %param.8) | copy-start | bytes 1966084
  1.1 18.9 %collective-permute-start.4 = (bf16[160,1024]{1,0:T(8,128)(2,1)S(1)}, bf16[160,1024]{1,0:T(8,128)(2,1)S(1)}, u32[]{:S(2)}, u32[]{:S(2)}) collective-permute-start(bf16[160,1024]{1,0:T(8,128)(2,1)S(1)} %constant_dynamic-slice_fusion.2), channel_id=1, source_target_pairs={{0,8},{1,9},{2,10},{3,11},{4,12},{5,13},{6,14},{7,15},{8,0},{9,1},... | collective-permute-start | bytes 983048 | tf_op jit(solution)/shard_map/ppermute | solution.py:159
  5.2 14.8 %collective-permute-start = (bf16[160,1024]{1,0:T(8,128)(2,1)S(1)}, bf16[160,1024]{1,0:T(8,128)(2,1)S(1)}, u32[]{:S(2)}, u32[]{:S(2)}) collective-permute-start(bf16[160,1024]{1,0:T(8,128)(2,1)S(1)} %constant_dynamic-slice_fusion.2), channel_id=1, source_target_pairs={{0,2},{1,3},{2,0},{3,1},{4,6},{5,7},{6,4},{7,5},{8,10},{9,11},{10,... | collective-permute-start | bytes 983048 | tf_op jit(solution)/shard_map/ppermute | solution.py:159
  6.7 2.9 %copy-start.1 = (bf16[128,5120]{1,0:T(8,128)(2,1)S(1)}, bf16[128,5120]{1,0:T(8,128)(2,1)}, u32[]{:S(2)}) copy-start(bf16[128,5120]{1,0:T(8,128)(2,1)} %tokens_ref.1) | copy-start | bytes 3932164
  6.7 2.9 %copy-start.2 = (s32[512]{0:T(512)S(1)}, s32[512]{0:T(512)}, u32[]{:S(2)}) copy-start(s32[512]{0:T(512)} %param.12) | copy-start | bytes 6148
  6.7 2.9 %copy-start.3 = (s32[128]{0:T(128)S(1)}, s32[128]{0:T(128)}, u32[]{:S(2)}) copy-start(s32[128]{0:T(128)} %param.13) | copy-start | bytes 1540
  8.0 38.0 %collective-permute-start.6 = (bf16[128,2560]{1,0:T(8,128)(2,1)S(1)}, bf16[128,2560]{1,0:T(8,128)(2,1)S(1)}, u32[]{:S(2)}, u32[]{:S(2)}) collective-permute-start(bf16[128,2560]{1,0:T(8,128)(2,1)S(1)} %pad_maximum_fusion.2), channel_id=1, source_target_pairs={{0,4},{1,5},{2,6},{3,7},{4,0},{5,1},{6,2},{7,3},{8,12},{9,13},{10,... | collective-permute-start | bytes 1966088 | tf_op jit(solution)/shard_map/ppermute | solution.py:159
  12.3 61.3 %all-to-all-start = ((bf16[16,16,5248]{2,1,0:T(8,128)(2,1)}), bf16[16,16,5248]{2,1,0:T(8,128)(2,1)}, u32[]{:S(2)}, u32[]{:S(2)}) async-start(bf16[16,16,5248]{2,1,0:T(8,128)(2,1)} %bitcast.5), calls=%async_computation | async-start | bytes 5373952 | tf_op jit(solution)/shard_map/all_to_all | solution.py:284
  20.1 18.9 %collective-permute-start.5 = (bf16[160,1024]{1,0:T(8,128)(2,1)S(1)}, bf16[160,1024]{1,0:T(8,128)(2,1)S(1)}, u32[]{:S(2)}, u32[]{:S(2)}) collective-permute-start(bf16[160,1024]{1,0:T(8,128)(2,1)S(1)} %collective-permute-done.4), channel_id=1, source_target_pairs={{0,2},{1,3},{2,0},{3,1},{4,6},{5,7},{6,4},{7,5},{8,10},{9,11},{10,... | collective-permute-start | bytes 983048 | tf_op jit(solution)/shard_map/ppermute | solution.py:159
  21.6 17.3 %collective-permute-start.1 = (bf16[160,1024]{1,0:T(8,128)(2,1)S(1)}, bf16[160,1024]{1,0:T(8,128)(2,1)S(1)}, u32[]{:S(2)}, u32[]{:S(2)}) collective-permute-start(bf16[160,1024]{1,0:T(8,128)(2,1)S(1)} %constant_dynamic-slice_fusion.2), channel_id=1, source_target_pairs={{0,16},{16,0},{1,17},{17,1},{2,18},{18,2},{3,19},{19,3},{4,20},{20... | collective-permute-start | bytes 983048 | tf_op jit(solution)/shard_map/ppermute | solution.py:159
  23.1 15.9 %collective-permute-start.2 = (bf16[160,1024]{1,0:T(8,128)(2,1)S(1)}, bf16[160,1024]{1,0:T(8,128)(2,1)S(1)}, u32[]{:S(2)}, u32[]{:S(2)}) collective-permute-start(bf16[160,1024]{1,0:T(8,128)(2,1)S(1)} %collective-permute-done), channel_id=1, source_target_pairs={{0,16},{16,0},{1,17},{17,1},{2,18},{18,2},{3,19},{19,3},{4,20},{20... | collective-permute-start | bytes 983048 | tf_op jit(solution)/shard_map/ppermute | solution.py:159
  46.0 0.9 copy-start.4
  46.9 13.3 %collective-permute-start.7 = (bf16[320,1024]{1,0:T(8,128)(2,1)S(1)}, bf16[320,1024]{1,0:T(8,128)(2,1)S(1)}, u32[]{:S(2)}, u32[]{:S(2)}) collective-permute-start(bf16[320,1024]{1,0:T(8,128)(2,1)S(1)} %pad_maximum_fusion.1), channel_id=1, source_target_pairs={{0,16},{16,0},{1,17},{17,1},{2,18},{18,2},{3,19},{19,3},{4,20},{20... | collective-permute-start | bytes 1966088 | tf_op jit(solution)/shard_map/ppermute | solution.py:159
  48.6 11.8 %copy-start.8 = (bf16[1024]{0:T(1024)(128)(2,1)S(1)}, bf16[1024]{0:T(1024)(128)(2,1)}, u32[]{:S(2)}) copy-start(bf16[1024]{0:T(1024)(128)(2,1)} %param.9) | copy-start | bytes 6148
  48.6 11.9 %collective-permute-start.3 = (bf16[640,1024]{1,0:T(8,128)(2,1)S(1)}, bf16[640,1024]{1,0:T(8,128)(2,1)}, u32[]{:S(2)}, u32[]{:S(2)}) collective-permute-start(bf16[640,1024]{1,0:T(8,128)(2,1)S(1)} %pad_maximum_fusion.refs_0_), channel_id=1, source_target_pairs={{0,1},{1,0},{2,3},{3,2},{4,5},{5,4},{6,7},{7,6},{8,9},{9,8},{10,11... | collective-permute-start | bytes 3932168 | tf_op jit(solution)/shard_map/ppermute | solution.py:159
  60.3 3.2 %collective-permute-start.8 = (bf16[640,1024]{1,0:T(8,128)(2,1)S(1)}, bf16[640,1024]{1,0:T(8,128)(2,1)}, u32[]{:S(2)}, u32[]{:S(2)}) collective-permute-start(bf16[640,1024]{1,0:T(8,128)(2,1)S(1)} %constant_dynamic-update-slice_fusion.refs_2_), channel_id=1, source_target_pairs={{0,1},{1,0},{2,3},{3,2},{4,5},{5,4},{6,7},{7,6},{8,9},{9,8},{10,11... | collective-permute-start | bytes 3932168 | tf_op jit(solution)/shard_map/ppermute | solution.py:159
  63.5 1.1 %copy-start.5 = (bf16[128,2560]{1,0:T(8,128)(2,1)S(1)}, bf16[128,2560]{1,0:T(8,128)(2,1)}, u32[]{:S(2)}) copy-start(bf16[128,2560]{1,0:T(8,128)(2,1)} %copy-done.4) | copy-start | bytes 1966084
  69.3 0.8 copy-start.6
  70.1 18.6 %collective-permute-start.9 = (bf16[128,1024]{1,0:T(8,128)(2,1)}, bf16[128,1024]{1,0:T(8,128)(2,1)S(1)}, u32[]{:S(2)}, u32[]{:S(2)}) collective-permute-start(bf16[128,1024]{1,0:T(8,128)(2,1)} %get-tuple-element.15), channel_id=1, source_target_pairs={{0,4},{1,5},{2,6},{3,7},{4,0},{5,1},{6,2},{7,3},{8,12},{9,13},{10,... | collective-permute-start | bytes 786440 | tf_op jit(solution)/shard_map/ppermute | solution.py:159
  73.6 15.2 %copy-start.7 = (f32[128,1024]{1,0:T(8,128)S(1)}, f32[128,1024]{1,0:T(8,128)}, u32[]{:S(2)}) copy-start(f32[128,1024]{1,0:T(8,128)} %copy-done.6) | copy-start | bytes 1572868
  78.7 24.5 %all-to-all-start.1 = ((bf16[16,16,1024]{2,1,0:T(8,128)(2,1)}), bf16[16,16,1024]{2,1,0:T(8,128)(2,1)S(1)}, u32[]{:S(2)}, u32[]{:S(2)}) async-start(bf16[16,16,1024]{2,1,0:T(8,128)(2,1)} %bitcast.12), calls=%async_computation.1 | async-start | bytes 1048576 | tf_op jit(solution)/shard_map/all_to_all | solution.py:303

commit v6 on v5

--- a/solution.py
+++ b/solution.py
@@ -115,7 +115,7 @@
     shrunk = jnp.where(keep, total, 0.0).astype(BF16)
     coming[-1].wait()
     columns = terms_ref.shape[1]
-    step = 512 if columns % 512 == 0 else columns
+    step = 256 if columns % 256 == 0 else columns
     going = []
     for i, start in enumerate(range(0, columns, step)):
         cut = pl.ds(start, step)
@@ -142,7 +142,7 @@
             pltpu.VMEM(expand.shape, BF16),
             pltpu.VMEM((places, columns), BF16),
             pltpu.SemaphoreType.DMA((2 * 8 + 2,)),
-            pltpu.SemaphoreType.DMA((pl.cdiv(columns, 512),)),
+            pltpu.SemaphoreType.DMA((pl.cdiv(columns, 256),)),
         ],
         compiler_params=pltpu.CompilerParams(vmem_limit_bytes=60 * 1024 * 1024),
         cost_estimate=pl.CostEstimate(

time: 105 us -> 105 us (level)
  no operation moved by 1% of the time
where the time goes in v6:
time: 105 us; the launch traced here: 104 us
  waiting for transfers between devices  58 us (55%)
  starting transfers between devices  27 us (26%)
  Pallas kernels  13.5 us (13%)
  local copies, waits for them, and re-layouts  5.23 us (5%)
    ppermute x10, waiting for transfers between devices, swap(): return lax.ppermute(x, axis, [(i, i ^ bit) for i in range(size)])  40.1 us
    all_to_all x1, waiting for transfers between devices, per_device(): lax.all_to_all(terms.reshape(holders, capacity, columns), 'wide', split_a...  14.4 us
    ppermute x10, starting transfers between devices, swap(): return lax.ppermute(x, axis, [(i, i ^ bit) for i in range(size)])  12.5 us
    all_to_all x1, starting transfers between devices, per_device(): lax.all_to_all(terms.reshape(holders, capacity, columns), 'wide', split_a...  10 us
    pallas_call x1, Pallas kernels, adapter_terms(): pl.pallas_call(_adapter_kernel, in_specs=[hbm] * 3, out_specs=hbm, out_sh...  5.13 us
    pallas_call x1, Pallas kernels, base_product(): pl.pallas_call(functools.partial(_base_kernel, marks), in_specs=[pl.Block...  4.71 us
    all_to_all x1, starting transfers between devices, per_device(): lax.all_to_all(outgoing.reshape(holders, capacity, width + LANES), 'wide'...  4.46 us
    unnamed x19, local copies, waits for them, and re-layouts  3.95 us
  transfers between devices with their start and end apart: 12, of which 7 were waited for; matrix products, arithmetic and copies ran while one was open for 2% of the time, Pallas kernels for 12%

profile of v6, /device:TPU:0, one launch (start us, length us, event | category | flops | bytes accessed | tf_op | source)
XLA Modules:
  0.0 104.2 jit_solution(10778122755914884540)
XLA Ops:
  0.0 1.1 %copy-done = bf16[320,1024]{1,0:T(8,128)(2,1)S(1)} copy-done((bf16[320,1024]{1,0:T(8,128)(2,1)S(1)}, bf16[320,1024]{1,0:T(8,128)(2,1)}, u32[]{:S(2)}) %copy-start) | copy-done | bytes 655384
  1.1 4.1 %collective-permute-start.4 = (bf16[160,1024]{1,0:T(8,128)(2,1)S(1)}, bf16[160,1024]{1,0:T(8,128)(2,1)S(1)}, u32[]{:S(2)}, u32[]{:S(2)}) collective-permute-start(bf16[160,1024]{1,0:T(8,128)(2,1)S(1)} %constant_dynamic-slice_fusion.2), channel_id=1, source_target_pairs={{0,8},{1,9},{2,10},{3,11},{4,12},{5,13},{6,14},{7,15},{8,0},{9,1},... | collective-permute-start | bytes 983048 | tf_op jit(solution)/shard_map/ppermute | solution.py:159
  5.2 1.5 %collective-permute-start = (bf16[160,1024]{1,0:T(8,128)(2,1)S(1)}, bf16[160,1024]{1,0:T(8,128)(2,1)S(1)}, u32[]{:S(2)}, u32[]{:S(2)}) collective-permute-start(bf16[160,1024]{1,0:T(8,128)(2,1)S(1)} %constant_dynamic-slice_fusion.2), channel_id=1, source_target_pairs={{0,2},{1,3},{2,0},{3,1},{4,6},{5,7},{6,4},{7,5},{8,10},{9,11},{10,... | collective-permute-start | bytes 983048 | tf_op jit(solution)/shard_map/ppermute | solution.py:159
  6.7 1.2 %constant_dynamic-slice_fusion.1 = (bf16[128,1280]{1,0:T(8,128)(2,1)S(1)}, bf16[128,1280]{1,0:T(8,128)(2,1)S(1)}) fusion(bf16[128,5120]{1,0:T(8,128)(2,1)} %tokens_ref.1, s32[]{:T(128)S(6)} %select_n.32, s32[]{:T(128)S(6)} %select_n.33), kind=kLoop, calls=%fused_computation.6 | loop fusion | bytes 1310728 | tf_op jit(solution)/shard_map/dynamic_slice | solution.py:292
  8.0 1.6 %collective-permute-start.6 = (bf16[128,2560]{1,0:T(8,128)(2,1)S(1)}, bf16[128,2560]{1,0:T(8,128)(2,1)S(1)}, u32[]{:S(2)}, u32[]{:S(2)}) collective-permute-start(bf16[128,2560]{1,0:T(8,128)(2,1)S(1)} %pad_maximum_fusion.2), channel_id=1, source_target_pairs={{0,4},{1,5},{2,6},{3,7},{4,0},{5,1},{6,2},{7,3},{8,12},{9,13},{10,... | collective-permute-start | bytes 1966088 | tf_op jit(solution)/shard_map/ppermute | solution.py:159
  9.7 2.7 %pack_rows.1 = (bf16[256,5248]{1,0:T(8,128)(2,1)}, bf16[128,256]{1,0:T(8,128)(2,1)S(1)}) custom-call(s32[1,512]{1,0:T(1,128)S(1)} %bitcast.10, s32[1,128]{1,0:T(1,128)S(1)} %bitcast.11, bf16[128,5120]{1,0:T(8,128)(2,1)S(1)} %copy-done.1), custom_call_target="tpu_custom_call" | custom-call | flops 335544320 | bytes 3932160 | tf_op jit(solution)/shard_map/pack_rows/pallas_call | solution.py:75
  12.3 4.5 %all-to-all-start = ((bf16[16,16,5248]{2,1,0:T(8,128)(2,1)}), bf16[16,16,5248]{2,1,0:T(8,128)(2,1)}, u32[]{:S(2)}, u32[]{:S(2)}) async-start(bf16[16,16,5248]{2,1,0:T(8,128)(2,1)} %bitcast.5), calls=%async_computation | async-start | bytes 5373952 | tf_op jit(solution)/shard_map/all_to_all | solution.py:284
  16.8 3.2 %collective-permute-done.4 = bf16[160,1024]{1,0:T(8,128)(2,1)S(1)} collective-permute-done((bf16[160,1024]{1,0:T(8,128)(2,1)S(1)}, bf16[160,1024]{1,0:T(8,128)(2,1)S(1)}, u32[]{:S(2)}, u32[]{:S(2)}) %collective-permute-start.4) | collective-permute-done | bytes 327712 | tf_op jit(solution)/shard_map/ppermute | solution.py:159
  20.1 1.6 %collective-permute-start.5 = (bf16[160,1024]{1,0:T(8,128)(2,1)S(1)}, bf16[160,1024]{1,0:T(8,128)(2,1)S(1)}, u32[]{:S(2)}, u32[]{:S(2)}) collective-permute-start(bf16[160,1024]{1,0:T(8,128)(2,1)S(1)} %collective-permute-done.4), channel_id=1, source_target_pairs={{0,2},{1,3},{2,0},{3,1},{4,6},{5,7},{6,4},{7,5},{8,10},{9,11},{10,... | collective-permute-start | bytes 983048 | tf_op jit(solution)/shard_map/ppermute | solution.py:159
  21.6 1.5 %collective-permute-start.1 = (bf16[160,1024]{1,0:T(8,128)(2,1)S(1)}, bf16[160,1024]{1,0:T(8,128)(2,1)S(1)}, u32[]{:S(2)}, u32[]{:S(2)}) collective-permute-start(bf16[160,1024]{1,0:T(8,128)(2,1)S(1)} %constant_dynamic-slice_fusion.2), channel_id=1, source_target_pairs={{0,16},{16,0},{1,17},{17,1},{2,18},{18,2},{3,19},{19,3},{4,20},{20... | collective-permute-start | bytes 983048 | tf_op jit(solution)/shard_map/ppermute | solution.py:159
  23.7 15.3 %collective-permute-done.5 = bf16[160,1024]{1,0:T(8,128)(2,1)S(1)} collective-permute-done((bf16[160,1024]{1,0:T(8,128)(2,1)S(1)}, bf16[160,1024]{1,0:T(8,128)(2,1)S(1)}, u32[]{:S(2)}, u32[]{:S(2)}) %collective-permute-start.5) | collective-permute-done | bytes 327712 | tf_op jit(solution)/shard_map/ppermute | solution.py:159
  39.0 7.0 %collective-permute-done.6.refs_5_ = bf16[128,2560]{1,0:T(8,128)(2,1)S(1)} collective-permute-done((bf16[128,2560]{1,0:T(8,128)(2,1)S(1)}, bf16[128,2560]{1,0:T(8,128)(2,1)S(1)}, u32[]{:S(2)}, u32[]{:S(2)}) %collective-permute-start.6) | collective-permute-done | bytes 655392 | tf_op jit(solution)/shard_map/ppermute | solution.py:159
  46.0 0.9 copy-done.4
  46.9 1.5 %collective-permute-start.7 = (bf16[320,1024]{1,0:T(8,128)(2,1)S(1)}, bf16[320,1024]{1,0:T(8,128)(2,1)S(1)}, u32[]{:S(2)}, u32[]{:S(2)}) collective-permute-start(bf16[320,1024]{1,0:T(8,128)(2,1)S(1)} %pad_maximum_fusion.1), channel_id=1, source_target_pairs={{0,16},{16,0},{1,17},{17,1},{2,18},{18,2},{3,19},{19,3},{4,20},{20... | collective-permute-start | bytes 1966088 | tf_op jit(solution)/shard_map/ppermute | solution.py:159
  48.7 11.5 %collective-permute-done.7 = bf16[320,1024]{1,0:T(8,128)(2,1)S(1)} collective-permute-done((bf16[320,1024]{1,0:T(8,128)(2,1)S(1)}, bf16[320,1024]{1,0:T(8,128)(2,1)S(1)}, u32[]{:S(2)}, u32[]{:S(2)}) %collective-permute-start.7) | collective-permute-done | bytes 655392 | tf_op jit(solution)/shard_map/ppermute | solution.py:159
  60.5 3.0 %collective-permute-done.8.refs_3_ = bf16[640,1024]{1,0:T(8,128)(2,1)} collective-permute-done((bf16[640,1024]{1,0:T(8,128)(2,1)S(1)}, bf16[640,1024]{1,0:T(8,128)(2,1)}, u32[]{:S(2)}, u32[]{:S(2)}) %collective-permute-start.8) | collective-permute-done | bytes 1310752 | tf_op jit(solution)/shard_map/ppermute | solution.py:159
  63.5 1.1 %copy-done.5 = bf16[128,2560]{1,0:T(8,128)(2,1)S(1)} copy-done((bf16[128,2560]{1,0:T(8,128)(2,1)S(1)}, bf16[128,2560]{1,0:T(8,128)(2,1)}, u32[]{:S(2)}) %copy-start.5) | copy-done | bytes 655384
  64.6 4.7 %base_product.1 = (f32[128,1024]{1,0:T(8,128)S(1)}, bf16[128,1024]{1,0:T(8,128)(2,1)}) custom-call(s32[3]{0:T(128)S(1)} %pad_add_fusion.me_ref, bf16[640,1024]{1,0:T(8,128)(2,1)S(1)} %pad_maximum_fusion.refs_0_, bf16[640,1024]{1,0:T(8,128)(2,1)} %collective-permute-done.3.refs_1_, bf16[640,1024]{1,0:T(8,128)(2,1)S(1)} %constant_dynamic-update-slice_fusion.refs_2_, ...), custom_call_target="tpu_custom_call" | custom-call | flops 24000000000 | bytes 5242880 | tf_op jit(solution)/shard_map/base_product/pallas_call | solution.py:216
  69.3 0.8 copy-done.6
  70.1 3.5 %all-to-all-done = bf16[16,16,5248]{2,1,0:T(8,128)(2,1)} async-done(((bf16[16,16,5248]{2,1,0:T(8,128)(2,1)}), bf16[16,16,5248]{2,1,0:T(8,128)(2,1)}, u32[]{:S(2)}, u32[]{:S(2)}) %all-to-all-start) | async-done | bytes 2687008 | tf_op jit(solution)/shard_map/all_to_all | solution.py:284
  73.6 5.1 %adapter_terms.1 = bf16[256,1024]{1,0:T(8,128)(2,1)} custom-call(bf16[256,5248]{1,0:T(8,128)(2,1)} %bitcast.6.rows_ref, bf16[5120,512]{1,0:T(8,128)(2,1)} %shrink_ref.1, bf16[512,1024]{1,0:T(8,128)(2,1)} %expand_ref.1), custom_call_target="tpu_custom_call" | custom-call | flops 1610612736 | bytes 9437184 | tf_op jit(solution)/shard_map/adapter_terms/pallas_call | solution.py:134
  78.8 10.0 %all-to-all-start.1 = ((bf16[16,16,1024]{2,1,0:T(8,128)(2,1)}), bf16[16,16,1024]{2,1,0:T(8,128)(2,1)S(1)}, u32[]{:S(2)}, u32[]{:S(2)}) async-start(bf16[16,16,1024]{2,1,0:T(8,128)(2,1)} %bitcast.12), calls=%async_computation.1 | async-start | bytes 1048576 | tf_op jit(solution)/shard_map/all_to_all | solution.py:303
  88.9 14.4 %all-to-all-done.1 = bf16[16,16,1024]{2,1,0:T(8,128)(2,1)S(1)} async-done(((bf16[16,16,1024]{2,1,0:T(8,128)(2,1)}), bf16[16,16,1024]{2,1,0:T(8,128)(2,1)S(1)}, u32[]{:S(2)}, u32[]{:S(2)}) %all-to-all-start.1) | async-done | bytes 524320 | tf_op jit(solution)/shard_map/all_to_all | solution.py:303
  103.3 0.9 add_terms.1
  (32 shorter events, 1.1 us)
Async XLA Ops:
  0.0 1.1 %copy-start = (bf16[320,1024]{1,0:T(8,128)(2,1)S(1)}, bf16[320,1024]{1,0:T(8,128)(2,1)}, u32[]{:S(2)}) copy-start(bf16[320,1024]{1,0:T(8,128)(2,1)} %param.8) | copy-start | bytes 1966084
  1.1 18.9 %collective-permute-start.4 = (bf16[160,1024]{1,0:T(8,128)(2,1)S(1)}, bf16[160,1024]{1,0:T(8,128)(2,1)S(1)}, u32[]{:S(2)}, u32[]{:S(2)}) collective-permute-start(bf16[160,1024]{1,0:T(8,128)(2,1)S(1)} %constant_dynamic-slice_fusion.2), channel_id=1, source_target_pairs={{0,8},{1,9},{2,10},{3,11},{4,12},{5,13},{6,14},{7,15},{8,0},{9,1},... | collective-permute-start | bytes 983048 | tf_op jit(solution)/shard_map/ppermute | solution.py:159
  5.2 14.8 %collective-permute-start = (bf16[160,1024]{1,0:T(8,128)(2,1)S(1)}, bf16[160,1024]{1,0:T(8,128)(2,1)S(1)}, u32[]{:S(2)}, u32[]{:S(2)}) collective-permute-start(bf16[160,1024]{1,0:T(8,128)(2,1)S(1)} %constant_dynamic-slice_fusion.2), channel_id=1, source_target_pairs={{0,2},{1,3},{2,0},{3,1},{4,6},{5,7},{6,4},{7,5},{8,10},{9,11},{10,... | collective-permute-start | bytes 983048 | tf_op jit(solution)/shard_map/ppermute | solution.py:159
  6.7 2.9 %copy-start.1 = (bf16[128,5120]{1,0:T(8,128)(2,1)S(1)}, bf16[128,5120]{1,0:T(8,128)(2,1)}, u32[]{:S(2)}) copy-start(bf16[128,5120]{1,0:T(8,128)(2,1)} %tokens_ref.1) | copy-start | bytes 3932164
  6.7 2.9 %copy-start.2 = (s32[512]{0:T(512)S(1)}, s32[512]{0:T(512)}, u32[]{:S(2)}) copy-start(s32[512]{0:T(512)} %param.12) | copy-start | bytes 6148
  6.7 2.9 %copy-start.3 = (s32[128]{0:T(128)S(1)}, s32[128]{0:T(128)}, u32[]{:S(2)}) copy-start(s32[128]{0:T(128)} %param.13) | copy-start | bytes 1540
  8.0 38.0 %collective-permute-start.6 = (bf16[128,2560]{1,0:T(8,128)(2,1)S(1)}, bf16[128,2560]{1,0:T(8,128)(2,1)S(1)}, u32[]{:S(2)}, u32[]{:S(2)}) collective-permute-start(bf16[128,2560]{1,0:T(8,128)(2,1)S(1)} %pad_maximum_fusion.2), channel_id=1, source_target_pairs={{0,4},{1,5},{2,6},{3,7},{4,0},{5,1},{6,2},{7,3},{8,12},{9,13},{10,... | collective-permute-start | bytes 1966088 | tf_op jit(solution)/shard_map/ppermute | solution.py:159
  12.3 61.3 %all-to-all-start = ((bf16[16,16,5248]{2,1,0:T(8,128)(2,1)}), bf16[16,16,5248]{2,1,0:T(8,128)(2,1)}, u32[]{:S(2)}, u32[]{:S(2)}) async-start(bf16[16,16,5248]{2,1,0:T(8,128)(2,1)} %bitcast.5), calls=%async_computation | async-start | bytes 5373952 | tf_op jit(solution)/shard_map/all_to_all | solution.py:284
  20.1 18.9 %collective-permute-start.5 = (bf16[160,1024]{1,0:T(8,128)(2,1)S(1)}, bf16[160,1024]{1,0:T(8,128)(2,1)S(1)}, u32[]{:S(2)}, u32[]{:S(2)}) collective-permute-start(bf16[160,1024]{1,0:T(8,128)(2,1)S(1)} %collective-permute-done.4), channel_id=1, source_target_pairs={{0,2},{1,3},{2,0},{3,1},{4,6},{5,7},{6,4},{7,5},{8,10},{9,11},{10,... | collective-permute-start | bytes 983048 | tf_op jit(solution)/shard_map/ppermute | solution.py:159
  21.6 17.3 %collective-permute-start.1 = (bf16[160,1024]{1,0:T(8,128)(2,1)S(1)}, bf16[160,1024]{1,0:T(8,128)(2,1)S(1)}, u32[]{:S(2)}, u32[]{:S(2)}) collective-permute-start(bf16[160,1024]{1,0:T(8,128)(2,1)S(1)} %constant_dynamic-slice_fusion.2), channel_id=1, source_target_pairs={{0,16},{16,0},{1,17},{17,1},{2,18},{18,2},{3,19},{19,3},{4,20},{20... | collective-permute-start | bytes 983048 | tf_op jit(solution)/shard_map/ppermute | solution.py:159
  23.1 15.9 %collective-permute-start.2 = (bf16[160,1024]{1,0:T(8,128)(2,1)S(1)}, bf16[160,1024]{1,0:T(8,128)(2,1)S(1)}, u32[]{:S(2)}, u32[]{:S(2)}) collective-permute-start(bf16[160,1024]{1,0:T(8,128)(2,1)S(1)} %collective-permute-done), channel_id=1, source_target_pairs={{0,16},{16,0},{1,17},{17,1},{2,18},{18,2},{3,19},{19,3},{4,20},{20... | collective-permute-start | bytes 983048 | tf_op jit(solution)/shard_map/ppermute | solution.py:159
  46.0 0.9 copy-start.4
  46.9 13.3 %collective-permute-start.7 = (bf16[320,1024]{1,0:T(8,128)(2,1)S(1)}, bf16[320,1024]{1,0:T(8,128)(2,1)S(1)}, u32[]{:S(2)}, u32[]{:S(2)}) collective-permute-start(bf16[320,1024]{1,0:T(8,128)(2,1)S(1)} %pad_maximum_fusion.1), channel_id=1, source_target_pairs={{0,16},{16,0},{1,17},{17,1},{2,18},{18,2},{3,19},{19,3},{4,20},{20... | collective-permute-start | bytes 1966088 | tf_op jit(solution)/shard_map/ppermute | solution.py:159
  48.6 11.8 %copy-start.8 = (bf16[1024]{0:T(1024)(128)(2,1)S(1)}, bf16[1024]{0:T(1024)(128)(2,1)}, u32[]{:S(2)}) copy-start(bf16[1024]{0:T(1024)(128)(2,1)} %param.9) | copy-start | bytes 6148
  48.6 11.9 %collective-permute-start.3 = (bf16[640,1024]{1,0:T(8,128)(2,1)S(1)}, bf16[640,1024]{1,0:T(8,128)(2,1)}, u32[]{:S(2)}, u32[]{:S(2)}) collective-permute-start(bf16[640,1024]{1,0:T(8,128)(2,1)S(1)} %pad_maximum_fusion.refs_0_), channel_id=1, source_target_pairs={{0,1},{1,0},{2,3},{3,2},{4,5},{5,4},{6,7},{7,6},{8,9},{9,8},{10,11... | collective-permute-start | bytes 3932168 | tf_op jit(solution)/shard_map/ppermute | solution.py:159
  60.3 3.2 %collective-permute-start.8 = (bf16[640,1024]{1,0:T(8,128)(2,1)S(1)}, bf16[640,1024]{1,0:T(8,128)(2,1)}, u32[]{:S(2)}, u32[]{:S(2)}) collective-permute-start(bf16[640,1024]{1,0:T(8,128)(2,1)S(1)} %constant_dynamic-update-slice_fusion.refs_2_), channel_id=1, source_target_pairs={{0,1},{1,0},{2,3},{3,2},{4,5},{5,4},{6,7},{7,6},{8,9},{9,8},{10,11... | collective-permute-start | bytes 3932168 | tf_op jit(solution)/shard_map/ppermute | solution.py:159
  63.5 1.1 %copy-start.5 = (bf16[128,2560]{1,0:T(8,128)(2,1)S(1)}, bf16[128,2560]{1,0:T(8,128)(2,1)}, u32[]{:S(2)}) copy-start(bf16[128,2560]{1,0:T(8,128)(2,1)} %copy-done.4) | copy-start | bytes 1966084
  69.3 0.8 copy-start.6
  70.1 18.7 %collective-permute-start.9 = (bf16[128,1024]{1,0:T(8,128)(2,1)}, bf16[128,1024]{1,0:T(8,128)(2,1)S(1)}, u32[]{:S(2)}, u32[]{:S(2)}) collective-permute-start(bf16[128,1024]{1,0:T(8,128)(2,1)} %get-tuple-element.15), channel_id=1, source_target_pairs={{0,4},{1,5},{2,6},{3,7},{4,0},{5,1},{6,2},{7,3},{8,12},{9,13},{10,... | collective-permute-start | bytes 786440 | tf_op jit(solution)/shard_map/ppermute | solution.py:159
  73.6 15.2 %copy-start.7 = (f32[128,1024]{1,0:T(8,128)S(1)}, f32[128,1024]{1,0:T(8,128)}, u32[]{:S(2)}) copy-start(f32[128,1024]{1,0:T(8,128)} %copy-done.6) | copy-start | bytes 1572868
  78.8 24.5 %all-to-all-start.1 = ((bf16[16,16,1024]{2,1,0:T(8,128)(2,1)}), bf16[16,16,1024]{2,1,0:T(8,128)(2,1)S(1)}, u32[]{:S(2)}, u32[]{:S(2)}) async-start(bf16[16,16,1024]{2,1,0:T(8,128)(2,1)} %bitcast.12), calls=%async_computation.1 | async-start | bytes 1048576 | tf_op jit(solution)/shard_map/all_to_all | solution.py:303
